TPU v7x, 512 devices: a whole 4x8x8 slice. The times are simulated.
512 devices in a mesh: dp: 32 (over y_hi, z), item: 16 (over x, y_lo, core).
Axes of the slice: x: 4, y: 8 (y_hi: 4, y_lo: 2; y = y_hi * 2 + y_lo), z: 8, core: 2. Of those that a mesh axis runs over, the one named last changes fastest.
Arguments:
- states: bfloat16 [262144, 256], P(('dp', 'item')), may hold values from -6 to 6
- next_states: bfloat16 [262144, 256], P(('dp', 'item')), may hold values from -6 to 6
- rewards: float32 [262144], P(('dp', 'item')), may hold values from 0 to 2
- slate_ids: int32 [262144, 10], P(('dp', 'item')), may hold values from 0 to 4095
- chosen: int32 [262144], P(('dp', 'item')), may hold values from 0 to 9
- next_slate: int32 [262144, 10], P(('dp', 'item')), may hold values from 0 to 4095
- table: float32 [16384, 128], P('item'), may hold values from -100 to 100
- first_moment: float32 [16384, 128], P('item'), may hold values from -0.15625 to 0.15625
- second_moment: float32 [16384, 128], P('item'), may hold values from 1e-06 to 0.0001
- cand_rows: int32 [4096], P('item'), may hold values from 0 to 1023, as said below
- w_hidden: bfloat16 [256, 512], replicated, may hold values from -0.375 to 0.375
- w_embed: bfloat16 [512, 128], replicated, may hold values from -0.25 to 0.25
Outputs:
- new_first: float32 [16384, 128], P('item')
- new_second: float32 [16384, 128], P('item')
- direction: float32 [16384, 128], P('item')
- grad_hidden: float32 [256, 512], replicated
- grad_embed: float32 [512, 128], replicated
- td_error: float32 [262144], P(('dp', 'item'))
Inputs may be any that keep to these rules, and one draw needn't show every extreme that they name: `cand_rows`: within each aligned block of 256 entries the entries are distinct.
All inputs are finite; a program needn't handle non-finite values.
Results may differ from a plain program's by a relative error of at most 0.006.
Values may be sent and summed in bfloat16 or wider, within the bound.
No kernel may reach another device: no remote copies, remote signals or barrier semaphores. Data moves between devices by JAX's collectives and lax.ppermute only.
A program may use at most 64 MiB of HBM per device.

v0:
```python
import math

import jax
import jax.numpy as jnp
from jax import lax
from jax.sharding import PartitionSpec as P

ADAM_STEP = 10


PENALTY = 0.5
DISCOUNT = 0.9
BETA_ONE = 0.9
BETA_TWO = 0.999
EPSILON = 1e-08


def tower(features, w_hidden, w_embed):
    hidden = jnp.maximum(
        jnp.dot(features, w_hidden, preferred_element_type=jnp.float32), 0.0
    ).astype(jnp.bfloat16)
    users = jnp.dot(hidden, w_embed, preferred_element_type=jnp.float32).astype(jnp.bfloat16)
    return (hidden, users)


def shards(
    states,
    next_states,
    rewards,
    slate_ids,
    chosen,
    next_slate,
    table,
    first_moment,
    second_moment,
    cand_rows,
    w_hidden,
    w_embed,
):
    embed_width = table.shape[1]
    local_slab = table[cand_rows].astype(jnp.bfloat16)
    slab = lax.all_gather(local_slab, "item", axis=0, tiled=True)
    total_cands = slab.shape[0]
    block_width = math.gcd(total_cands, 2048)
    nblocks = total_cands // block_width
    slab_blocks = slab.reshape(nblocks, block_width, embed_width)
    block_starts = jnp.arange(nblocks, dtype=jnp.int32) * block_width
    hidden, users = tower(states, w_hidden, w_embed)
    _, next_users = tower(next_states, w_hidden, w_embed)
    sessions = users.shape[0]

    def forward(carry, inputs):
        running_max, running_sum = carry
        block_slab, _ = inputs
        scores = jnp.dot(users, block_slab.T, preferred_element_type=jnp.float32)
        newest = jnp.maximum(running_max, jnp.max(scores, axis=1))
        running_sum = running_sum * jnp.exp(running_max - newest) + jnp.sum(
            jnp.exp(scores - newest[:, None]), axis=1
        )
        return ((newest, running_sum), None)

    init = (jnp.full((sessions,), -jnp.inf, jnp.float32), jnp.zeros((sessions,), jnp.float32))
    (running_max, running_sum), _ = lax.scan(forward, init, (slab_blocks, block_starts))
    lse = running_max + jnp.log(running_sum)
    slate_q = jnp.einsum("bse,be->bs", slab[slate_ids], users, preferred_element_type=jnp.float32)
    next_q = jnp.einsum(
        "bse,be->bs", slab[next_slate], next_users, preferred_element_type=jnp.float32
    )
    weights = jax.nn.softmax(next_q, axis=1)
    target = rewards + DISCOUNT * jnp.sum(weights * next_q, axis=1)
    picked_q = jnp.take_along_axis(slate_q, chosen[:, None], axis=1)[:, 0]
    delta = picked_q - target
    clicked = jnp.take_along_axis(slate_ids, chosen[:, None], axis=1)[:, 0]
    scale = 1.0 / sessions

    def backward(user_acc, inputs):
        block_slab, first_col = inputs
        scores = jnp.dot(users, block_slab.T, preferred_element_type=jnp.float32)
        columns = first_col + jnp.arange(block_width, dtype=jnp.int32)
        onehot = (clicked[:, None] == columns[None, :]).astype(jnp.float32)
        score_grad = (
            (PENALTY * jnp.exp(scores - lse[:, None]) + (delta - PENALTY)[:, None] * onehot) * scale
        ).astype(jnp.bfloat16)
        user_acc = user_acc + jnp.dot(score_grad, block_slab, preferred_element_type=jnp.float32)
        block_grad = jnp.dot(score_grad.T, users, preferred_element_type=jnp.float32)
        return (user_acc, block_grad)

    user_acc, grad_blocks = lax.scan(
        backward, jnp.zeros((sessions, embed_width), jnp.float32), (slab_blocks, block_starts)
    )
    cand_grad = grad_blocks.reshape(total_cands, embed_width)
    user_grad = user_acc.astype(jnp.bfloat16)
    local_embed = jnp.dot(hidden.T, user_grad, preferred_element_type=jnp.float32)
    back = jnp.dot(user_grad, w_embed.T, preferred_element_type=jnp.float32)
    pre_grad = jnp.where(hidden > 0, back, 0.0).astype(jnp.bfloat16)
    local_hidden = jnp.dot(states.T, pre_grad, preferred_element_type=jnp.float32)
    summed = lax.psum_scatter(cand_grad, "item", scatter_dimension=0, tiled=True)
    owner_grad = lax.psum(summed, "dp")
    grad_hidden, grad_embed = lax.psum((local_hidden, local_embed), ("dp", "item"))
    table_grad = jnp.zeros(table.shape, jnp.float32).at[cand_rows].add(owner_grad)
    new_first = BETA_ONE * first_moment + (1.0 - BETA_ONE) * table_grad
    new_second = BETA_TWO * second_moment + (1.0 - BETA_TWO) * table_grad * table_grad
    correct_one = 1.0 - BETA_ONE**ADAM_STEP
    correct_two = 1.0 - BETA_TWO**ADAM_STEP
    direction = new_first / correct_one / (jnp.sqrt(new_second / correct_two) + EPSILON)
    return (new_first, new_second, direction, grad_hidden, grad_embed, delta)


def solution(mesh):
    placed = (
        P(("dp", "item"), None),
        P(("dp", "item"), None),
        P(("dp", "item")),
        P(("dp", "item"), None),
        P(("dp", "item")),
        P(("dp", "item"), None),
        P("item", None),
        P("item", None),
        P("item", None),
        P("item"),
        P(),
        P(),
    )
    return jax.shard_map(
        shards,
        mesh=mesh,
        in_specs=placed,
        out_specs=(P("item", None), P("item", None), P("item", None), P(), P(), P(("dp", "item"))),
        check_vma=False,
    )
```

profile of v0, /device:TPU:1, one launch (start us, length us, event | category | flops | bytes accessed | tf_op | source)
XLA Modules:
  0.0 753.3 jit_solution(6338077787540600950)
XLA Ops:
  7.2 0.7 compare_select_fusion.3
  8.0 0.3 copy-done
  8.2 1.4 gather_fusion
  9.7 0.8 compare_select_fusion
  10.5 0.1 copy.23
  10.6 0.2 reshape.85
  10.8 0.8 compare_select_fusion.1
  11.6 0.1 copy.22
  11.7 0.2 reshape.77
  11.9 0.7 compare_select_fusion.2
  12.6 4.5 gather_fusion.3
  17.2 1.2 fusion.21
  18.5 0.3 fusion.14
  18.8 0.3 convolution_convert_fusion
  19.1 35.3 %all-gather.2.cloned.1.call-done = bf16[4096,128]{1,0:T(8,128)(2,1)} async-done(((bf16[256,128]{1,0:T(8,128)(2,1)}), bf16[4096,128]{1,0:T(8,128)(2,1)}) %all-gather.2.cloned.1.call-update) | async-done | bytes 1048592 | tf_op jit(solution)/shard_map/all_gather | solution.py:42
  54.4 15.1 %gather_fusion.2 = bf16[5120,128]{1,0:T(8,128)(2,1)S(1)} fusion(bf16[4096,128]{1,0:T(8,128)(2,1)} %all-gather.2.cloned.1.call-done, s32[5120]{0:T(1024)S(1)} %broadcast_clamp_fusion), kind=kCustom, calls=%fused_computation.2 | custom fusion | bytes 2641920 | tf_op jit(solution)/shard_map/gather | solution.py:67
  69.6 1.6 reshape.84
  71.1 2.9 fusion.26
  74.2 11.0 %while.28 = (s32[]{:T(128)}, f32[512]{0:T(512)S(1)}, f32[512]{0:T(512)S(1)}, bf16[2,2048,128]{2,1,0:T(8,128)(2,1)S(1)}, bf16[512,128]{1,0:T(8,128)(2,1)S(1)}, /*index=5*/s32[]{:T(128)}, s32[]{:T(128)}) while((s32[]{:T(128)}, f32[512]{0:T(512)S(1)}, f32[512]{0:T(512)S(1)}, bf16[2,2048,128]{2,1,0:T(8,128)(2,1)S(1)}, ...), condition=%wide.region_3.4_spmd.clone, body=%wide.region_0.3_spmd.clone.sunk | while | flops 271583744 | bytes 9070684 | solution.py:63
  74.2 2.7 fusion.77
  76.9 2.8 exponential_reduce_fusion.2
  79.8 2.7 fusion.77
  82.4 2.8 exponential_reduce_fusion.2
  85.3 15.1 %gather_fusion.1 = bf16[5120,128]{1,0:T(8,128)(2,1)S(1)} fusion(bf16[4096,128]{1,0:T(8,128)(2,1)S(1)} %bitcast.90, s32[5120]{0:T(1024)S(1)} %broadcast_clamp_fusion.1), kind=kCustom, calls=%fused_computation.1 | custom fusion | bytes 2641920 | tf_op jit(solution)/shard_map/gather | solution.py:65
  100.4 1.6 reshape.76
  101.9 2.8 fusion.28
  104.7 3.8 gather_fusion.4
  108.5 16.1 %while.29 = (s32[]{:T(128)}, f32[512,128]{1,0:T(8,128)S(1)}, f32[2,2048,128]{2,1,0:T(8,128)}, bf16[2,2048,128]{2,1,0:T(8,128)(2,1)S(1)}, bf16[512,128]{1,0:T(8,1...) while((s32[]{:T(128)}, f32[512,128]{1,0:T(8,128)S(1)}, ...), condition=%wide.region_8.9_spmd.clone, body=%wide.region_7.8_spmd.clone.sunk | while | flops 812780032 | bytes 17590956 | solution.py:88
  108.6 0.6 dynamic_slice.41
  109.1 0.6 iota_add_fusion.2
  109.8 2.5 fusion.85
  112.4 2.5 convolution_add_fusion.2
  114.9 1.7 fusion.86
  116.6 0.6 dynamic_slice.41
  117.1 0.6 iota_add_fusion.2
  117.8 2.5 fusion.85
  120.4 2.5 convolution_add_fusion.2
  122.9 1.7 fusion.86
  124.7 1.0 copy-done.5
  125.6 1.0 fusion.33
  126.7 1.5 fusion.18
  128.3 63.5 %reduce-scatter.2.cloned.1.call-done = f32[256,128]{1,0:T(8,128)} async-done(((f32[4096,128]{1,0:T(8,128)}), f32[256,128]{1,0:T(8,128)}) %reduce-scatter.2.cloned.1.call-update) | async-done | bytes 131088 | tf_op jit(solution)/shard_map/reduce_scatter | solution.py:97
  191.8 278.0 %all-reduce.6.cloned.1.call-done = (f32[256,512]{0,1:T(8,128)}, f32[512,128]{1,0:T(8,128)}) async-done(((f32[256,512]{0,1:T(8,128)}, f32[512,128]{1,0:T(8,128)}), (f32[256,512]{0,1:T(8,128)}, f32[512,128]{1,0:T(8,128)})) %all-reduce.6.cloned.1.call-update) | async-done | bytes 786448 | tf_op jit(solution)/shard_map/psum | solution.py:99
  469.8 2.0 copy.24
  471.8 270.9 %all-reduce.4.cloned.1.call-done = f32[256,128]{1,0:T(8,128)} async-done(((f32[256,128]{1,0:T(8,128)}), f32[256,128]{1,0:T(8,128)}) %all-reduce.4.cloned.1.call-update) | async-done | bytes 131088 | tf_op jit(solution)/shard_map/psum | solution.py:98
  742.8 1.9 scatter_custom_fusion
  744.7 1.3 add_divide_fusion
  746.0 0.7 copy.55
  (67 shorter events, 0.7 us)
Async XLA Ops:
  7.2 1.1 copy-start
  7.2 5.4 copy-start.3
  7.2 47.2 %all-gather.2.cloned.1.call-start = ((), (), s32[]{:S(2)}) async-start(), calls=%async_computation.1 | async-start | bytes 1114112 | tf_op jit(solution)/shard_map/all_gather | solution.py:42
  8.2 9.0 %copy-start.9 = (bf16[256,512]{1,0:T(8,128)(2,1)S(1)}, bf16[256,512]{1,0:T(8,128)(2,1)}, u32[]{:S(2)}) copy-start(bf16[256,512]{1,0:T(8,128)(2,1)} %param.26) | copy-start | bytes 786436
  8.2 9.0 %copy-start.12 = (bf16[512,128]{1,0:T(8,128)(2,1)S(1)}, bf16[512,128]{1,0:T(8,128)(2,1)}, u32[]{:S(2)}) copy-start(bf16[512,128]{1,0:T(8,128)(2,1)} %param.27) | copy-start | bytes 393220
  8.2 9.0 %copy-start.16 = (bf16[512,256]{1,0:T(8,128)(2,1)S(1)}, bf16[512,256]{1,0:T(8,128)(2,1)}, u32[]{:S(2)}) copy-start(bf16[512,256]{1,0:T(8,128)(2,1)} %param.17) | copy-start | bytes 786436
  9.6 182.2 %reduce-scatter.2.cloned.1.call-start = ((), (), s32[]{:S(2)}) async-start(), calls=%async_computation.2 | async-start | bytes 2228224 | tf_op jit(solution)/shard_map/reduce_scatter | solution.py:97
  10.8 7.6 %copy-start.14 = (s32[512]{0:T(512)S(1)}, s32[512]{0:T(512)}, u32[]{:S(2)}) copy-start(s32[512]{0:T(512)} %param.20) | copy-start | bytes 6148
  11.6 6.9 copy-start.10
  18.8 50.8 %copy-start.4 = (bf16[512,512]{1,0:T(8,128)(2,1)}, bf16[512,512]{1,0:T(8,128)(2,1)S(1)}, u32[]{:S(2)}) copy-start(bf16[512,512]{1,0:T(8,128)(2,1)S(1)} %fusion.14) | copy-start | bytes 1572868
  71.1 3.1 copy-start.1
  101.9 6.6 copy-start.15
  112.4 2.5 copy-start.2
  120.4 2.5 copy-start.2
  124.6 3.6 copy-start.13
  124.6 1.0 copy-start.5
  124.6 2.1 copy-start.11
  124.6 345.2 %all-reduce.6.cloned.1.call-start = ((), (), s32[]{:S(2)}) async-start(), calls=%async_computation.4 | async-start | bytes 1572864 | tf_op jit(solution)/shard_map/psum | solution.py:99
  126.7 618.0 %copy-start.6 = (f32[1024,128]{1,0:T(8,128)S(1)}, f32[1024,128]{1,0:T(8,128)}, u32[]{:S(2)}) copy-start(f32[1024,128]{1,0:T(8,128)} %param.24) | copy-start | bytes 1572868
  126.7 618.0 %copy-start.7 = (f32[1024,128]{1,0:T(8,128)S(1)}, f32[1024,128]{1,0:T(8,128)}, u32[]{:S(2)}) copy-start(f32[1024,128]{1,0:T(8,128)} %param.23) | copy-start | bytes 1572868
  128.2 614.5 %all-reduce.4.cloned.1.call-start = ((), (), s32[]{:S(2)}) async-start(), calls=%async_computation.3 | async-start | bytes 262144 | tf_op jit(solution)/shard_map/psum | solution.py:98
  471.8 274.2 %copy-start.8 = (f32[512,128]{1,0:T(8,128)S(1)}, f32[512,128]{1,0:T(8,128)}, u32[]{:S(2)}) copy-start(f32[512,128]{1,0:T(8,128)} %get-tuple-element.403) | copy-start | bytes 786436
Sparse Core Ops, SparseCore 0:
  10.7 43.6 all-gather.1
  124.7 67.0 reduce-scatter.1
  197.5 272.1 all-reduce.5
  472.5 270.1 all-reduce.3
where the time goes:
time: 767 us; the launch traced here: 753 us
  waiting for transfers between devices  648 us (84%)
  local copies, waits for them, and re-layouts  49 us (6%)
  matrix products  28.8 us (4%)
  between operations  14 us (2%)
  other arithmetic  13.3 us (2%)
    psum x1, waiting for transfers between devices, shards(): lax.psum((local_hidden, local_embed), ('dp', 'item'))  278 us
    psum x1, waiting for transfers between devices, shards(): owner_grad = lax.psum(summed, 'dp')  271 us
    reduce_scatter x1, waiting for transfers between devices, shards(): lax.psum_scatter(cand_grad, 'item', scatter_dimension=0, tiled=True)  63.5 us
    all_gather x1, waiting for transfers between devices, shards(): slab = lax.all_gather(local_slab, 'item', axis=0, tiled=True)  35.3 us
    gather x2, local copies, waits for them, and re-layouts, shards(): slab[next_slate]  16.7 us
    gather x2, local copies, waits for them, and re-layouts, shards(): slab[slate_ids]  16.7 us
  transfers between devices with their start and end apart: 4, of which 4 were waited for; matrix products, arithmetic and copies ran while one was open for 2% of the time, Pallas kernels for 0%

commit v1 on v0

v1 whole, which is shorter than its diff:
```python
import jax
import jax.numpy as jnp
from jax import lax
from jax.experimental import pallas as pl
from jax.experimental.pallas import tpu as pltpu
from jax.sharding import Mesh
from jax.sharding import PartitionSpec as P

ADAM_STEP = 10
PENALTY = 0.5
DISCOUNT = 0.9
BETA_ONE = 0.9
BETA_TWO = 0.999
EPSILON = 1e-08

AXES = ("h", "z", "x", "l", "c")
SIZES = (4, 8, 4, 2, 2)
ITEM = ("x", "l", "c")
CHIPS = 8
CORES = 2
BLOCK = 256
PACK = 352
SLATE = 10
F32 = jnp.float32
BF16 = jnp.bfloat16
NT = (((1,), (1,)), ((), ()))
NN = (((1,), (0,)), ((), ()))
PARAMS = pltpu.CompilerParams(vmem_limit_bytes=48 * 1024 * 1024)


def dot(left, right, dims=NN):
    return lax.dot_general(left, right, dims, preferred_element_type=F32)


def gather_kernel(rows_ref, table_ref, out_ref):
    row = rows_ref[...].astype(F32)
    eye = lax.broadcasted_iota(jnp.int32, (128, 128), 0) == lax.broadcasted_iota(
        jnp.int32, (128, 128), 1
    )
    width = table_ref.shape[0]
    lane = lax.broadcasted_iota(jnp.int32, (128, width), 1).astype(F32)
    table = table_ref[...].astype(BF16)
    for half in range(BLOCK // 128):
        part = row[:, half * 128 : half * 128 + 128]
        column = jnp.sum(jnp.where(eye, part, 0.0), axis=1, keepdims=True)
        onehot = (lane == column).astype(F32).astype(BF16)
        slab = dot(onehot, table).astype(BF16)
        for copy in range(out_ref.shape[0]):
            out_ref[copy, half * 128 : half * 128 + 128, :] = slab


def main_kernel(
    core_ref,
    states_ref,
    next_ref,
    rewards_ref,
    slate_ref,
    chosen_ref,
    upcoming_ref,
    own_ref,
    other_ref,
    w_hidden_ref,
    w_embed_ref,
    keep_ref,
    send_ref,
    delta_ref,
    hidden_t_ref,
    users_t_ref,
    next_users_ref,
    scores_ref,
    next_scores_ref,
    low_ref,
    high_ref,
    next_q_ref,
    grad_ref,
    grad_hidden_ref,
    grad_embed_ref,
):
    core = core_ref[0]
    sessions = states_ref.shape[0]
    slabs = (own_ref, other_ref)
    outs = (keep_ref, send_ref)
    w_hidden = w_hidden_ref[...]
    w_embed = w_embed_ref[...]

    hidden_t = jnp.maximum(dot(w_hidden.T, states_ref[...], NT), 0.0).astype(BF16)
    hidden_t_ref[...] = hidden_t
    users_t_ref[...] = dot(w_embed.T, hidden_t).astype(BF16)
    next_hidden = jnp.maximum(dot(next_ref[...], w_hidden), 0.0).astype(BF16)
    next_users_ref[...] = dot(next_hidden, w_embed).astype(BF16)

    flip = core * BLOCK
    slate = jnp.bitwise_xor(slate_ref[...], flip)
    place = lax.broadcasted_iota(jnp.int32, slate.shape, 0)
    clicked = jnp.sum(jnp.where(place == chosen_ref[...], slate, 0), axis=0, keepdims=True)
    upcoming = jnp.bitwise_xor(upcoming_ref[...], flip)
    padded = jnp.concatenate(
        [upcoming, jnp.zeros((128 - SLATE, sessions), jnp.int32)], axis=0
    )
    for part in range(sessions // 128):
        rows = slice(part * 128, part * 128 + 128)
        turned = padded[:, rows].astype(F32).T.astype(jnp.int32)
        low_ref[rows, :] = jnp.bitwise_and(turned, 127)
        high_ref[rows, :] = lax.shift_right_logical(turned, 7)

    sub = lax.broadcasted_iota(jnp.int32, (8, sessions), 0)
    behind = jnp.broadcast_to(clicked, (8, sessions)) - sub

    def forward(chip, carry):
        highest, picked = carry
        for side in range(CORES):
            block = chip * CORES + side
            slab = slabs[side][chip]
            scores = dot(slab, users_t_ref[...])
            scores_ref[block] = scores
            first = block * BLOCK
            for step in range(BLOCK // 8):
                piece = scores[step * 8 : step * 8 + 8]
                highest = jnp.maximum(highest, piece)
                picked = picked + jnp.where(behind == first + step * 8, piece, 0.0)
            next_scores = dot(next_users_ref[...], slab, NT)
            next_scores_ref[block * 2] = next_scores[:, :128]
            next_scores_ref[block * 2 + 1] = next_scores[:, 128:]
        return highest, picked

    highest, picked = lax.fori_loop(
        0,
        CHIPS,
        forward,
        (jnp.full((8, sessions), -jnp.inf, F32), jnp.zeros((8, sessions), F32)),
    )
    highest = jnp.max(highest, axis=0, keepdims=True)
    picked = jnp.sum(picked, axis=0, keepdims=True)

    def look_up(group, _):
        for inner in range(2):
            rows = pl.ds(pl.multiple_of(group * 16 + inner * 8, 8), 8)
            low = low_ref[rows, :]
            high = high_ref[rows, :]
            found = jnp.zeros((8, 128), F32)
            for chunk in range(next_scores_ref.shape[0]):
                piece = jnp.take_along_axis(next_scores_ref[chunk, rows, :], low, axis=1)
                found = jnp.where(high == chunk, piece, found)
            next_q_ref[rows, :] = found
        return 0

    lax.fori_loop(0, sessions // 16, look_up, 0)
    next_q = jnp.concatenate(
        [next_q_ref[part * 128 : part * 128 + 128, :].T[:16] for part in range(sessions // 128)],
        axis=1,
    )
    shown = lax.broadcasted_iota(jnp.int32, next_q.shape, 0) < SLATE
    top = jnp.max(jnp.where(shown, next_q, -jnp.inf), axis=0, keepdims=True)
    weights = jnp.where(shown, jnp.exp(next_q - top), 0.0)
    mean = jnp.sum(jnp.where(shown, weights * next_q, 0.0), axis=0, keepdims=True) / jnp.sum(
        weights, axis=0, keepdims=True
    )
    delta = picked - (rewards_ref[...] + DISCOUNT * mean)
    delta_ref[...] = delta

    def exponentials(block, total):
        for step in range(BLOCK // 8):
            rows = slice(step * 8, step * 8 + 8)
            piece = jnp.exp(scores_ref[block, rows, :] - highest)
            scores_ref[block, rows, :] = piece
            total = total + piece
        return total

    total = lax.fori_loop(
        0, CHIPS * CORES, exponentials, jnp.zeros((8, sessions), F32)
    )
    total = jnp.sum(total, axis=0, keepdims=True)
    scale = 1.0 / sessions
    gain = jnp.broadcast_to((PENALTY * scale) / total, (8, sessions))
    extra = jnp.broadcast_to((delta - PENALTY) * scale, (8, sessions))

    def backward(chip, user_grad_t):
        for side in range(CORES):
            block = chip * CORES + side
            first = block * BLOCK
            for step in range(BLOCK // 16):
                pieces = []
                for inner in range(2):
                    row = step * 16 + inner * 8
                    piece = scores_ref[block, row : row + 8, :] * gain
                    pieces.append(piece + jnp.where(behind == first + row, extra, 0.0))
                grad_ref[step * 16 : step * 16 + 16, :] = jnp.concatenate(pieces, axis=0).astype(
                    BF16
                )
            grad = grad_ref[...]
            slab = slabs[side][chip]
            user_grad_t = user_grad_t + dot(slab.T, grad)
            outs[side][chip, :BLOCK, :] = dot(grad, users_t_ref[...], NT).astype(BF16)
        return user_grad_t

    embed = own_ref.shape[2]
    user_grad_t = lax.fori_loop(0, CHIPS, backward, jnp.zeros((embed, sessions), F32)).astype(BF16)

    hidden_t = hidden_t_ref[...]
    grad_embed_ref[...] = dot(hidden_t, user_grad_t, NT)
    back = dot(w_embed, user_grad_t)
    pre_grad_t = jnp.where(hidden_t.astype(F32) > 0, back, 0.0).astype(BF16)
    grad_hidden_ref[...] = dot(states_ref[...].T, pre_grad_t, NT)
    for chip in range(CHIPS):
        for side in range(CORES):
            index = chip * CORES + jnp.bitwise_xor(core, side)
            rows = pl.ds(pl.multiple_of(index * 16, 16), 16)
            for quarter in range(4):
                at = BLOCK + quarter * 16
                outs[side][chip, at : at + 16, :] = grad_hidden_ref[
                    rows, quarter * 128 : quarter * 128 + 128
                ].astype(BF16)
            rows = pl.ds(pl.multiple_of(index * 32, 32), 32)
            outs[side][chip, BLOCK + 64 :, :] = grad_embed_ref[rows, :].astype(BF16)


def adam_kernel(
    rows_ref, grad_ref, first_ref, second_ref, tower_ref, new_first_ref, new_second_ref,
    direction_ref, grad_hidden_ref, grad_embed_ref,
):
    shape = (first_ref.shape[0], BLOCK)
    onehot = lax.broadcasted_iota(jnp.int32, shape, 0) == rows_ref[...]
    table_grad = dot(onehot.astype(F32).astype(BF16), grad_ref[...])
    new_first = BETA_ONE * first_ref[...] + (1.0 - BETA_ONE) * table_grad
    new_second = BETA_TWO * second_ref[...] + (1.0 - BETA_TWO) * table_grad * table_grad
    new_first_ref[...] = new_first
    new_second_ref[...] = new_second
    correct_one = 1.0 - BETA_ONE**ADAM_STEP
    correct_two = 1.0 - BETA_TWO**ADAM_STEP
    direction_ref[...] = new_first / correct_one / (jnp.sqrt(new_second / correct_two) + EPSILON)
    for item in range(CHIPS * CORES):
        for quarter in range(4):
            grad_hidden_ref[item * 16 : item * 16 + 16, quarter * 128 : quarter * 128 + 128] = (
                tower_ref[item, quarter * 16 : quarter * 16 + 16, :].astype(F32)
            )
        grad_embed_ref[item * 32 : item * 32 + 32, :] = tower_ref[item, 64:, :].astype(F32)


def spread(array, copies):
    return jnp.broadcast_to(array[None], (copies, *array.shape))


def swap(array, axes):
    return lax.all_to_all(array, axes, 0, 0, tiled=True)


def main_call(core, states, next_states, rewards, slate_t, chosen, next_slate_t, own, other, w_hidden, w_embed):
    sessions, features = states.shape
    hidden, embed = w_embed.shape
    vmem = pl.BlockSpec(memory_space=pltpu.VMEM)
    return pl.pallas_call(
        main_kernel,
        in_specs=[pl.BlockSpec(memory_space=pltpu.SMEM)] + [vmem] * 10,
        out_specs=[vmem] * 3,
        out_shape=[
            jax.ShapeDtypeStruct((CHIPS, PACK, embed), BF16),
            jax.ShapeDtypeStruct((CHIPS, PACK, embed), BF16),
            jax.ShapeDtypeStruct((1, sessions), F32),
        ],
        scratch_shapes=[
            pltpu.VMEM((hidden, sessions), BF16),
            pltpu.VMEM((embed, sessions), BF16),
            pltpu.VMEM((sessions, embed), BF16),
            pltpu.VMEM((CHIPS * CORES, BLOCK, sessions), F32),
            pltpu.VMEM((CHIPS * CORES * 2, sessions, 128), F32),
            pltpu.VMEM((sessions, 128), jnp.int32),
            pltpu.VMEM((sessions, 128), jnp.int32),
            pltpu.VMEM((sessions, 128), F32),
            pltpu.VMEM((BLOCK, sessions), BF16),
            pltpu.VMEM((features, hidden), F32),
            pltpu.VMEM((hidden, embed), F32),
        ],
        compiler_params=PARAMS,
    )(core, states, next_states, rewards, slate_t, chosen, next_slate_t, own, other, w_hidden, w_embed)


def shards(
    states,
    next_states,
    rewards,
    slate_ids,
    chosen,
    next_slate,
    table,
    first_moment,
    second_moment,
    cand_rows,
    w_hidden,
    w_embed,
):
    embed = table.shape[1]
    sessions = states.shape[0]
    vmem = pl.BlockSpec(memory_space=pltpu.VMEM)
    rows = cand_rows.reshape(1, BLOCK)
    pair = [(0, 1), (1, 0)]

    copies = pl.pallas_call(
        gather_kernel,
        in_specs=[vmem, vmem],
        out_specs=vmem,
        out_shape=jax.ShapeDtypeStruct((CHIPS, BLOCK, embed), BF16),
        compiler_params=PARAMS,
    )(rows, table)
    own = swap(copies, ("x", "l"))
    other = lax.ppermute(own, "c", pair)
    keep, send, delta = main_call(
        lax.axis_index("c").astype(jnp.int32).reshape(1),
        states,
        next_states,
        rewards.reshape(1, sessions),
        slate_ids.T,
        chosen.reshape(1, sessions),
        next_slate.T,
        own,
        other,
        w_hidden,
        w_embed,
    )
    got = lax.ppermute(send, "c", pair)
    part = (keep.astype(F32) + got.astype(F32)).astype(BF16)
    part = jnp.sum(swap(part, ("x", "l")).astype(F32), axis=0)
    part = swap(part.reshape(8, PACK // 8, embed), "z")
    part = jnp.sum(part, axis=0)
    part = jnp.sum(swap(spread(part, 4), "h"), axis=0).astype(BF16)
    whole = swap(spread(part, 8), "z").reshape(PACK, embed)
    tower = swap(spread(whole[BLOCK:], CHIPS * CORES), ITEM)

    moment = jax.ShapeDtypeStruct(first_moment.shape, F32)
    new_first, new_second, direction, grad_hidden, grad_embed = pl.pallas_call(
        adam_kernel,
        in_specs=[vmem] * 5,
        out_specs=[vmem] * 5,
        out_shape=[
            moment,
            moment,
            moment,
            jax.ShapeDtypeStruct(w_hidden.shape, F32),
            jax.ShapeDtypeStruct(w_embed.shape, F32),
        ],
        compiler_params=PARAMS,
    )(rows, whole[:BLOCK], first_moment, second_moment, tower)
    return (new_first, new_second, direction, grad_hidden, grad_embed, delta.reshape(sessions))


def solution(mesh):
    torus = Mesh(mesh.devices.reshape(SIZES), AXES)
    every = P(AXES)
    item = P(ITEM)
    placed = (every,) * 6 + (item,) * 4 + (P(), P())
    return jax.shard_map(
        shards,
        mesh=torus,
        in_specs=placed,
        out_specs=(item, item, item, P(), P(), every),
        check_vma=False,
    )
```

time: 767 us -> 119 us (0.16); the launches traced: 753 us -> 118 us
  waiting for transfers between devices: 648 us -> 11.8 us
  blocking collectives: 0 us -> 67.4 us
  local copies, waits for them, and re-layouts: 49 us -> 2.65 us
  matrix products: 28.8 us -> 0 us
  starting transfers between devices: 0.16 us -> 17.8 us
  Pallas kernels: 0 us -> 17.4 us
  between operations: 14 us -> 0.85 us
  other arithmetic: 13.3 us -> 0.34 us
    psum x2 -> x0, waiting for transfers between devices: 549 us -> none  [the longest x1 278 us: shards(): lax.psum((local_hidden, local_embed), ('dp', 'item'))]
    all_to_all x0 -> x5, blocking collectives: none -> 67.4 us  [swap(): return lax.all_to_all(array, axes, 0, 0, tiled=True)]
    reduce_scatter x1 -> x0, waiting for transfers between devices: 63.5 us -> none  [shards(): lax.psum_scatter(cand_grad, 'item', scatter_dimension=0, tiled=True)]
    gather x7 -> x0, local copies, waits for them, and re-layouts: 43.1 us -> none  [the longest x2 16.7 us: shards(): slab[next_slate]]
    all_gather x1 -> x0, waiting for transfers between devices: 35.3 us -> none  [shards(): slab = lax.all_gather(local_slab, 'item', axis=0, tiled=True)]
    dot_general x15 -> x0, matrix products: 28.8 us -> none  [the longest x2 5.32 us: forward(): scores = jnp.dot(users, block_slab.T, preferred_element_type=jnp.float32)]
    pallas_call x0 -> x3, Pallas kernels: none -> 17.4 us  [the longest x1 15.2 us: main_call(): pl.pallas_call(main_kernel, in_specs=[pl.BlockSpec(memory_space=pltpu.SME...]
    ppermute x0 -> x2, starting transfers between devices: none -> 8.95 us  [the longest x1 6.68 us: shards(): other = lax.ppermute(own, 'c', pair)]
  transfers between devices with their start and end apart: 4 -> 3, of which waited for: 4 -> 3; matrix products, arithmetic and copies ran while one was open for 2% -> 0% of each run, Pallas kernels for 0% -> 0%
where the time goes in v1:
time: 119 us; the launch traced here: 118 us
  blocking collectives  67.4 us (57%)
  starting transfers between devices  17.8 us (15%)
  Pallas kernels  17.4 us (15%)
  waiting for transfers between devices  11.8 us (10%)
  local copies, waits for them, and re-layouts  2.65 us (2%)
    all_to_all x5, blocking collectives, swap(): return lax.all_to_all(array, axes, 0, 0, tiled=True)  67.4 us
    pallas_call x1, Pallas kernels, main_call(): pl.pallas_call(main_kernel, in_specs=[pl.BlockSpec(memory_space=pltpu.SME...  15.2 us
    all_to_all x1, starting transfers between devices, swap(): return lax.all_to_all(array, axes, 0, 0, tiled=True)  8.81 us
    all_to_all x1, waiting for transfers between devices, swap(): return lax.all_to_all(array, axes, 0, 0, tiled=True)  8.46 us
    ppermute x1, starting transfers between devices, shards(): other = lax.ppermute(own, 'c', pair)  6.68 us
  transfers between devices with their start and end apart: 3, of which 3 were waited for; matrix products, arithmetic and copies ran while one was open for 0% of the time, Pallas kernels for 0%

profile of v1, /device:TPU:1, one launch (start us, length us, event | category | flops | bytes accessed | tf_op | source)
XLA Modules:
  0.0 118.2 jit_solution(10270855082551572102)
XLA Ops:
  0.6 0.0 copy-start
  0.6 1.0 copy-done
  1.7 0.0 copy-start.9
  1.7 0.7 copy-done.9
  2.4 0.4 shard_map.163
  2.7 0.0 copy-start.3
  2.7 0.0 copy-start.4
  2.7 0.0 copy-start.5
  2.8 0.0 copy-start.6
  2.8 0.0 copy-start.7
  2.8 0.0 copy-start.8
  2.8 0.0 copy-start.11
  2.8 0.0 copy-start.12
  2.8 13.3 %all_to_all.30.own_ref = bf16[8,256,128]{2,1,0:T(8,128)(2,1)S(1)} all-to-all(bf16[8,256,128]{2,1,0:T(8,128)(2,1)S(1)} %shard_map.163), channel_id=1, replica_groups=mesh['h'=4,'z'=8,'x'=4,'l'=2,'c'=2] {'x','l'}, dimensions={0} | all-to-all | bytes 1048576 | tf_op jit(solution)/shard_map/all_to_all | solution.py:244
  16.1 6.7 %collective-permute-start = (bf16[8,256,128]{2,1,0:T(8,128)(2,1)S(1)}, bf16[8,256,128]{2,1,0:T(8,128)(2,1)S(1)}, u32[]{:S(2)}, u32[]{:S(2)}) collective-permute-start(bf16[8,256,128]{2,1,0:T(8,128)(2,1)S(1)} %all_to_all.30.own_ref), channel_id=1, source_target_pairs={{0,1},{1,0},{2,3},{3,2},{4,5},{5,4},{6,7},{7,6},{8,9},{9,8},{10,11... | collective-permute-start | bytes 1572872 | tf_op jit(solution)/shard_map/ppermute | solution.py:305
  22.8 1.5 %collective-permute-done.other_ref = bf16[8,256,128]{2,1,0:T(8,128)(2,1)S(1)} collective-permute-done((bf16[8,256,128]{2,1,0:T(8,128)(2,1)S(1)}, bf16[8,256,128]{2,1,0:T(8,128)(2,1)S(1)}, u32[]{:S(2)}, u32[]{:S(2)}) %collective-permute-start) | collective-permute-done | bytes 524320 | tf_op jit(solution)/shard_map/ppermute | solution.py:305
  24.3 0.0 copy-done.3
  24.3 0.0 copy-done.4
  24.3 0.0 copy-done.5
  24.4 0.0 copy-done.6
  24.4 0.0 copy-done.7
  24.4 0.0 copy-done.8
  24.4 0.0 copy-done.11
  24.4 0.0 copy-done.12
  24.4 15.2 %shard_map.164 = (bf16[8,352,128]{2,1,0:T(8,128)(2,1)S(1)}, bf16[8,352,128]{2,1,0:T(8,128)(2,1)S(1)}, f32[1,512]{1,0:T(1,128)}) custom-call(s32[1]{0:T(128)} %bitcast.1.core_ref, bf16[512,256]{1,0:T(8,128)(2,1)S(1)} %copy-done.3, bf16[512,256]{1,0:T(8,128)(2,1)S(1)} %copy-done.4, f32[1,512]{1,0:T(1,128)S(1)} %bitcast.11, s32[10,512]{1,0:T(8,128)S(1)} %bitcast.7, ...), custom_call_target="tpu_custom_call" | custom-call | tf_op jit(solution)/shard_map/pallas_call | solution.py:251
  39.6 2.3 %collective-permute-start.1 = (bf16[8,352,128]{2,1,0:T(8,128)(2,1)S(1)}, bf16[8,352,128]{2,1,0:T(8,128)(2,1)S(1)}, u32[]{:S(2)}, u32[]{:S(2)}) collective-permute-start(bf16[8,352,128]{2,1,0:T(8,128)(2,1)S(1)} %get-tuple-element.15), channel_id=1, source_target_pairs={{0,1},{1,0},{2,3},{3,2},{4,5},{5,4},{6,7},{7,6},{8,9},{9,8},{10,11... | collective-permute-start | bytes 2162696 | tf_op jit(solution)/shard_map/ppermute | solution.py:319
  41.8 1.8 %collective-permute-done.1 = bf16[8,352,128]{2,1,0:T(8,128)(2,1)S(1)} collective-permute-done((bf16[8,352,128]{2,1,0:T(8,128)(2,1)S(1)}, bf16[8,352,128]{2,1,0:T(8,128)(2,1)S(1)}, u32[]{:S(2)}, u32[]{:S(2)}) %collective-permute-start.1) | collective-permute-done | bytes 720928 | tf_op jit(solution)/shard_map/ppermute | solution.py:319
  43.6 0.2 add_convert_fusion
  43.9 14.0 %all_to_all.31 = bf16[8,352,128]{2,1,0:T(8,128)(2,1)S(1)} all-to-all(bf16[8,352,128]{2,1,0:T(8,128)(2,1)S(1)} %add_convert_fusion), channel_id=1, replica_groups=mesh['h'=4,'z'=8,'x'=4,'l'=2,'c'=2] {'x','l'}, dimensions={0} | all-to-all | bytes 1441792 | tf_op jit(solution)/shard_map/all_to_all | solution.py:244
  57.9 0.1 convert_reduce_fusion
  58.0 17.4 %all_to_all.32 = f32[8,44,128]{2,1,0:T(8,128)S(1)} all-to-all(f32[8,44,128]{2,1,0:T(8,128)S(1)} %reshape.42), channel_id=1, replica_groups=mesh['h'=4,'z'=8,'x'=4,'l'=2,'c'=2] {'z'}, dimensions={0} | all-to-all | bytes 360448 | tf_op jit(solution)/shard_map/all_to_all | solution.py:244
  75.4 12.8 %all_to_all.33 = f32[4,44,128]{2,1,0:T(8,128)S(1)} all-to-all(f32[4,44,128]{2,1,0:T(8,128)S(1)} %broadcast_in_dim.6), channel_id=1, replica_groups=mesh['h'=4,'z'=8,'x'=4,'l'=2,'c'=2] {'h'}, dimensions={0} | all-to-all | bytes 180224 | tf_op jit(solution)/shard_map/all_to_all | solution.py:244
  88.2 10.0 %all_to_all.34 = bf16[8,44,128]{2,1,0:T(8,128)(2,1)S(1)} all-to-all(bf16[8,44,128]{2,1,0:T(8,128)(2,1)S(1)} %broadcast_in_dim.7), channel_id=1, replica_groups=mesh['h'=4,'z'=8,'x'=4,'l'=2,'c'=2] {'z'}, dimensions={0} | all-to-all | bytes 180224 | tf_op jit(solution)/shard_map/all_to_all | solution.py:244
  98.2 0.0 copy-start.1
  98.2 0.0 copy-start.2
  98.2 0.0 copy-start.10
  98.2 0.8 broadcast_in_dim.8
  99.0 8.8 %all-to-all-start.5 = ((bf16[16,96,128]{2,1,0:T(8,128)(2,1)}), bf16[16,96,128]{2,1,0:T(8,128)(2,1)S(1)}, u32[]{:S(2)}, u32[]{:S(2)}) async-start(bf16[16,96,128]{2,1,0:T(8,128)(2,1)} %broadcast_in_dim.8), calls=%async_computation.5 | async-start | bytes 786432 | tf_op jit(solution)/shard_map/all_to_all | solution.py:244
  107.8 8.5 %all-to-all-done.5.tower_ref = bf16[16,96,128]{2,1,0:T(8,128)(2,1)S(1)} async-done(((bf16[16,96,128]{2,1,0:T(8,128)(2,1)}), bf16[16,96,128]{2,1,0:T(8,128)(2,1)S(1)}, u32[]{:S(2)}, u32[]{:S(2)}) %all-to-all-start.5) | async-done | bytes 393248 | tf_op jit(solution)/shard_map/all_to_all | solution.py:244
  116.3 0.0 copy-done.1
  116.3 0.0 copy-done.2
  116.3 0.0 copy-done.10
  116.3 1.9 %shard_map.165 = (f32[1024,128]{1,0:T(8,128)}, f32[1024,128]{1,0:T(8,128)}, f32[1024,128]{1,0:T(8,128)}, f32[256,512]{1,0:T(8,128)}, f32[512,128]{1,0:T(8,128)}) custom-call(s32[1,256]{1,0:T(1,128)S(1)} %bitcast.10, bf16[256,128]{1,0:T(8,128)(2,1)S(1)} %slice.8.grad_ref, f32[1024,128]{1,0:T(8,128)S(1)} %copy-done.1, f32[1024,128]{1,0:T(8,128)S(1)} %copy-done.2, ...), custom_call_target="tpu_custom_call" | custom-call | tf_op jit(solution)/shard_map/pallas_call | solution.py:329
  (8 shorter events, 0.1 us)
Async XLA Ops:
  0.6 1.0 copy-start
  1.7 0.7 copy-start.9
  2.7 21.6 %copy-start.3 = (bf16[512,256]{1,0:T(8,128)(2,1)S(1)}, bf16[512,256]{1,0:T(8,128)(2,1)}, u32[]{:S(2)}) copy-start(bf16[512,256]{1,0:T(8,128)(2,1)} %states_ref.1) | copy-start | bytes 786436
  2.7 21.6 %copy-start.4 = (bf16[512,256]{1,0:T(8,128)(2,1)S(1)}, bf16[512,256]{1,0:T(8,128)(2,1)}, u32[]{:S(2)}) copy-start(bf16[512,256]{1,0:T(8,128)(2,1)} %next_ref.1) | copy-start | bytes 786436
  2.7 21.6 %copy-start.5 = (bf16[256,512]{1,0:T(8,128)(2,1)S(1)}, bf16[256,512]{1,0:T(8,128)(2,1)}, u32[]{:S(2)}) copy-start(bf16[256,512]{1,0:T(8,128)(2,1)} %w_hidden_ref.1) | copy-start | bytes 786436
  2.8 21.6 %copy-start.6 = (bf16[512,128]{1,0:T(8,128)(2,1)S(1)}, bf16[512,128]{1,0:T(8,128)(2,1)}, u32[]{:S(2)}) copy-start(bf16[512,128]{1,0:T(8,128)(2,1)} %w_embed_ref.1) | copy-start | bytes 393220
  2.8 21.6 %copy-start.7 = (s32[512,10]{0,1:T(8,128)S(1)}, s32[512,10]{0,1:T(8,128)}, u32[]{:S(2)}) copy-start(s32[512,10]{0,1:T(8,128)} %param.15) | copy-start | bytes 61444
  2.8 21.6 %copy-start.8 = (s32[512,10]{0,1:T(8,128)S(1)}, s32[512,10]{0,1:T(8,128)}, u32[]{:S(2)}) copy-start(s32[512,10]{0,1:T(8,128)} %param.17) | copy-start | bytes 61444
  2.8 21.6 %copy-start.11 = (f32[512]{0:T(512)S(1)}, f32[512]{0:T(512)}, u32[]{:S(2)}) copy-start(f32[512]{0:T(512)} %param.14) | copy-start | bytes 6148
  2.8 21.6 %copy-start.12 = (s32[512]{0:T(512)S(1)}, s32[512]{0:T(512)}, u32[]{:S(2)}) copy-start(s32[512]{0:T(512)} %param.16) | copy-start | bytes 6148
  16.1 8.2 %collective-permute-start = (bf16[8,256,128]{2,1,0:T(8,128)(2,1)S(1)}, bf16[8,256,128]{2,1,0:T(8,128)(2,1)S(1)}, u32[]{:S(2)}, u32[]{:S(2)}) collective-permute-start(bf16[8,256,128]{2,1,0:T(8,128)(2,1)S(1)} %all_to_all.30.own_ref), channel_id=1, source_target_pairs={{0,1},{1,0},{2,3},{3,2},{4,5},{5,4},{6,7},{7,6},{8,9},{9,8},{10,11... | collective-permute-start | bytes 1572872 | tf_op jit(solution)/shard_map/ppermute | solution.py:305
  39.6 4.1 %collective-permute-start.1 = (bf16[8,352,128]{2,1,0:T(8,128)(2,1)S(1)}, bf16[8,352,128]{2,1,0:T(8,128)(2,1)S(1)}, u32[]{:S(2)}, u32[]{:S(2)}) collective-permute-start(bf16[8,352,128]{2,1,0:T(8,128)(2,1)S(1)} %get-tuple-element.15), channel_id=1, source_target_pairs={{0,1},{1,0},{2,3},{3,2},{4,5},{5,4},{6,7},{7,6},{8,9},{9,8},{10,11... | collective-permute-start | bytes 2162696 | tf_op jit(solution)/shard_map/ppermute | solution.py:319
  98.2 18.1 %copy-start.1 = (f32[1024,128]{1,0:T(8,128)S(1)}, f32[1024,128]{1,0:T(8,128)}, u32[]{:S(2)}) copy-start(f32[1024,128]{1,0:T(8,128)} %first_ref.1) | copy-start | bytes 1572868
  98.2 18.1 %copy-start.2 = (f32[1024,128]{1,0:T(8,128)S(1)}, f32[1024,128]{1,0:T(8,128)}, u32[]{:S(2)}) copy-start(f32[1024,128]{1,0:T(8,128)} %second_ref.1) | copy-start | bytes 1572868
  98.2 18.1 %copy-start.10 = (s32[256]{0:T(256)S(1)}, s32[256]{0:T(256)}, u32[]{:S(2)}) copy-start(s32[256]{0:T(256)} %param.21) | copy-start | bytes 3076
  99.0 17.3 %all-to-all-start.5 = ((bf16[16,96,128]{2,1,0:T(8,128)(2,1)}), bf16[16,96,128]{2,1,0:T(8,128)(2,1)S(1)}, u32[]{:S(2)}, u32[]{:S(2)}) async-start(bf16[16,96,128]{2,1,0:T(8,128)(2,1)} %broadcast_in_dim.8), calls=%async_computation.5 | async-start | bytes 786432 | tf_op jit(solution)/shard_map/all_to_all | solution.py:244

commit v2 on v1

--- a/solution.py
+++ b/solution.py
@@ -20,6 +20,8 @@
 CORES = 2
 BLOCK = 256
 PACK = 352
+DP = 32
+PIECE = 12
 SLATE = 10
 F32 = jnp.float32
 BF16 = jnp.bfloat16
@@ -39,38 +41,70 @@
     )
     width = table_ref.shape[0]
     lane = lax.broadcasted_iota(jnp.int32, (128, width), 1).astype(F32)
-    table = table_ref[...].astype(BF16)
+    onehots = []
     for half in range(BLOCK // 128):
         part = row[:, half * 128 : half * 128 + 128]
         column = jnp.sum(jnp.where(eye, part, 0.0), axis=1, keepdims=True)
-        onehot = (lane == column).astype(F32).astype(BF16)
+        onehots.append((lane == column).astype(F32).astype(BF16))
+    table = table_ref[...].astype(BF16)
+    for half, onehot in enumerate(onehots):
         slab = dot(onehot, table).astype(BF16)
         for copy in range(out_ref.shape[0]):
             out_ref[copy, half * 128 : half * 128 + 128, :] = slab
 
 
+def tower_kernel(
+    core_ref,
+    states_ref,
+    next_ref,
+    upcoming_ref,
+    w_hidden_ref,
+    w_embed_ref,
+    hidden_t_ref,
+    users_t_ref,
+    next_users_ref,
+    low_ref,
+    high_ref,
+):
+    sessions = states_ref.shape[0]
+    w_hidden = w_hidden_ref[...]
+    w_embed = w_embed_ref[...]
+    hidden_t = jnp.maximum(dot(w_hidden.T, states_ref[...], NT), 0.0).astype(BF16)
+    hidden_t_ref[...] = hidden_t
+    users_t_ref[...] = dot(w_embed.T, hidden_t).astype(BF16)
+    next_hidden = jnp.maximum(dot(next_ref[...], w_hidden), 0.0).astype(BF16)
+    next_users_ref[...] = dot(next_hidden, w_embed).astype(BF16)
+
+    upcoming = jnp.bitwise_xor(upcoming_ref[...], core_ref[0] * BLOCK)
+    padded = jnp.concatenate(
+        [upcoming, jnp.zeros((128 - SLATE, sessions), jnp.int32)], axis=0
+    )
+    for part in range(sessions // 128):
+        rows = slice(part * 128, part * 128 + 128)
+        turned = padded[:, rows].astype(F32).T.astype(jnp.int32)
+        low_ref[rows, :] = jnp.bitwise_and(turned, 127)
+        high_ref[rows, :] = lax.shift_right_logical(turned, 7)
+
+
 def main_kernel(
     core_ref,
     states_ref,
-    next_ref,
+    hidden_t_ref,
+    users_t_ref,
+    next_users_ref,
+    low_ref,
+    high_ref,
     rewards_ref,
     slate_ref,
     chosen_ref,
-    upcoming_ref,
     own_ref,
     other_ref,
-    w_hidden_ref,
     w_embed_ref,
     keep_ref,
     send_ref,
     delta_ref,
-    hidden_t_ref,
-    users_t_ref,
-    next_users_ref,
     scores_ref,
     next_scores_ref,
-    low_ref,
-    high_ref,
     next_q_ref,
     grad_ref,
     grad_hidden_ref,
@@ -80,47 +114,48 @@
     sessions = states_ref.shape[0]
     slabs = (own_ref, other_ref)
     outs = (keep_ref, send_ref)
-    w_hidden = w_hidden_ref[...]
     w_embed = w_embed_ref[...]
 
-    hidden_t = jnp.maximum(dot(w_hidden.T, states_ref[...], NT), 0.0).astype(BF16)
-    hidden_t_ref[...] = hidden_t
-    users_t_ref[...] = dot(w_embed.T, hidden_t).astype(BF16)
-    next_hidden = jnp.maximum(dot(next_ref[...], w_hidden), 0.0).astype(BF16)
-    next_users_ref[...] = dot(next_hidden, w_embed).astype(BF16)
-
-    flip = core * BLOCK
-    slate = jnp.bitwise_xor(slate_ref[...], flip)
+    slate = jnp.bitwise_xor(slate_ref[...], core * BLOCK)
     place = lax.broadcasted_iota(jnp.int32, slate.shape, 0)
     clicked = jnp.sum(jnp.where(place == chosen_ref[...], slate, 0), axis=0, keepdims=True)
-    upcoming = jnp.bitwise_xor(upcoming_ref[...], flip)
-    padded = jnp.concatenate(
-        [upcoming, jnp.zeros((128 - SLATE, sessions), jnp.int32)], axis=0
-    )
-    for part in range(sessions // 128):
-        rows = slice(part * 128, part * 128 + 128)
-        turned = padded[:, rows].astype(F32).T.astype(jnp.int32)
-        low_ref[rows, :] = jnp.bitwise_and(turned, 127)
-        high_ref[rows, :] = lax.shift_right_logical(turned, 7)
-
     sub = lax.broadcasted_iota(jnp.int32, (8, sessions), 0)
     behind = jnp.broadcast_to(clicked, (8, sessions)) - sub
 
+    def next_forward(chip, _):
+        for side in range(CORES):
+            block = chip * CORES + side
+            next_scores = dot(next_users_ref[...], slabs[side][chip], NT)
+            next_scores_ref[block * 2] = next_scores[:, :128]
+            next_scores_ref[block * 2 + 1] = next_scores[:, 128:]
+        return 0
+
+    lax.fori_loop(0, CHIPS, next_forward, 0, unroll=8)
+
+    groups = sessions // 8 // CHIPS
+
     def forward(chip, carry):
         highest, picked = carry
+        for inner in range(groups):
+            rows = pl.ds(pl.multiple_of((chip * groups + inner) * 8, 8), 8)
+            low = low_ref[rows, :]
+            high = high_ref[rows, :]
+            found = jnp.zeros((8, 128), F32)
+            for chunk in range(next_scores_ref.shape[0]):
+                piece = jnp.take_along_axis(
+                    next_scores_ref[chunk, rows, :], low, axis=1, mode="promise_in_bounds"
+                )
+                found = jnp.where(high == chunk, piece, found)
+            next_q_ref[rows, :] = found
         for side in range(CORES):
             block = chip * CORES + side
-            slab = slabs[side][chip]
-            scores = dot(slab, users_t_ref[...])
+            scores = dot(slabs[side][chip], users_t_ref[...])
             scores_ref[block] = scores
             first = block * BLOCK
             for step in range(BLOCK // 8):
                 piece = scores[step * 8 : step * 8 + 8]
                 highest = jnp.maximum(highest, piece)
                 picked = picked + jnp.where(behind == first + step * 8, piece, 0.0)
-            next_scores = dot(next_users_ref[...], slab, NT)
-            next_scores_ref[block * 2] = next_scores[:, :128]
-            next_scores_ref[block * 2 + 1] = next_scores[:, 128:]
         return highest, picked
 
     highest, picked = lax.fori_loop(
@@ -128,23 +163,11 @@
         CHIPS,
         forward,
         (jnp.full((8, sessions), -jnp.inf, F32), jnp.zeros((8, sessions), F32)),
+        unroll=2,
     )
     highest = jnp.max(highest, axis=0, keepdims=True)
     picked = jnp.sum(picked, axis=0, keepdims=True)
 
-    def look_up(group, _):
-        for inner in range(2):
-            rows = pl.ds(pl.multiple_of(group * 16 + inner * 8, 8), 8)
-            low = low_ref[rows, :]
-            high = high_ref[rows, :]
-            found = jnp.zeros((8, 128), F32)
-            for chunk in range(next_scores_ref.shape[0]):
-                piece = jnp.take_along_axis(next_scores_ref[chunk, rows, :], low, axis=1)
-                found = jnp.where(high == chunk, piece, found)
-            next_q_ref[rows, :] = found
-        return 0
-
-    lax.fori_loop(0, sessions // 16, look_up, 0)
     next_q = jnp.concatenate(
         [next_q_ref[part * 128 : part * 128 + 128, :].T[:16] for part in range(sessions // 128)],
         axis=1,
@@ -167,7 +190,7 @@
         return total
 
     total = lax.fori_loop(
-        0, CHIPS * CORES, exponentials, jnp.zeros((8, sessions), F32)
+        0, CHIPS * CORES, exponentials, jnp.zeros((8, sessions), F32), unroll=4
     )
     total = jnp.sum(total, axis=0, keepdims=True)
     scale = 1.0 / sessions
@@ -194,7 +217,9 @@
         return user_grad_t
 
     embed = own_ref.shape[2]
-    user_grad_t = lax.fori_loop(0, CHIPS, backward, jnp.zeros((embed, sessions), F32)).astype(BF16)
+    user_grad_t = lax.fori_loop(
+        0, CHIPS, backward, jnp.zeros((embed, sessions), F32), unroll=4
+    ).astype(BF16)
 
     hidden_t = hidden_t_ref[...]
     grad_embed_ref[...] = dot(hidden_t, user_grad_t, NT)
@@ -215,8 +240,7 @@
 
 
 def adam_kernel(
-    rows_ref, grad_ref, first_ref, second_ref, tower_ref, new_first_ref, new_second_ref,
-    direction_ref, grad_hidden_ref, grad_embed_ref,
+    rows_ref, grad_ref, first_ref, second_ref, new_first_ref, new_second_ref, direction_ref
 ):
     shape = (first_ref.shape[0], BLOCK)
     onehot = lax.broadcasted_iota(jnp.int32, shape, 0) == rows_ref[...]
@@ -228,6 +252,9 @@
     correct_one = 1.0 - BETA_ONE**ADAM_STEP
     correct_two = 1.0 - BETA_TWO**ADAM_STEP
     direction_ref[...] = new_first / correct_one / (jnp.sqrt(new_second / correct_two) + EPSILON)
+
+
+def unpack_kernel(tower_ref, grad_hidden_ref, grad_embed_ref):
     for item in range(CHIPS * CORES):
         for quarter in range(4):
             grad_hidden_ref[item * 16 : item * 16 + 16, quarter * 128 : quarter * 128 + 128] = (
@@ -244,13 +271,33 @@
     return lax.all_to_all(array, axes, 0, 0, tiled=True)
 
 
-def main_call(core, states, next_states, rewards, slate_t, chosen, next_slate_t, own, other, w_hidden, w_embed):
+def tower_call(core, states, next_states, next_slate_t, w_hidden, w_embed):
+    sessions = states.shape[0]
+    hidden, embed = w_embed.shape
+    vmem = pl.BlockSpec(memory_space=pltpu.VMEM)
+    places = jax.ShapeDtypeStruct((sessions, 128), jnp.int32)
+    return pl.pallas_call(
+        tower_kernel,
+        in_specs=[pl.BlockSpec(memory_space=pltpu.SMEM)] + [vmem] * 5,
+        out_specs=[vmem] * 5,
+        out_shape=[
+            jax.ShapeDtypeStruct((hidden, sessions), BF16),
+            jax.ShapeDtypeStruct((embed, sessions), BF16),
+            jax.ShapeDtypeStruct((sessions, embed), BF16),
+            places,
+            places,
+        ],
+        compiler_params=PARAMS,
+    )(core, states, next_states, next_slate_t, w_hidden, w_embed)
+
+
+def main_call(core, states, towers, rewards, slate_t, chosen, own, other, w_embed):
     sessions, features = states.shape
     hidden, embed = w_embed.shape
     vmem = pl.BlockSpec(memory_space=pltpu.VMEM)
     return pl.pallas_call(
         main_kernel,
-        in_specs=[pl.BlockSpec(memory_space=pltpu.SMEM)] + [vmem] * 10,
+        in_specs=[pl.BlockSpec(memory_space=pltpu.SMEM)] + [vmem] * 12,
         out_specs=[vmem] * 3,
         out_shape=[
             jax.ShapeDtypeStruct((CHIPS, PACK, embed), BF16),
@@ -258,20 +305,15 @@
             jax.ShapeDtypeStruct((1, sessions), F32),
         ],
         scratch_shapes=[
-            pltpu.VMEM((hidden, sessions), BF16),
-            pltpu.VMEM((embed, sessions), BF16),
-            pltpu.VMEM((sessions, embed), BF16),
             pltpu.VMEM((CHIPS * CORES, BLOCK, sessions), F32),
             pltpu.VMEM((CHIPS * CORES * 2, sessions, 128), F32),
-            pltpu.VMEM((sessions, 128), jnp.int32),
-            pltpu.VMEM((sessions, 128), jnp.int32),
             pltpu.VMEM((sessions, 128), F32),
             pltpu.VMEM((BLOCK, sessions), BF16),
             pltpu.VMEM((features, hidden), F32),
             pltpu.VMEM((hidden, embed), F32),
         ],
         compiler_params=PARAMS,
-    )(core, states, next_states, rewards, slate_t, chosen, next_slate_t, own, other, w_hidden, w_embed)
+    )(core, states, *towers, rewards, slate_t, chosen, own, other, w_embed)
 
 
 def shards(
@@ -296,49 +338,53 @@
 
     copies = pl.pallas_call(
         gather_kernel,
-        in_specs=[vmem, vmem],
+        in_specs=[vmem] * 2,
         out_specs=vmem,
         out_shape=jax.ShapeDtypeStruct((CHIPS, BLOCK, embed), BF16),
         compiler_params=PARAMS,
     )(rows, table)
+    core = lax.axis_index("c").astype(jnp.int32).reshape(1)
+    towers = tower_call(core, states, next_states, next_slate.T, w_hidden, w_embed)
     own = swap(copies, ("x", "l"))
     other = lax.ppermute(own, "c", pair)
     keep, send, delta = main_call(
-        lax.axis_index("c").astype(jnp.int32).reshape(1),
+        core,
         states,
-        next_states,
+        towers,
         rewards.reshape(1, sessions),
         slate_ids.T,
         chosen.reshape(1, sessions),
-        next_slate.T,
         own,
         other,
-        w_hidden,
         w_embed,
     )
+
     got = lax.ppermute(send, "c", pair)
     part = (keep.astype(F32) + got.astype(F32)).astype(BF16)
     part = jnp.sum(swap(part, ("x", "l")).astype(F32), axis=0)
-    part = swap(part.reshape(8, PACK // 8, embed), "z")
-    part = jnp.sum(part, axis=0)
-    part = jnp.sum(swap(spread(part, 4), "h"), axis=0).astype(BF16)
-    whole = swap(spread(part, 8), "z").reshape(PACK, embed)
-    tower = swap(spread(whole[BLOCK:], CHIPS * CORES), ITEM)
+    part = jnp.pad(part, ((0, PIECE * DP - PACK), (0, 0))).reshape(DP, PIECE, embed)
+    part = jnp.sum(swap(part, ("h", "z")), axis=0).astype(BF16)
+    whole = swap(spread(part, DP), ("h", "z")).reshape(DP * PIECE, embed)
+    tower = swap(spread(whole[BLOCK:PACK], CHIPS * CORES), ITEM)
 
     moment = jax.ShapeDtypeStruct(first_moment.shape, F32)
-    new_first, new_second, direction, grad_hidden, grad_embed = pl.pallas_call(
+    new_first, new_second, direction = pl.pallas_call(
         adam_kernel,
-        in_specs=[vmem] * 5,
-        out_specs=[vmem] * 5,
+        in_specs=[vmem] * 4,
+        out_specs=[vmem] * 3,
+        out_shape=[moment, moment, moment],
+        compiler_params=PARAMS,
+    )(rows, whole[:BLOCK], first_moment, second_moment)
+    grad_hidden, grad_embed = pl.pallas_call(
+        unpack_kernel,
+        in_specs=[vmem],
+        out_specs=[vmem] * 2,
         out_shape=[
-            moment,
-            moment,
-            moment,
             jax.ShapeDtypeStruct(w_hidden.shape, F32),
             jax.ShapeDtypeStruct(w_embed.shape, F32),
         ],
         compiler_params=PARAMS,
-    )(rows, whole[:BLOCK], first_moment, second_moment, tower)
+    )(tower)
     return (new_first, new_second, direction, grad_hidden, grad_embed, delta.reshape(sessions))
 
 

time: 119 us -> 112 us (0.941)
  Pallas kernels: 17.4 us -> 13 us
  blocking collectives: 67.4 us -> 70.6 us
  starting transfers between devices: 17.8 us -> 14.7 us
  waiting for transfers between devices: 11.8 us -> 9.15 us
    pallas_call x1, Pallas kernels: 15.2 us -> 9.2 us  [main_call(): pl.pallas_call(main_kernel, in_specs=[pl.BlockSpec(memory_space=pltpu.SME...]
    all_to_all x5 -> x4, blocking collectives: 67.4 us -> 70.6 us  [swap(): return lax.all_to_all(array, axes, 0, 0, tiled=True)]
    all_to_all x1, starting transfers between devices: 8.81 us -> 5.65 us  [swap(): return lax.all_to_all(array, axes, 0, 0, tiled=True)]
    all_to_all x1, waiting for transfers between devices: 8.46 us -> 6.78 us  [swap(): return lax.all_to_all(array, axes, 0, 0, tiled=True)]
    pallas_call x2 -> x4, Pallas kernels: 2.26 us -> 3.82 us  [the longest x1 1.65 us: shards(): pl.pallas_call(adam_kernel, in_specs=[vmem] * 4, out_specs=[vmem] * 3, ou...]
  transfers between devices with their start and end apart: 3 -> 3, of which waited for: 3 -> 3; matrix products, arithmetic and copies ran while one was open for 0% -> 0% of each run, Pallas kernels for 0% -> 2%
where the time goes in v2:
time: 112 us; the launch traced here: 111 us
  blocking collectives  70.6 us (63%)
  starting transfers between devices  14.7 us (13%)
  Pallas kernels  13 us (12%)
  waiting for transfers between devices  9.15 us (8%)
  local copies, waits for them, and re-layouts  2.66 us (2%)
    all_to_all x4, blocking collectives, swap(): return lax.all_to_all(array, axes, 0, 0, tiled=True)  70.6 us
    pallas_call x1, Pallas kernels, main_call(): pl.pallas_call(main_kernel, in_specs=[pl.BlockSpec(memory_space=pltpu.SME...  9.2 us
    ppermute x1, starting transfers between devices, shards(): other = lax.ppermute(own, 'c', pair)  6.81 us
    all_to_all x1, waiting for transfers between devices, swap(): return lax.all_to_all(array, axes, 0, 0, tiled=True)  6.78 us
    all_to_all x1, starting transfers between devices, swap(): return lax.all_to_all(array, axes, 0, 0, tiled=True)  5.65 us
    ppermute x1, starting transfers between devices, shards(): got = lax.ppermute(send, 'c', pair)  2.28 us
  transfers between devices with their start and end apart: 3, of which 3 were waited for; matrix products, arithmetic and copies ran while one was open for 0% of the time, Pallas kernels for 2%

profile of v2, /device:TPU:1, one launch (start us, length us, event | category | flops | bytes accessed | tf_op | source)
XLA Modules:
  0.0 111.3 jit_solution(14727012564168865880)
XLA Ops:
  0.6 0.0 copy-start.2
  0.6 1.0 copy-done.2
  1.7 0.0 copy-start.9
  1.7 0.7 copy-done.9
  2.4 0.4 shard_map.164
  2.7 0.0 copy-start
  2.7 0.0 copy-start.1
  2.7 0.0 copy-start.5
  2.8 0.0 copy-start.6
  2.8 0.0 copy-start.8
  2.8 13.3 %all_to_all.25.own_ref = bf16[8,256,128]{2,1,0:T(8,128)(2,1)S(1)} all-to-all(bf16[8,256,128]{2,1,0:T(8,128)(2,1)S(1)} %shard_map.164), channel_id=1, replica_groups=mesh['h'=4,'z'=8,'x'=4,'l'=2,'c'=2] {'x','l'}, dimensions={0} | all-to-all | bytes 1048576 | tf_op jit(solution)/shard_map/all_to_all | solution.py:271
  16.1 0.0 copy-start.7
  16.1 0.0 copy-start.11
  16.1 0.0 copy-start.12
  16.1 6.8 %collective-permute-start = (bf16[8,256,128]{2,1,0:T(8,128)(2,1)S(1)}, bf16[8,256,128]{2,1,0:T(8,128)(2,1)S(1)}, u32[]{:S(2)}, u32[]{:S(2)}) collective-permute-start(bf16[8,256,128]{2,1,0:T(8,128)(2,1)S(1)} %all_to_all.25.own_ref), channel_id=1, source_target_pairs={{0,1},{1,0},{2,3},{3,2},{4,5},{5,4},{6,7},{7,6},{8,9},{9,8},{10,11... | collective-permute-start | bytes 1572872 | tf_op jit(solution)/shard_map/ppermute | solution.py:349
  22.9 0.0 copy-done
  22.9 0.0 copy-done.1
  23.0 0.0 copy-done.5
  23.0 0.0 copy-done.6
  23.0 0.0 copy-done.8
  23.0 0.9 shard_map.163
  23.9 0.6 collective-permute-done.other_ref
  24.4 0.0 copy-done.7
  24.4 0.0 copy-done.11
  24.4 0.0 copy-done.12
  24.5 9.2 %shard_map.165 = (bf16[8,352,128]{2,1,0:T(8,128)(2,1)S(1)}, bf16[8,352,128]{2,1,0:T(8,128)(2,1)S(1)}, f32[1,512]{1,0:T(1,128)}) custom-call(s32[1]{0:T(128)} %bitcast.1.core_ref, bf16[512,256]{1,0:T(8,128)(2,1)S(1)} %copy-done, bf16[512,512]{1,0:T(8,128)(2,1)S(1)} %get-tuple-element.19.hidden_t_ref, bf16[128,512]{1,0:T(8,128)(2,1)S(1)} %get-tuple-element.20.users_t_ref, ...), custom_call_target="tpu_custom_call" | custom-call | tf_op jit(solution)/shard_map/pallas_call | solution.py:298
  33.7 2.3 %collective-permute-start.1 = (bf16[8,352,128]{2,1,0:T(8,128)(2,1)S(1)}, bf16[8,352,128]{2,1,0:T(8,128)(2,1)S(1)}, u32[]{:S(2)}, u32[]{:S(2)}) collective-permute-start(bf16[8,352,128]{2,1,0:T(8,128)(2,1)S(1)} %get-tuple-element.25), channel_id=1, source_target_pairs={{0,1},{1,0},{2,3},{3,2},{4,5},{5,4},{6,7},{7,6},{8,9},{9,8},{10,11... | collective-permute-start | bytes 2162696 | tf_op jit(solution)/shard_map/ppermute | solution.py:362
  35.9 1.8 %collective-permute-done.1 = bf16[8,352,128]{2,1,0:T(8,128)(2,1)S(1)} collective-permute-done((bf16[8,352,128]{2,1,0:T(8,128)(2,1)S(1)}, bf16[8,352,128]{2,1,0:T(8,128)(2,1)S(1)}, u32[]{:S(2)}, u32[]{:S(2)}) %collective-permute-start.1) | collective-permute-done | bytes 720928 | tf_op jit(solution)/shard_map/ppermute | solution.py:362
  37.7 0.2 add_convert_fusion
  37.9 14.0 %all_to_all.26 = bf16[8,352,128]{2,1,0:T(8,128)(2,1)S(1)} all-to-all(bf16[8,352,128]{2,1,0:T(8,128)(2,1)S(1)} %add_convert_fusion), channel_id=1, replica_groups=mesh['h'=4,'z'=8,'x'=4,'l'=2,'c'=2] {'x','l'}, dimensions={0} | all-to-all | bytes 1441792 | tf_op jit(solution)/shard_map/all_to_all | solution.py:271
  51.9 0.1 convert_reduce_fusion
  52.1 25.6 %all_to_all.27 = f32[32,12,128]{2,1,0:T(8,128)S(1)} all-to-all(f32[32,12,128]{2,1,0:T(8,128)S(1)} %reshape.41), channel_id=1, replica_groups=mesh['h'=4,'z'=8,'x'=4,'l'=2,'c'=2] {'h','z'}, dimensions={0} | all-to-all | bytes 393216 | tf_op jit(solution)/shard_map/all_to_all | solution.py:271
  77.8 17.6 %all_to_all.28 = bf16[32,12,128]{2,1,0:T(8,128)(2,1)S(1)} all-to-all(bf16[32,12,128]{2,1,0:T(8,128)(2,1)S(1)} %broadcast_in_dim.4), channel_id=1, replica_groups=mesh['h'=4,'z'=8,'x'=4,'l'=2,'c'=2] {'h','z'}, dimensions={0} | all-to-all | bytes 196608 | tf_op jit(solution)/shard_map/all_to_all | solution.py:271
  95.4 0.0 copy-start.3
  95.4 0.0 copy-start.4
  95.4 0.0 copy-start.10
  95.5 0.8 broadcast_in_dim.5
  96.3 5.7 %all-to-all-start.4 = ((bf16[16,96,128]{2,1,0:T(8,128)(2,1)}), bf16[16,96,128]{2,1,0:T(8,128)(2,1)S(1)}, u32[]{:S(2)}, u32[]{:S(2)}) async-start(bf16[16,96,128]{2,1,0:T(8,128)(2,1)} %broadcast_in_dim.5), calls=%async_computation.4 | async-start | bytes 786432 | tf_op jit(solution)/shard_map/all_to_all | solution.py:271
  101.9 0.0 copy-done.3
  101.9 0.0 copy-done.4
  101.9 0.0 copy-done.10
  102.0 1.6 %shard_map.166 = (f32[1024,128]{1,0:T(8,128)}, f32[1024,128]{1,0:T(8,128)}, f32[1024,128]{1,0:T(8,128)}) custom-call(s32[1,256]{1,0:T(1,128)S(1)} %bitcast.10, bf16[256,128]{1,0:T(8,128)(2,1)S(1)} %slice.8.grad_ref, f32[1024,128]{1,0:T(8,128)S(1)} %copy-done.3, f32[1024,128]{1,0:T(8,128)S(1)} %copy-done.4), custom_call_target="tpu_custom_call" | custom-call | tf_op jit(solution)/shard_map/pallas_call | solution.py:371
  103.6 6.8 %all-to-all-done.4.tower_ref = bf16[16,96,128]{2,1,0:T(8,128)(2,1)S(1)} async-done(((bf16[16,96,128]{2,1,0:T(8,128)(2,1)}), bf16[16,96,128]{2,1,0:T(8,128)(2,1)S(1)}, u32[]{:S(2)}, u32[]{:S(2)}) %all-to-all-start.4) | async-done | bytes 393248 | tf_op jit(solution)/shard_map/all_to_all | solution.py:271
  110.4 0.9 shard_map.167
  (7 shorter events, 0.1 us)
Async XLA Ops:
  0.6 1.0 copy-start.2
  1.7 0.7 copy-start.9
  2.7 20.2 %copy-start = (bf16[512,256]{1,0:T(8,128)(2,1)S(1)}, bf16[512,256]{1,0:T(8,128)(2,1)}, u32[]{:S(2)}) copy-start(bf16[512,256]{1,0:T(8,128)(2,1)} %states_ref.3) | copy-start | bytes 786436
  2.7 20.2 %copy-start.1 = (bf16[512,128]{1,0:T(8,128)(2,1)S(1)}, bf16[512,128]{1,0:T(8,128)(2,1)}, u32[]{:S(2)}) copy-start(bf16[512,128]{1,0:T(8,128)(2,1)} %w_embed_ref.3) | copy-start | bytes 393220
  2.7 20.2 %copy-start.5 = (bf16[512,256]{1,0:T(8,128)(2,1)S(1)}, bf16[512,256]{1,0:T(8,128)(2,1)}, u32[]{:S(2)}) copy-start(bf16[512,256]{1,0:T(8,128)(2,1)} %next_ref.1) | copy-start | bytes 786436
  2.8 20.2 %copy-start.6 = (bf16[256,512]{1,0:T(8,128)(2,1)S(1)}, bf16[256,512]{1,0:T(8,128)(2,1)}, u32[]{:S(2)}) copy-start(bf16[256,512]{1,0:T(8,128)(2,1)} %w_hidden_ref.1) | copy-start | bytes 786436
  2.8 20.2 %copy-start.8 = (s32[512,10]{0,1:T(8,128)S(1)}, s32[512,10]{0,1:T(8,128)}, u32[]{:S(2)}) copy-start(s32[512,10]{0,1:T(8,128)} %param.17) | copy-start | bytes 61444
  16.1 8.3 %copy-start.7 = (s32[512,10]{0,1:T(8,128)S(1)}, s32[512,10]{0,1:T(8,128)}, u32[]{:S(2)}) copy-start(s32[512,10]{0,1:T(8,128)} %param.15) | copy-start | bytes 61444
  16.1 8.3 %copy-start.11 = (f32[512]{0:T(512)S(1)}, f32[512]{0:T(512)}, u32[]{:S(2)}) copy-start(f32[512]{0:T(512)} %param.14) | copy-start | bytes 6148
  16.1 8.3 %copy-start.12 = (s32[512]{0:T(512)S(1)}, s32[512]{0:T(512)}, u32[]{:S(2)}) copy-start(s32[512]{0:T(512)} %param.16) | copy-start | bytes 6148
  16.1 8.3 %collective-permute-start = (bf16[8,256,128]{2,1,0:T(8,128)(2,1)S(1)}, bf16[8,256,128]{2,1,0:T(8,128)(2,1)S(1)}, u32[]{:S(2)}, u32[]{:S(2)}) collective-permute-start(bf16[8,256,128]{2,1,0:T(8,128)(2,1)S(1)} %all_to_all.25.own_ref), channel_id=1, source_target_pairs={{0,1},{1,0},{2,3},{3,2},{4,5},{5,4},{6,7},{7,6},{8,9},{9,8},{10,11... | collective-permute-start | bytes 1572872 | tf_op jit(solution)/shard_map/ppermute | solution.py:349
  33.7 4.1 %collective-permute-start.1 = (bf16[8,352,128]{2,1,0:T(8,128)(2,1)S(1)}, bf16[8,352,128]{2,1,0:T(8,128)(2,1)S(1)}, u32[]{:S(2)}, u32[]{:S(2)}) collective-permute-start(bf16[8,352,128]{2,1,0:T(8,128)(2,1)S(1)} %get-tuple-element.25), channel_id=1, source_target_pairs={{0,1},{1,0},{2,3},{3,2},{4,5},{5,4},{6,7},{7,6},{8,9},{9,8},{10,11... | collective-permute-start | bytes 2162696 | tf_op jit(solution)/shard_map/ppermute | solution.py:362
  95.4 6.5 %copy-start.3 = (f32[1024,128]{1,0:T(8,128)S(1)}, f32[1024,128]{1,0:T(8,128)}, u32[]{:S(2)}) copy-start(f32[1024,128]{1,0:T(8,128)} %first_ref.1) | copy-start | bytes 1572868
  95.4 6.5 %copy-start.4 = (f32[1024,128]{1,0:T(8,128)S(1)}, f32[1024,128]{1,0:T(8,128)}, u32[]{:S(2)}) copy-start(f32[1024,128]{1,0:T(8,128)} %second_ref.1) | copy-start | bytes 1572868
  95.4 6.5 %copy-start.10 = (s32[256]{0:T(256)S(1)}, s32[256]{0:T(256)}, u32[]{:S(2)}) copy-start(s32[256]{0:T(256)} %param.21) | copy-start | bytes 3076
  96.3 14.1 %all-to-all-start.4 = ((bf16[16,96,128]{2,1,0:T(8,128)(2,1)}), bf16[16,96,128]{2,1,0:T(8,128)(2,1)S(1)}, u32[]{:S(2)}, u32[]{:S(2)}) async-start(bf16[16,96,128]{2,1,0:T(8,128)(2,1)} %broadcast_in_dim.5), calls=%async_computation.4 | async-start | bytes 786432 | tf_op jit(solution)/shard_map/all_to_all | solution.py:271

commit v3 on v2

--- a/solution.py
+++ b/solution.py
@@ -21,7 +21,8 @@
 BLOCK = 256
 PACK = 352
 DP = 32
-PIECE = 12
+PIECE = 16
+TOWER_PIECES = (PACK - BLOCK) // 8
 SLATE = 10
 F32 = jnp.float32
 BF16 = jnp.bfloat16
@@ -122,22 +123,19 @@
     sub = lax.broadcasted_iota(jnp.int32, (8, sessions), 0)
     behind = jnp.broadcast_to(clicked, (8, sessions)) - sub
 
-    def next_forward(chip, _):
-        for side in range(CORES):
-            block = chip * CORES + side
-            next_scores = dot(next_users_ref[...], slabs[side][chip], NT)
-            next_scores_ref[block * 2] = next_scores[:, :128]
-            next_scores_ref[block * 2 + 1] = next_scores[:, 128:]
-        return 0
-
-    lax.fori_loop(0, CHIPS, next_forward, 0, unroll=8)
-
-    groups = sessions // 8 // CHIPS
-
-    def forward(chip, carry):
-        highest, picked = carry
-        for inner in range(groups):
-            rows = pl.ds(pl.multiple_of((chip * groups + inner) * 8, 8), 8)
+    blocks = [(chip, side) for chip in range(CHIPS) for side in range(CORES)]
+    next_users = next_users_ref[...]
+    for block, (chip, side) in enumerate(blocks):
+        next_scores = dot(next_users, slabs[side][chip], NT)
+        next_scores_ref[block * 2] = next_scores[:, :128]
+        next_scores_ref[block * 2 + 1] = next_scores[:, 128:]
+
+    highest = jnp.full((8, sessions), -jnp.inf, F32)
+    picked = jnp.zeros((8, sessions), F32)
+    groups = sessions // 8 // len(blocks)
+    for block, (chip, side) in enumerate(blocks):
+        for group in range(block * groups, (block + 1) * groups):
+            rows = slice(group * 8, group * 8 + 8)
             low = low_ref[rows, :]
             high = high_ref[rows, :]
             found = jnp.zeros((8, 128), F32)
@@ -147,24 +145,12 @@
                 )
                 found = jnp.where(high == chunk, piece, found)
             next_q_ref[rows, :] = found
-        for side in range(CORES):
-            block = chip * CORES + side
-            scores = dot(slabs[side][chip], users_t_ref[...])
-            scores_ref[block] = scores
-            first = block * BLOCK
-            for step in range(BLOCK // 8):
-                piece = scores[step * 8 : step * 8 + 8]
-                highest = jnp.maximum(highest, piece)
-                picked = picked + jnp.where(behind == first + step * 8, piece, 0.0)
-        return highest, picked
-
-    highest, picked = lax.fori_loop(
-        0,
-        CHIPS,
-        forward,
-        (jnp.full((8, sessions), -jnp.inf, F32), jnp.zeros((8, sessions), F32)),
-        unroll=2,
-    )
+        scores = dot(slabs[side][chip], users_t_ref[...])
+        scores_ref[block] = scores
+        for step in range(BLOCK // 8):
+            piece = scores[step * 8 : step * 8 + 8]
+            highest = jnp.maximum(highest, piece)
+            picked = jnp.where(behind == block * BLOCK + step * 8, piece, picked)
     highest = jnp.max(highest, axis=0, keepdims=True)
     picked = jnp.sum(picked, axis=0, keepdims=True)
 
@@ -190,36 +176,31 @@
         return total
 
     total = lax.fori_loop(
-        0, CHIPS * CORES, exponentials, jnp.zeros((8, sessions), F32), unroll=4
+        0, CHIPS * CORES, exponentials, jnp.zeros((8, sessions), F32), unroll=8
     )
     total = jnp.sum(total, axis=0, keepdims=True)
     scale = 1.0 / sessions
     gain = jnp.broadcast_to((PENALTY * scale) / total, (8, sessions))
     extra = jnp.broadcast_to((delta - PENALTY) * scale, (8, sessions))
 
-    def backward(chip, user_grad_t):
-        for side in range(CORES):
-            block = chip * CORES + side
-            first = block * BLOCK
-            for step in range(BLOCK // 16):
-                pieces = []
-                for inner in range(2):
-                    row = step * 16 + inner * 8
-                    piece = scores_ref[block, row : row + 8, :] * gain
-                    pieces.append(piece + jnp.where(behind == first + row, extra, 0.0))
-                grad_ref[step * 16 : step * 16 + 16, :] = jnp.concatenate(pieces, axis=0).astype(
-                    BF16
+    user_grad_t = jnp.zeros((own_ref.shape[2], sessions), F32)
+    for block, (chip, side) in enumerate(blocks):
+        for step in range(BLOCK // 16):
+            pieces = []
+            for inner in range(2):
+                row = step * 16 + inner * 8
+                piece = scores_ref[block, row : row + 8, :] * gain
+                pieces.append(
+                    piece + jnp.where(behind == block * BLOCK + row, extra, 0.0)
                 )
-            grad = grad_ref[...]
-            slab = slabs[side][chip]
-            user_grad_t = user_grad_t + dot(slab.T, grad)
-            outs[side][chip, :BLOCK, :] = dot(grad, users_t_ref[...], NT).astype(BF16)
-        return user_grad_t
-
-    embed = own_ref.shape[2]
-    user_grad_t = lax.fori_loop(
-        0, CHIPS, backward, jnp.zeros((embed, sessions), F32), unroll=4
-    ).astype(BF16)
+            grad_ref[block, step * 16 : step * 16 + 16, :] = jnp.concatenate(
+                pieces, axis=0
+            ).astype(BF16)
+        grad = grad_ref[block]
+        slab = slabs[side][chip]
+        user_grad_t = user_grad_t + dot(slab.T, grad)
+        outs[side][chip, :BLOCK, :] = dot(grad, users_t_ref[...], NT).astype(outs[side].dtype)
+    user_grad_t = user_grad_t.astype(BF16)
 
     hidden_t = hidden_t_ref[...]
     grad_embed_ref[...] = dot(hidden_t, user_grad_t, NT)
@@ -234,17 +215,51 @@
                 at = BLOCK + quarter * 16
                 outs[side][chip, at : at + 16, :] = grad_hidden_ref[
                     rows, quarter * 128 : quarter * 128 + 128
-                ].astype(BF16)
+                ].astype(outs[side].dtype)
             rows = pl.ds(pl.multiple_of(index * 32, 32), 32)
-            outs[side][chip, BLOCK + 64 :, :] = grad_embed_ref[rows, :].astype(BF16)
+            outs[side][chip, BLOCK + 64 :, :] = grad_embed_ref[rows, :].astype(outs[side].dtype)
+
+
+def cut_kernel(parts_ref, out_ref):
+    def total(first):
+        rows = slice(first, first + 16)
+        return sum(parts_ref[chip, rows, :].astype(F32) for chip in range(parts_ref.shape[0]))
+
+    towers = []
+    for first in range(BLOCK, PACK, 16):
+        both = total(first)
+        towers += [both[:8], both[8:]]
+    for first in range(0, BLOCK, 16):
+        both = total(first)
+        for inner in range(2):
+            piece = first // 8 + inner
+            tower = towers[piece] if piece < TOWER_PIECES else jnp.zeros_like(both[:8])
+            out_ref[piece] = jnp.concatenate(
+                [both[inner * 8 : inner * 8 + 8], tower], axis=0
+            ).astype(BF16)
+
+
+def piece_kernel(parts_ref, out_ref):
+    total = sum(parts_ref[part].astype(F32) for part in range(parts_ref.shape[0])).astype(BF16)
+    for copy in range(out_ref.shape[0]):
+        out_ref[copy] = total
+
+
+def tower_copies_kernel(pieces_ref, out_ref):
+    rows = jnp.concatenate(
+        [pieces_ref[piece].astype(F32)[8:] for piece in range(TOWER_PIECES)], axis=0
+    ).astype(BF16)
+    for copy in range(out_ref.shape[0]):
+        out_ref[copy] = rows
 
 
 def adam_kernel(
-    rows_ref, grad_ref, first_ref, second_ref, new_first_ref, new_second_ref, direction_ref
+    rows_ref, pieces_ref, first_ref, second_ref, new_first_ref, new_second_ref, direction_ref
 ):
     shape = (first_ref.shape[0], BLOCK)
     onehot = lax.broadcasted_iota(jnp.int32, shape, 0) == rows_ref[...]
-    table_grad = dot(onehot.astype(F32).astype(BF16), grad_ref[...])
+    grad = jnp.concatenate([pieces_ref[piece].astype(F32)[:8] for piece in range(DP)], axis=0)
+    table_grad = dot(onehot.astype(F32).astype(BF16), grad.astype(BF16))
     new_first = BETA_ONE * first_ref[...] + (1.0 - BETA_ONE) * table_grad
     new_second = BETA_TWO * second_ref[...] + (1.0 - BETA_TWO) * table_grad * table_grad
     new_first_ref[...] = new_first
@@ -263,8 +278,15 @@
         grad_embed_ref[item * 32 : item * 32 + 32, :] = tower_ref[item, 64:, :].astype(F32)
 
 
-def spread(array, copies):
-    return jnp.broadcast_to(array[None], (copies, *array.shape))
+def in_vmem(kernel, array, shape):
+    vmem = pl.BlockSpec(memory_space=pltpu.VMEM)
+    return pl.pallas_call(
+        kernel,
+        in_specs=[vmem],
+        out_specs=vmem,
+        out_shape=jax.ShapeDtypeStruct(shape, BF16),
+        compiler_params=PARAMS,
+    )(array)
 
 
 def swap(array, axes):
@@ -300,7 +322,7 @@
         in_specs=[pl.BlockSpec(memory_space=pltpu.SMEM)] + [vmem] * 12,
         out_specs=[vmem] * 3,
         out_shape=[
-            jax.ShapeDtypeStruct((CHIPS, PACK, embed), BF16),
+            jax.ShapeDtypeStruct((CHIPS, PACK, embed), F32),
             jax.ShapeDtypeStruct((CHIPS, PACK, embed), BF16),
             jax.ShapeDtypeStruct((1, sessions), F32),
         ],
@@ -308,7 +330,7 @@
             pltpu.VMEM((CHIPS * CORES, BLOCK, sessions), F32),
             pltpu.VMEM((CHIPS * CORES * 2, sessions, 128), F32),
             pltpu.VMEM((sessions, 128), F32),
-            pltpu.VMEM((BLOCK, sessions), BF16),
+            pltpu.VMEM((CHIPS * CORES, BLOCK, sessions), BF16),
             pltpu.VMEM((features, hidden), F32),
             pltpu.VMEM((hidden, embed), F32),
         ],
@@ -360,12 +382,12 @@
     )
 
     got = lax.ppermute(send, "c", pair)
-    part = (keep.astype(F32) + got.astype(F32)).astype(BF16)
-    part = jnp.sum(swap(part, ("x", "l")).astype(F32), axis=0)
-    part = jnp.pad(part, ((0, PIECE * DP - PACK), (0, 0))).reshape(DP, PIECE, embed)
-    part = jnp.sum(swap(part, ("h", "z")), axis=0).astype(BF16)
-    whole = swap(spread(part, DP), ("h", "z")).reshape(DP * PIECE, embed)
-    tower = swap(spread(whole[BLOCK:PACK], CHIPS * CORES), ITEM)
+    part = (keep + got.astype(F32)).astype(BF16)
+    pieces = in_vmem(cut_kernel, swap(part, ("x", "l")), (DP, PIECE, embed))
+    pieces = in_vmem(piece_kernel, swap(pieces, ("h", "z")), (DP, PIECE, embed))
+    pieces = swap(pieces, ("h", "z"))
+    tower = in_vmem(tower_copies_kernel, pieces, (CHIPS * CORES, PACK - BLOCK, embed))
+    tower = swap(tower, ITEM)
 
     moment = jax.ShapeDtypeStruct(first_moment.shape, F32)
     new_first, new_second, direction = pl.pallas_call(
@@ -374,7 +396,7 @@
         out_specs=[vmem] * 3,
         out_shape=[moment, moment, moment],
         compiler_params=PARAMS,
-    )(rows, whole[:BLOCK], first_moment, second_moment)
+    )(rows, pieces, first_moment, second_moment)
     grad_hidden, grad_embed = pl.pallas_call(
         unpack_kernel,
         in_specs=[vmem],

time: 112 us -> 108 us (0.964)
  blocking collectives: 70.6 us -> 66.6 us
  starting transfers between devices: 14.7 us -> 16.5 us
    all_to_all x4, blocking collectives: 70.6 us -> 66.6 us  [swap(): return lax.all_to_all(array, axes, 0, 0, tiled=True)]
    all_to_all x1, starting transfers between devices: 5.65 us -> 7.54 us  [swap(): return lax.all_to_all(array, axes, 0, 0, tiled=True)]
    pallas_call x1, Pallas kernels: 9.2 us -> 7.71 us  [main_call(): pl.pallas_call(main_kernel, in_specs=[pl.BlockSpec(memory_space=pltpu.SME...]
where the time goes in v3:
time: 108 us
  blocking collectives  66.6 us (62%)
  starting transfers between devices  16.5 us (15%)
  Pallas kernels  12.5 us (12%)
  waiting for transfers between devices  9.16 us (8%)
  local copies, waits for them, and re-layouts  1.8 us (2%)
    all_to_all x4, blocking collectives, swap(): return lax.all_to_all(array, axes, 0, 0, tiled=True)  66.6 us
    pallas_call x1, Pallas kernels, main_call(): pl.pallas_call(main_kernel, in_specs=[pl.BlockSpec(memory_space=pltpu.SME...  7.71 us
    all_to_all x1, starting transfers between devices, swap(): return lax.all_to_all(array, axes, 0, 0, tiled=True)  7.54 us
    all_to_all x1, waiting for transfers between devices, swap(): return lax.all_to_all(array, axes, 0, 0, tiled=True)  6.8 us
    ppermute x1, starting transfers between devices, shards(): other = lax.ppermute(own, 'c', pair)  6.68 us
    ppermute x1, starting transfers between devices, shards(): got = lax.ppermute(send, 'c', pair)  2.28 us
  transfers between devices with their start and end apart: 3, of which 3 were waited for; matrix products, arithmetic and copies ran while one was open for 0% of the time, Pallas kernels for 2%

profile of v3, /device:TPU:1, one launch (start us, length us, event | category | flops | bytes accessed | tf_op | source)
XLA Modules:
  0.0 107.5 jit_solution(6096956806292112776)
XLA Ops:
  0.6 0.0 copy-start.1
  0.6 0.0 copy-start
  0.7 0.0 copy-start.2
  0.7 1.1 %copy-done.2 = f32[1024,128]{1,0:T(8,128)S(1)} copy-done((f32[1024,128]{1,0:T(8,128)S(1)}, f32[1024,128]{1,0:T(8,128)}, u32[]{:S(2)}) %copy-start.2) | copy-done | bytes 524312
  1.7 0.0 copy-start.9
  1.7 0.7 copy-done.9
  2.4 0.0 copy-start.5
  2.4 0.0 copy-start.6
  2.4 0.0 copy-start.8
  2.4 0.0 copy-start.7
  2.4 0.0 copy-start.11
  2.4 0.0 copy-start.12
  2.5 0.4 shard_map.164
  2.8 13.2 %all_to_all.25.own_ref = bf16[8,256,128]{2,1,0:T(8,128)(2,1)S(1)} all-to-all(bf16[8,256,128]{2,1,0:T(8,128)(2,1)S(1)} %shard_map.164), channel_id=1, replica_groups=mesh['h'=4,'z'=8,'x'=4,'l'=2,'c'=2] {'x','l'}, dimensions={0} | all-to-all | bytes 1048576 | tf_op jit(solution)/shard_map/all_to_all | solution.py:293
  16.0 6.7 %collective-permute-start = (bf16[8,256,128]{2,1,0:T(8,128)(2,1)S(1)}, bf16[8,256,128]{2,1,0:T(8,128)(2,1)S(1)}, u32[]{:S(2)}, u32[]{:S(2)}) collective-permute-start(bf16[8,256,128]{2,1,0:T(8,128)(2,1)S(1)} %all_to_all.25.own_ref), channel_id=1, source_target_pairs={{0,1},{1,0},{2,3},{3,2},{4,5},{5,4},{6,7},{7,6},{8,9},{9,8},{10,11... | collective-permute-start | bytes 1572872 | tf_op jit(solution)/shard_map/ppermute | solution.py:371
  22.7 0.0 copy-done.1
  22.7 0.0 copy-done
  22.7 0.0 copy-done.5
  22.7 0.0 copy-done.6
  22.8 0.0 copy-done.8
  22.8 0.9 shard_map.163
  23.7 0.6 collective-permute-done.other_ref
  24.2 0.0 copy-done.7
  24.2 0.0 copy-done.11
  24.2 0.0 copy-done.12
  24.2 7.7 %shard_map.165 = (f32[8,352,128]{2,1,0:T(8,128)S(1)}, bf16[8,352,128]{2,1,0:T(8,128)(2,1)S(1)}, f32[1,512]{1,0:T(1,128)}) custom-call(s32[1]{0:T(128)} %bitcast.1.core_ref, bf16[512,256]{1,0:T(8,128)(2,1)S(1)} %copy-done, bf16[512,512]{1,0:T(8,128)(2,1)S(1)} %get-tuple-element.19.hidden_t_ref, bf16[128,512]{1,0:T(8,128)(2,1)S(1)} %get-tuple-element.20.users_t_ref, ...), custom_call_target="tpu_custom_call" | custom-call | tf_op jit(solution)/shard_map/pallas_call | solution.py:320
  31.9 2.3 %collective-permute-start.1 = (bf16[8,352,128]{2,1,0:T(8,128)(2,1)S(1)}, bf16[8,352,128]{2,1,0:T(8,128)(2,1)S(1)}, u32[]{:S(2)}, u32[]{:S(2)}) collective-permute-start(bf16[8,352,128]{2,1,0:T(8,128)(2,1)S(1)} %get-tuple-element.25), channel_id=1, source_target_pairs={{0,1},{1,0},{2,3},{3,2},{4,5},{5,4},{6,7},{7,6},{8,9},{9,8},{10,11... | collective-permute-start | bytes 2162696 | tf_op jit(solution)/shard_map/ppermute | solution.py:384
  34.2 1.8 %collective-permute-done.1 = bf16[8,352,128]{2,1,0:T(8,128)(2,1)S(1)} collective-permute-done((bf16[8,352,128]{2,1,0:T(8,128)(2,1)S(1)}, bf16[8,352,128]{2,1,0:T(8,128)(2,1)S(1)}, u32[]{:S(2)}, u32[]{:S(2)}) %collective-permute-start.1) | collective-permute-done | bytes 720928 | tf_op jit(solution)/shard_map/ppermute | solution.py:384
  36.0 0.2 add_convert_fusion
  36.2 14.0 %all_to_all.26.parts_ref = bf16[8,352,128]{2,1,0:T(8,128)(2,1)S(1)} all-to-all(bf16[8,352,128]{2,1,0:T(8,128)(2,1)S(1)} %add_convert_fusion), channel_id=1, replica_groups=mesh['h'=4,'z'=8,'x'=4,'l'=2,'c'=2] {'x','l'}, dimensions={0} | all-to-all | bytes 1441792 | tf_op jit(solution)/shard_map/all_to_all | solution.py:293
  50.2 0.0 copy-start.3
  50.2 0.0 copy-start.4
  50.2 0.0 copy-start.10
  50.2 0.1 shard_map.166
  50.3 25.0 %all_to_all.27.parts_ref = bf16[32,16,128]{2,1,0:T(8,128)(2,1)S(1)} all-to-all(bf16[32,16,128]{2,1,0:T(8,128)(2,1)S(1)} %shard_map.166), channel_id=1, replica_groups=mesh['h'=4,'z'=8,'x'=4,'l'=2,'c'=2] {'h','z'}, dimensions={0} | all-to-all | bytes 262144 | tf_op jit(solution)/shard_map/all_to_all | solution.py:293
  75.4 14.4 %all_to_all.28.pieces_ref = bf16[32,16,128]{2,1,0:T(8,128)(2,1)S(1)} all-to-all(bf16[32,16,128]{2,1,0:T(8,128)(2,1)S(1)} %shard_map.167), channel_id=1, replica_groups=mesh['h'=4,'z'=8,'x'=4,'l'=2,'c'=2] {'h','z'}, dimensions={0} | all-to-all | bytes 262144 | tf_op jit(solution)/shard_map/all_to_all | solution.py:293
  89.8 0.8 shard_map.169
  90.6 7.5 %all-to-all-start.4 = ((bf16[16,96,128]{2,1,0:T(8,128)(2,1)}), bf16[16,96,128]{2,1,0:T(8,128)(2,1)S(1)}, u32[]{:S(2)}, u32[]{:S(2)}) async-start(bf16[16,96,128]{2,1,0:T(8,128)(2,1)} %shard_map.169), calls=%async_computation.4 | async-start | bytes 786432 | tf_op jit(solution)/shard_map/all_to_all | solution.py:293
  98.1 0.0 copy-done.3
  98.1 0.0 copy-done.4
  98.1 0.0 copy-done.10
  98.1 1.6 %shard_map.168 = (f32[1024,128]{1,0:T(8,128)}, f32[1024,128]{1,0:T(8,128)}, f32[1024,128]{1,0:T(8,128)}) custom-call(s32[1,256]{1,0:T(1,128)S(1)} %bitcast.10, bf16[32,16,128]{2,1,0:T(8,128)(2,1)S(1)} %all_to_all.28.pieces_ref, f32[1024,128]{1,0:T(8,128)S(1)} %copy-done.3, f32[1024,128]{1,0:T(8,128)S(1)} %copy-done.4), custom_call_target="tpu_custom_call" | custom-call | tf_op jit(solution)/shard_map/pallas_call | solution.py:393
  99.8 6.8 %all-to-all-done.4.tower_ref = bf16[16,96,128]{2,1,0:T(8,128)(2,1)S(1)} async-done(((bf16[16,96,128]{2,1,0:T(8,128)(2,1)}), bf16[16,96,128]{2,1,0:T(8,128)(2,1)S(1)}, u32[]{:S(2)}, u32[]{:S(2)}) %all-to-all-start.4) | async-done | bytes 393248 | tf_op jit(solution)/shard_map/all_to_all | solution.py:293
  106.6 0.9 shard_map.170
  (1 shorter events, 0.0 us)
Async XLA Ops:
  0.6 22.1 %copy-start.1 = (bf16[512,128]{1,0:T(8,128)(2,1)S(1)}, bf16[512,128]{1,0:T(8,128)(2,1)}, u32[]{:S(2)}) copy-start(bf16[512,128]{1,0:T(8,128)(2,1)} %w_embed_ref.3) | copy-start | bytes 393220
  0.6 22.1 %copy-start = (bf16[512,256]{1,0:T(8,128)(2,1)S(1)}, bf16[512,256]{1,0:T(8,128)(2,1)}, u32[]{:S(2)}) copy-start(bf16[512,256]{1,0:T(8,128)(2,1)} %states_ref.3) | copy-start | bytes 786436
  0.7 1.1 %copy-start.2 = (f32[1024,128]{1,0:T(8,128)S(1)}, f32[1024,128]{1,0:T(8,128)}, u32[]{:S(2)}) copy-start(f32[1024,128]{1,0:T(8,128)} %table_ref.1) | copy-start | bytes 1572868
  1.7 0.7 copy-start.9
  2.4 20.3 %copy-start.5 = (bf16[512,256]{1,0:T(8,128)(2,1)S(1)}, bf16[512,256]{1,0:T(8,128)(2,1)}, u32[]{:S(2)}) copy-start(bf16[512,256]{1,0:T(8,128)(2,1)} %next_ref.1) | copy-start | bytes 786436
  2.4 20.3 %copy-start.6 = (bf16[256,512]{1,0:T(8,128)(2,1)S(1)}, bf16[256,512]{1,0:T(8,128)(2,1)}, u32[]{:S(2)}) copy-start(bf16[256,512]{1,0:T(8,128)(2,1)} %w_hidden_ref.1) | copy-start | bytes 786436
  2.4 20.3 %copy-start.8 = (s32[512,10]{0,1:T(8,128)S(1)}, s32[512,10]{0,1:T(8,128)}, u32[]{:S(2)}) copy-start(s32[512,10]{0,1:T(8,128)} %param.17) | copy-start | bytes 61444
  2.4 21.8 %copy-start.7 = (s32[512,10]{0,1:T(8,128)S(1)}, s32[512,10]{0,1:T(8,128)}, u32[]{:S(2)}) copy-start(s32[512,10]{0,1:T(8,128)} %param.15) | copy-start | bytes 61444
  2.4 21.8 %copy-start.11 = (f32[512]{0:T(512)S(1)}, f32[512]{0:T(512)}, u32[]{:S(2)}) copy-start(f32[512]{0:T(512)} %param.14) | copy-start | bytes 6148
  2.4 21.8 %copy-start.12 = (s32[512]{0:T(512)S(1)}, s32[512]{0:T(512)}, u32[]{:S(2)}) copy-start(s32[512]{0:T(512)} %param.16) | copy-start | bytes 6148
  16.0 8.2 %collective-permute-start = (bf16[8,256,128]{2,1,0:T(8,128)(2,1)S(1)}, bf16[8,256,128]{2,1,0:T(8,128)(2,1)S(1)}, u32[]{:S(2)}, u32[]{:S(2)}) collective-permute-start(bf16[8,256,128]{2,1,0:T(8,128)(2,1)S(1)} %all_to_all.25.own_ref), channel_id=1, source_target_pairs={{0,1},{1,0},{2,3},{3,2},{4,5},{5,4},{6,7},{7,6},{8,9},{9,8},{10,11... | collective-permute-start | bytes 1572872 | tf_op jit(solution)/shard_map/ppermute | solution.py:371
  31.9 4.1 %collective-permute-start.1 = (bf16[8,352,128]{2,1,0:T(8,128)(2,1)S(1)}, bf16[8,352,128]{2,1,0:T(8,128)(2,1)S(1)}, u32[]{:S(2)}, u32[]{:S(2)}) collective-permute-start(bf16[8,352,128]{2,1,0:T(8,128)(2,1)S(1)} %get-tuple-element.25), channel_id=1, source_target_pairs={{0,1},{1,0},{2,3},{3,2},{4,5},{5,4},{6,7},{7,6},{8,9},{9,8},{10,11... | collective-permute-start | bytes 2162696 | tf_op jit(solution)/shard_map/ppermute | solution.py:384
  50.2 47.9 %copy-start.3 = (f32[1024,128]{1,0:T(8,128)S(1)}, f32[1024,128]{1,0:T(8,128)}, u32[]{:S(2)}) copy-start(f32[1024,128]{1,0:T(8,128)} %first_ref.1) | copy-start | bytes 1572868
  50.2 47.9 %copy-start.4 = (f32[1024,128]{1,0:T(8,128)S(1)}, f32[1024,128]{1,0:T(8,128)}, u32[]{:S(2)}) copy-start(f32[1024,128]{1,0:T(8,128)} %second_ref.1) | copy-start | bytes 1572868
  50.2 47.9 %copy-start.10 = (s32[256]{0:T(256)S(1)}, s32[256]{0:T(256)}, u32[]{:S(2)}) copy-start(s32[256]{0:T(256)} %param.21) | copy-start | bytes 3076
  90.6 16.0 %all-to-all-start.4 = ((bf16[16,96,128]{2,1,0:T(8,128)(2,1)}), bf16[16,96,128]{2,1,0:T(8,128)(2,1)S(1)}, u32[]{:S(2)}, u32[]{:S(2)}) async-start(bf16[16,96,128]{2,1,0:T(8,128)(2,1)} %shard_map.169), calls=%async_computation.4 | async-start | bytes 786432 | tf_op jit(solution)/shard_map/all_to_all | solution.py:293

commit v4 on v3

--- a/solution.py
+++ b/solution.py
@@ -16,13 +16,14 @@
 AXES = ("h", "z", "x", "l", "c")
 SIZES = (4, 8, 4, 2, 2)
 ITEM = ("x", "l", "c")
+Y = ("h", "l")
+XZ = ("z", "x")
 CHIPS = 8
 CORES = 2
 BLOCK = 256
-PACK = 352
-DP = 32
-PIECE = 16
-TOWER_PIECES = (PACK - BLOCK) // 8
+PLANE = 32
+EIGHTH = BLOCK // 8
+TOWER = 32
 SLATE = 10
 F32 = jnp.float32
 BF16 = jnp.bfloat16
@@ -199,7 +200,12 @@
         grad = grad_ref[block]
         slab = slabs[side][chip]
         user_grad_t = user_grad_t + dot(slab.T, grad)
-        outs[side][chip, :BLOCK, :] = dot(grad, users_t_ref[...], NT).astype(outs[side].dtype)
+        slab_grad = dot(grad, users_t_ref[...], NT).astype(outs[side].dtype)
+        at = chip % 2 * EIGHTH
+        for z in range(8):
+            outs[side][z * 4 + chip // 2, at : at + EIGHTH, :] = slab_grad[
+                z * EIGHTH : z * EIGHTH + EIGHTH
+            ]
     user_grad_t = user_grad_t.astype(BF16)
 
     hidden_t = hidden_t_ref[...]
@@ -207,59 +213,41 @@
     back = dot(w_embed, user_grad_t)
     pre_grad_t = jnp.where(hidden_t.astype(F32) > 0, back, 0.0).astype(BF16)
     grad_hidden_ref[...] = dot(states_ref[...].T, pre_grad_t, NT)
-    for chip in range(CHIPS):
-        for side in range(CORES):
-            index = chip * CORES + jnp.bitwise_xor(core, side)
-            rows = pl.ds(pl.multiple_of(index * 16, 16), 16)
-            for quarter in range(4):
-                at = BLOCK + quarter * 16
-                outs[side][chip, at : at + 16, :] = grad_hidden_ref[
-                    rows, quarter * 128 : quarter * 128 + 128
-                ].astype(outs[side].dtype)
-            rows = pl.ds(pl.multiple_of(index * 32, 32), 32)
-            outs[side][chip, BLOCK + 64 :, :] = grad_embed_ref[rows, :].astype(outs[side].dtype)
-
-
-def cut_kernel(parts_ref, out_ref):
-    def total(first):
-        rows = slice(first, first + 16)
-        return sum(parts_ref[chip, rows, :].astype(F32) for chip in range(parts_ref.shape[0]))
-
-    towers = []
-    for first in range(BLOCK, PACK, 16):
-        both = total(first)
-        towers += [both[:8], both[8:]]
-    for first in range(0, BLOCK, 16):
-        both = total(first)
-        for inner in range(2):
-            piece = first // 8 + inner
-            tower = towers[piece] if piece < TOWER_PIECES else jnp.zeros_like(both[:8])
-            out_ref[piece] = jnp.concatenate(
-                [both[inner * 8 : inner * 8 + 8], tower], axis=0
-            ).astype(BF16)
-
-
-def piece_kernel(parts_ref, out_ref):
+    for side in range(CORES):
+        half = jnp.bitwise_xor(core, side)
+        for piece in range(PLANE):
+            quarter, part = piece // 8, piece % 8
+            rows = pl.ds(pl.multiple_of(half * 128 + part * 16, 16), 16)
+            outs[side][piece, 2 * EIGHTH : 2 * EIGHTH + 16, :] = grad_hidden_ref[
+                rows, quarter * 128 : quarter * 128 + 128
+            ].astype(outs[side].dtype)
+            rows = pl.ds(pl.multiple_of(half * 256 + piece * 8, 8), 8)
+            outs[side][piece, 2 * EIGHTH + 16 :, :] = jnp.concatenate(
+                [grad_embed_ref[rows, :], jnp.zeros((8, 128), F32)], axis=0
+            ).astype(outs[side].dtype)
+
+
+def plane_kernel(parts_ref, out_ref):
+    total = sum(parts_ref[part].astype(F32) for part in range(parts_ref.shape[0])).astype(BF16)
+    for to in range(out_ref.shape[0]):
+        at = to % 2 * EIGHTH
+        out_ref[to, :EIGHTH, :] = total[at : at + EIGHTH]
+        out_ref[to, EIGHTH:, :] = total[2 * EIGHTH :]
+
+
+def line_kernel(parts_ref, out_ref):
     total = sum(parts_ref[part].astype(F32) for part in range(parts_ref.shape[0])).astype(BF16)
     for copy in range(out_ref.shape[0]):
         out_ref[copy] = total
 
 
-def tower_copies_kernel(pieces_ref, out_ref):
-    rows = jnp.concatenate(
-        [pieces_ref[piece].astype(F32)[8:] for piece in range(TOWER_PIECES)], axis=0
-    ).astype(BF16)
-    for copy in range(out_ref.shape[0]):
-        out_ref[copy] = rows
-
-
 def adam_kernel(
-    rows_ref, pieces_ref, first_ref, second_ref, new_first_ref, new_second_ref, direction_ref
+    x_ref, rows_ref, pieces_ref, first_ref, second_ref, new_first_ref, new_second_ref, direction_ref
 ):
     shape = (first_ref.shape[0], BLOCK)
     onehot = lax.broadcasted_iota(jnp.int32, shape, 0) == rows_ref[...]
-    grad = jnp.concatenate([pieces_ref[piece].astype(F32)[:8] for piece in range(DP)], axis=0)
-    table_grad = dot(onehot.astype(F32).astype(BF16), grad.astype(BF16))
+    grad = jnp.concatenate([pieces_ref[z * 4 + x_ref[0], :EIGHTH, :] for z in range(8)], axis=0)
+    table_grad = dot(onehot.astype(F32).astype(BF16), grad)
     new_first = BETA_ONE * first_ref[...] + (1.0 - BETA_ONE) * table_grad
     new_second = BETA_TWO * second_ref[...] + (1.0 - BETA_TWO) * table_grad * table_grad
     new_first_ref[...] = new_first
@@ -269,13 +257,17 @@
     direction_ref[...] = new_first / correct_one / (jnp.sqrt(new_second / correct_two) + EPSILON)
 
 
-def unpack_kernel(tower_ref, grad_hidden_ref, grad_embed_ref):
-    for item in range(CHIPS * CORES):
-        for quarter in range(4):
-            grad_hidden_ref[item * 16 : item * 16 + 16, quarter * 128 : quarter * 128 + 128] = (
-                tower_ref[item, quarter * 16 : quarter * 16 + 16, :].astype(F32)
-            )
-        grad_embed_ref[item * 32 : item * 32 + 32, :] = tower_ref[item, 64:, :].astype(F32)
+def unpack_kernel(core_ref, own_ref, other_ref, grad_hidden_ref, grad_embed_ref):
+    for side, pieces_ref in enumerate((own_ref, other_ref)):
+        half = jnp.bitwise_xor(core_ref[0], side)
+        for piece in range(PLANE):
+            quarter, part = piece // 8, piece % 8
+            rows = pl.ds(pl.multiple_of(half * 128 + part * 16, 16), 16)
+            grad_hidden_ref[rows, quarter * 128 : quarter * 128 + 128] = pieces_ref[
+                piece, EIGHTH : EIGHTH + 16, :
+            ].astype(F32)
+            rows = pl.ds(pl.multiple_of(half * 256 + piece * 8, 8), 8)
+            grad_embed_ref[rows, :] = pieces_ref[piece, EIGHTH + 16 :, :].astype(F32)[:8]
 
 
 def in_vmem(kernel, array, shape):
@@ -322,8 +314,8 @@
         in_specs=[pl.BlockSpec(memory_space=pltpu.SMEM)] + [vmem] * 12,
         out_specs=[vmem] * 3,
         out_shape=[
-            jax.ShapeDtypeStruct((CHIPS, PACK, embed), F32),
-            jax.ShapeDtypeStruct((CHIPS, PACK, embed), BF16),
+            jax.ShapeDtypeStruct((PLANE, 2 * EIGHTH + TOWER, embed), F32),
+            jax.ShapeDtypeStruct((PLANE, 2 * EIGHTH + TOWER, embed), BF16),
             jax.ShapeDtypeStruct((1, sessions), F32),
         ],
         scratch_shapes=[
@@ -383,30 +375,30 @@
 
     got = lax.ppermute(send, "c", pair)
     part = (keep + got.astype(F32)).astype(BF16)
-    pieces = in_vmem(cut_kernel, swap(part, ("x", "l")), (DP, PIECE, embed))
-    pieces = in_vmem(piece_kernel, swap(pieces, ("h", "z")), (DP, PIECE, embed))
-    pieces = swap(pieces, ("h", "z"))
-    tower = in_vmem(tower_copies_kernel, pieces, (CHIPS * CORES, PACK - BLOCK, embed))
-    tower = swap(tower, ITEM)
+    part = in_vmem(plane_kernel, swap(part, XZ), (8, EIGHTH + TOWER, embed))
+    part = in_vmem(line_kernel, swap(part, Y), (PLANE, EIGHTH + TOWER, embed))
+    pieces = swap(part, XZ)
+    other_pieces = lax.ppermute(pieces, "c", pair)
 
     moment = jax.ShapeDtypeStruct(first_moment.shape, F32)
+    scalar = pl.BlockSpec(memory_space=pltpu.SMEM)
     new_first, new_second, direction = pl.pallas_call(
         adam_kernel,
-        in_specs=[vmem] * 4,
+        in_specs=[scalar] + [vmem] * 4,
         out_specs=[vmem] * 3,
         out_shape=[moment, moment, moment],
         compiler_params=PARAMS,
-    )(rows, pieces, first_moment, second_moment)
+    )(lax.axis_index("x").astype(jnp.int32).reshape(1), rows, pieces, first_moment, second_moment)
     grad_hidden, grad_embed = pl.pallas_call(
         unpack_kernel,
-        in_specs=[vmem],
+        in_specs=[scalar] + [vmem] * 2,
         out_specs=[vmem] * 2,
         out_shape=[
             jax.ShapeDtypeStruct(w_hidden.shape, F32),
             jax.ShapeDtypeStruct(w_embed.shape, F32),
         ],
         compiler_params=PARAMS,
-    )(tower)
+    )(core, pieces, other_pieces)
     return (new_first, new_second, direction, grad_hidden, grad_embed, delta.reshape(sessions))
 
 

time: 108 us -> 110 us (1.019)
  blocking collectives: 66.6 us -> 76.9 us
  waiting for transfers between devices: 9.16 us -> 2.46 us
    all_to_all x4, blocking collectives: 66.6 us -> 76.9 us  [swap(): return lax.all_to_all(array, axes, 0, 0, tiled=True)]
    all_to_all x1 -> x0, starting transfers between devices: 7.54 us -> none  [swap(): return lax.all_to_all(array, axes, 0, 0, tiled=True)]
    ppermute x0 -> x1, starting transfers between devices: none -> 7.43 us  [shards(): other_pieces = lax.ppermute(pieces, 'c', pair)]
    all_to_all x1 -> x0, waiting for transfers between devices: 6.8 us -> none  [swap(): return lax.all_to_all(array, axes, 0, 0, tiled=True)]
  transfers between devices with their start and end apart: 3 -> 3, of which waited for: 3 -> 2; matrix products, arithmetic and copies ran while one was open for 0% -> 0% of each run, Pallas kernels for 2% -> 2%
where the time goes in v4:
time: 110 us
  blocking collectives  76.9 us (70%)
  starting transfers between devices  16.4 us (15%)
  Pallas kernels  11.4 us (10%)
  waiting for transfers between devices  2.46 us (2%)
  local copies, waits for them, and re-layouts  1.8 us (2%)
    all_to_all x4, blocking collectives, swap(): return lax.all_to_all(array, axes, 0, 0, tiled=True)  76.9 us
    ppermute x1, starting transfers between devices, shards(): other_pieces = lax.ppermute(pieces, 'c', pair)  7.43 us
    pallas_call x1, Pallas kernels, main_call(): pl.pallas_call(main_kernel, in_specs=[pl.BlockSpec(memory_space=pltpu.SME...  7.34 us
    ppermute x1, starting transfers between devices, shards(): other = lax.ppermute(own, 'c', pair)  6.68 us
    ppermute x1, starting transfers between devices, shards(): got = lax.ppermute(send, 'c', pair)  2.29 us
  transfers between devices with their start and end apart: 3, of which 2 were waited for; matrix products, arithmetic and copies ran while one was open for 0% of the time, Pallas kernels for 2%

profile of v4, /device:TPU:1, one launch (start us, length us, event | category | flops | bytes accessed | tf_op | source)
XLA Modules:
  0.0 109.9 jit_solution(898852664286196187)
XLA Ops:
  0.6 0.0 copy-start.3
  0.6 0.0 copy-start
  0.7 0.0 copy-start.4
  0.7 1.1 copy-done.4
  1.7 0.0 copy-start.9
  1.7 0.7 copy-done.9
  2.4 0.0 copy-start.5
  2.4 0.0 copy-start.6
  2.4 0.0 copy-start.8
  2.4 0.0 copy-start.7
  2.4 0.0 copy-start.11
  2.4 0.0 copy-start.12
  2.5 0.4 shard_map.164
  2.8 13.2 %all_to_all.20.own_ref = bf16[8,256,128]{2,1,0:T(8,128)(2,1)S(1)} all-to-all(bf16[8,256,128]{2,1,0:T(8,128)(2,1)S(1)} %shard_map.164), channel_id=1, replica_groups=mesh['h'=4,'z'=8,'x'=4,'l'=2,'c'=2] {'x','l'}, dimensions={0} | all-to-all | bytes 1048576 | tf_op jit(solution)/shard_map/all_to_all | solution.py:285
  16.0 6.7 %collective-permute-start = (bf16[8,256,128]{2,1,0:T(8,128)(2,1)S(1)}, bf16[8,256,128]{2,1,0:T(8,128)(2,1)S(1)}, u32[]{:S(2)}, u32[]{:S(2)}) collective-permute-start(bf16[8,256,128]{2,1,0:T(8,128)(2,1)S(1)} %all_to_all.20.own_ref), channel_id=1, source_target_pairs={{0,1},{1,0},{2,3},{3,2},{4,5},{5,4},{6,7},{7,6},{8,9},{9,8},{10,11... | collective-permute-start | bytes 1572872 | tf_op jit(solution)/shard_map/ppermute | solution.py:363
  22.7 0.0 copy-done.3
  22.7 0.0 copy-done
  22.7 0.0 copy-done.5
  22.7 0.0 copy-done.6
  22.8 0.0 copy-done.8
  22.8 0.9 shard_map.163
  23.7 0.6 collective-permute-done.other_ref
  24.2 0.0 copy-done.7
  24.2 0.0 copy-done.11
  24.2 0.0 copy-done.12
  24.2 7.3 %shard_map.165 = (f32[32,96,128]{2,1,0:T(8,128)S(1)}, bf16[32,96,128]{2,1,0:T(8,128)(2,1)S(1)}, f32[1,512]{1,0:T(1,128)}) custom-call(s32[1]{0:T(128)} %bitcast.2.core_ref, bf16[512,256]{1,0:T(8,128)(2,1)S(1)} %copy-done, bf16[512,512]{1,0:T(8,128)(2,1)S(1)} %get-tuple-element.19.hidden_t_ref, bf16[128,512]{1,0:T(8,128)(2,1)S(1)} %get-tuple-element.20.users_t_ref, ...), custom_call_target="tpu_custom_call" | custom-call | tf_op jit(solution)/shard_map/pallas_call | solution.py:312
  31.6 2.3 %collective-permute-start.1 = (bf16[32,96,128]{2,1,0:T(8,128)(2,1)S(1)}, bf16[32,96,128]{2,1,0:T(8,128)(2,1)S(1)}, u32[]{:S(2)}, u32[]{:S(2)}) collective-permute-start(bf16[32,96,128]{2,1,0:T(8,128)(2,1)S(1)} %get-tuple-element.25), channel_id=1, source_target_pairs={{0,1},{1,0},{2,3},{3,2},{4,5},{5,4},{6,7},{7,6},{8,9},{9,8},{10,11... | collective-permute-start | bytes 2359304 | tf_op jit(solution)/shard_map/ppermute | solution.py:376
  33.9 1.9 %collective-permute-done.1 = bf16[32,96,128]{2,1,0:T(8,128)(2,1)S(1)} collective-permute-done((bf16[32,96,128]{2,1,0:T(8,128)(2,1)S(1)}, bf16[32,96,128]{2,1,0:T(8,128)(2,1)S(1)}, u32[]{:S(2)}, u32[]{:S(2)}) %collective-permute-start.1) | collective-permute-done | bytes 786464 | tf_op jit(solution)/shard_map/ppermute | solution.py:376
  35.8 0.2 add_convert_fusion
  36.0 30.8 %all_to_all.21.parts_ref = bf16[32,96,128]{2,1,0:T(8,128)(2,1)S(1)} all-to-all(bf16[32,96,128]{2,1,0:T(8,128)(2,1)S(1)} %add_convert_fusion), channel_id=1, replica_groups=mesh['h'=4,'z'=8,'x'=4,'l'=2,'c'=2] {'z','x'}, dimensions={0} | all-to-all | bytes 1572864 | tf_op jit(solution)/shard_map/all_to_all | solution.py:285
  66.8 0.0 copy-start.1
  66.8 0.0 copy-start.2
  66.8 0.0 copy-start.10
  66.8 0.1 shard_map.166
  66.9 13.9 %all_to_all.22.parts_ref = bf16[8,64,128]{2,1,0:T(8,128)(2,1)S(1)} all-to-all(bf16[8,64,128]{2,1,0:T(8,128)(2,1)S(1)} %shard_map.166), channel_id=1, replica_groups=mesh['h'=4,'z'=8,'x'=4,'l'=2,'c'=2] {'h','l'}, dimensions={0} | all-to-all | bytes 262144 | tf_op jit(solution)/shard_map/all_to_all | solution.py:285
  80.8 0.1 shard_map.167
  80.9 19.0 %all_to_all.23.pieces_ref.own_ref = bf16[32,64,128]{2,1,0:T(8,128)(2,1)S(1)} all-to-all(bf16[32,64,128]{2,1,0:T(8,128)(2,1)S(1)} %shard_map.167), channel_id=1, replica_groups=mesh['h'=4,'z'=8,'x'=4,'l'=2,'c'=2] {'z','x'}, dimensions={0} | all-to-all | bytes 1048576 | tf_op jit(solution)/shard_map/all_to_all | solution.py:285
  99.9 7.4 %collective-permute-start.2 = (bf16[32,64,128]{2,1,0:T(8,128)(2,1)S(1)}, bf16[32,64,128]{2,1,0:T(8,128)(2,1)S(1)}, u32[]{:S(2)}, u32[]{:S(2)}) collective-permute-start(bf16[32,64,128]{2,1,0:T(8,128)(2,1)S(1)} %all_to_all.23.pieces_ref.own_ref), channel_id=1, source_target_pairs={{0,1},{1,0},{2,3},{3,2},{4,5},{5,4},{6,7},{7,6},{8,9},{9,8},{10,11... | collective-permute-start | bytes 1572872 | tf_op jit(solution)/shard_map/ppermute | solution.py:381
  107.3 0.0 copy-done.1
  107.3 0.0 copy-done.2
  107.3 0.0 copy-done.10
  107.3 1.6 %shard_map.168 = (f32[1024,128]{1,0:T(8,128)}, f32[1024,128]{1,0:T(8,128)}, f32[1024,128]{1,0:T(8,128)}) custom-call(s32[1]{0:T(128)} %bitcast.x_ref, s32[1,256]{1,0:T(1,128)S(1)} %bitcast.11, bf16[32,64,128]{2,1,0:T(8,128)(2,1)S(1)} %all_to_all.23.pieces_ref.own_ref, f32[1024,128]{1,0:T(8,128)S(1)} %copy-done.1, f32[1024,128]{1,0:T(8,128)S(1)} %copy-done.2), custom_call_target="tpu_custom_call" | custom-call | tf_op jit(solution)/shard_map/pallas_call | solution.py:385
  109.0 0.0 collective-permute-done.2.other_ref
  109.0 0.9 shard_map.169
Async XLA Ops:
  0.6 22.1 %copy-start.3 = (bf16[512,128]{1,0:T(8,128)(2,1)S(1)}, bf16[512,128]{1,0:T(8,128)(2,1)}, u32[]{:S(2)}) copy-start(bf16[512,128]{1,0:T(8,128)(2,1)} %w_embed_ref.3) | copy-start | bytes 393220
  0.6 22.1 %copy-start = (bf16[512,256]{1,0:T(8,128)(2,1)S(1)}, bf16[512,256]{1,0:T(8,128)(2,1)}, u32[]{:S(2)}) copy-start(bf16[512,256]{1,0:T(8,128)(2,1)} %states_ref.3) | copy-start | bytes 786436
  0.7 1.1 copy-start.4
  1.7 0.7 copy-start.9
  2.4 20.3 %copy-start.5 = (bf16[512,256]{1,0:T(8,128)(2,1)S(1)}, bf16[512,256]{1,0:T(8,128)(2,1)}, u32[]{:S(2)}) copy-start(bf16[512,256]{1,0:T(8,128)(2,1)} %next_ref.1) | copy-start | bytes 786436
  2.4 20.3 %copy-start.6 = (bf16[256,512]{1,0:T(8,128)(2,1)S(1)}, bf16[256,512]{1,0:T(8,128)(2,1)}, u32[]{:S(2)}) copy-start(bf16[256,512]{1,0:T(8,128)(2,1)} %w_hidden_ref.1) | copy-start | bytes 786436
  2.4 20.3 %copy-start.8 = (s32[512,10]{0,1:T(8,128)S(1)}, s32[512,10]{0,1:T(8,128)}, u32[]{:S(2)}) copy-start(s32[512,10]{0,1:T(8,128)} %param.17) | copy-start | bytes 61444
  2.4 21.8 %copy-start.7 = (s32[512,10]{0,1:T(8,128)S(1)}, s32[512,10]{0,1:T(8,128)}, u32[]{:S(2)}) copy-start(s32[512,10]{0,1:T(8,128)} %param.15) | copy-start | bytes 61444
  2.4 21.8 %copy-start.11 = (f32[512]{0:T(512)S(1)}, f32[512]{0:T(512)}, u32[]{:S(2)}) copy-start(f32[512]{0:T(512)} %param.14) | copy-start | bytes 6148
  2.4 21.8 %copy-start.12 = (s32[512]{0:T(512)S(1)}, s32[512]{0:T(512)}, u32[]{:S(2)}) copy-start(s32[512]{0:T(512)} %param.16) | copy-start | bytes 6148
  16.0 8.2 %collective-permute-start = (bf16[8,256,128]{2,1,0:T(8,128)(2,1)S(1)}, bf16[8,256,128]{2,1,0:T(8,128)(2,1)S(1)}, u32[]{:S(2)}, u32[]{:S(2)}) collective-permute-start(bf16[8,256,128]{2,1,0:T(8,128)(2,1)S(1)} %all_to_all.20.own_ref), channel_id=1, source_target_pairs={{0,1},{1,0},{2,3},{3,2},{4,5},{5,4},{6,7},{7,6},{8,9},{9,8},{10,11... | collective-permute-start | bytes 1572872 | tf_op jit(solution)/shard_map/ppermute | solution.py:363
  31.6 4.2 %collective-permute-start.1 = (bf16[32,96,128]{2,1,0:T(8,128)(2,1)S(1)}, bf16[32,96,128]{2,1,0:T(8,128)(2,1)S(1)}, u32[]{:S(2)}, u32[]{:S(2)}) collective-permute-start(bf16[32,96,128]{2,1,0:T(8,128)(2,1)S(1)} %get-tuple-element.25), channel_id=1, source_target_pairs={{0,1},{1,0},{2,3},{3,2},{4,5},{5,4},{6,7},{7,6},{8,9},{9,8},{10,11... | collective-permute-start | bytes 2359304 | tf_op jit(solution)/shard_map/ppermute | solution.py:376
  66.8 40.5 %copy-start.1 = (f32[1024,128]{1,0:T(8,128)S(1)}, f32[1024,128]{1,0:T(8,128)}, u32[]{:S(2)}) copy-start(f32[1024,128]{1,0:T(8,128)} %first_ref.1) | copy-start | bytes 1572868
  66.8 40.5 %copy-start.2 = (f32[1024,128]{1,0:T(8,128)S(1)}, f32[1024,128]{1,0:T(8,128)}, u32[]{:S(2)}) copy-start(f32[1024,128]{1,0:T(8,128)} %second_ref.1) | copy-start | bytes 1572868
  66.8 40.6 %copy-start.10 = (s32[256]{0:T(256)S(1)}, s32[256]{0:T(256)}, u32[]{:S(2)}) copy-start(s32[256]{0:T(256)} %param.21) | copy-start | bytes 3076
  99.9 9.1 %collective-permute-start.2 = (bf16[32,64,128]{2,1,0:T(8,128)(2,1)S(1)}, bf16[32,64,128]{2,1,0:T(8,128)(2,1)S(1)}, u32[]{:S(2)}, u32[]{:S(2)}) collective-permute-start(bf16[32,64,128]{2,1,0:T(8,128)(2,1)S(1)} %all_to_all.23.pieces_ref.own_ref), channel_id=1, source_target_pairs={{0,1},{1,0},{2,3},{3,2},{4,5},{5,4},{6,7},{7,6},{8,9},{9,8},{10,11... | collective-permute-start | bytes 1572872 | tf_op jit(solution)/shard_map/ppermute | solution.py:381

commit v5 on v3

--- a/solution.py
+++ b/solution.py
@@ -20,9 +20,9 @@
 CORES = 2
 BLOCK = 256
 PACK = 352
-DP = 32
-PIECE = 16
-TOWER_PIECES = (PACK - BLOCK) // 8
+DP = (4, 8)
+SHARE = BLOCK // 8
+PIECE = SHARE + 16
 SLATE = 10
 F32 = jnp.float32
 BF16 = jnp.bfloat16
@@ -35,23 +35,10 @@
     return lax.dot_general(left, right, dims, preferred_element_type=F32)
 
 
-def gather_kernel(rows_ref, table_ref, out_ref):
-    row = rows_ref[...].astype(F32)
-    eye = lax.broadcasted_iota(jnp.int32, (128, 128), 0) == lax.broadcasted_iota(
-        jnp.int32, (128, 128), 1
-    )
-    width = table_ref.shape[0]
-    lane = lax.broadcasted_iota(jnp.int32, (128, width), 1).astype(F32)
-    onehots = []
-    for half in range(BLOCK // 128):
-        part = row[:, half * 128 : half * 128 + 128]
-        column = jnp.sum(jnp.where(eye, part, 0.0), axis=1, keepdims=True)
-        onehots.append((lane == column).astype(F32).astype(BF16))
-    table = table_ref[...].astype(BF16)
-    for half, onehot in enumerate(onehots):
-        slab = dot(onehot, table).astype(BF16)
-        for copy in range(out_ref.shape[0]):
-            out_ref[copy, half * 128 : half * 128 + 128, :] = slab
+def copies_kernel(rows_ref, out_ref):
+    rows = rows_ref[...].astype(BF16)
+    for copy in range(out_ref.shape[0]):
+        out_ref[copy] = rows
 
 
 def tower_kernel(
@@ -221,22 +208,22 @@
 
 
 def cut_kernel(parts_ref, out_ref):
-    def total(first):
-        rows = slice(first, first + 16)
+    def total(first, length):
+        rows = slice(first, first + length)
         return sum(parts_ref[chip, rows, :].astype(F32) for chip in range(parts_ref.shape[0]))
 
-    towers = []
-    for first in range(BLOCK, PACK, 16):
-        both = total(first)
-        towers += [both[:8], both[8:]]
-    for first in range(0, BLOCK, 16):
-        both = total(first)
-        for inner in range(2):
-            piece = first // 8 + inner
-            tower = towers[piece] if piece < TOWER_PIECES else jnp.zeros_like(both[:8])
-            out_ref[piece] = jnp.concatenate(
-                [both[inner * 8 : inner * 8 + 8], tower], axis=0
-            ).astype(BF16)
+    for z in range(DP[1]):
+        if z < 4:
+            tower = total(BLOCK + z * 16, 16)
+        else:
+            both = total(BLOCK + 64 + (z - 4) // 2 * 16, 16)
+            half = both[(z - 4) % 2 * 8 : (z - 4) % 2 * 8 + 8]
+            tower = jnp.concatenate([half, jnp.zeros_like(half)], axis=0)
+        cands = total(z * SHARE, SHARE).astype(BF16)
+        tower = tower.astype(BF16)
+        for h in range(DP[0]):
+            out_ref[h * DP[1] + z, :SHARE, :] = cands
+            out_ref[h * DP[1] + z, SHARE:, :] = tower
 
 
 def piece_kernel(parts_ref, out_ref):
@@ -246,20 +233,37 @@
 
 
 def tower_copies_kernel(pieces_ref, out_ref):
-    rows = jnp.concatenate(
-        [pieces_ref[piece].astype(F32)[8:] for piece in range(TOWER_PIECES)], axis=0
-    ).astype(BF16)
+    parts = [pieces_ref[z, SHARE:, :] for z in range(4)]
+    for z in range(4, 8, 2):
+        halves = [pieces_ref[z + more, SHARE:, :].astype(F32)[:8] for more in range(2)]
+        parts.append(jnp.concatenate(halves, axis=0).astype(BF16))
+    rows = jnp.concatenate(parts, axis=0)
     for copy in range(out_ref.shape[0]):
         out_ref[copy] = rows
 
 
 def adam_kernel(
-    rows_ref, pieces_ref, first_ref, second_ref, new_first_ref, new_second_ref, direction_ref
+    rows_ref,
+    pieces_ref,
+    first_ref,
+    second_ref,
+    tower_ref,
+    new_first_ref,
+    new_second_ref,
+    direction_ref,
+    grad_hidden_ref,
+    grad_embed_ref,
 ):
+    for item in range(CHIPS * CORES):
+        for quarter in range(4):
+            grad_hidden_ref[item * 16 : item * 16 + 16, quarter * 128 : quarter * 128 + 128] = (
+                tower_ref[item, quarter * 16 : quarter * 16 + 16, :].astype(F32)
+            )
+        grad_embed_ref[item * 32 : item * 32 + 32, :] = tower_ref[item, 64:, :].astype(F32)
     shape = (first_ref.shape[0], BLOCK)
     onehot = lax.broadcasted_iota(jnp.int32, shape, 0) == rows_ref[...]
-    grad = jnp.concatenate([pieces_ref[piece].astype(F32)[:8] for piece in range(DP)], axis=0)
-    table_grad = dot(onehot.astype(F32).astype(BF16), grad.astype(BF16))
+    grad = jnp.concatenate([pieces_ref[z, :SHARE, :] for z in range(DP[1])], axis=0)
+    table_grad = dot(onehot.astype(F32).astype(BF16), grad)
     new_first = BETA_ONE * first_ref[...] + (1.0 - BETA_ONE) * table_grad
     new_second = BETA_TWO * second_ref[...] + (1.0 - BETA_TWO) * table_grad * table_grad
     new_first_ref[...] = new_first
@@ -267,15 +271,6 @@
     correct_one = 1.0 - BETA_ONE**ADAM_STEP
     correct_two = 1.0 - BETA_TWO**ADAM_STEP
     direction_ref[...] = new_first / correct_one / (jnp.sqrt(new_second / correct_two) + EPSILON)
-
-
-def unpack_kernel(tower_ref, grad_hidden_ref, grad_embed_ref):
-    for item in range(CHIPS * CORES):
-        for quarter in range(4):
-            grad_hidden_ref[item * 16 : item * 16 + 16, quarter * 128 : quarter * 128 + 128] = (
-                tower_ref[item, quarter * 16 : quarter * 16 + 16, :].astype(F32)
-            )
-        grad_embed_ref[item * 32 : item * 32 + 32, :] = tower_ref[item, 64:, :].astype(F32)
 
 
 def in_vmem(kernel, array, shape):
@@ -358,13 +353,8 @@
     rows = cand_rows.reshape(1, BLOCK)
     pair = [(0, 1), (1, 0)]
 
-    copies = pl.pallas_call(
-        gather_kernel,
-        in_specs=[vmem] * 2,
-        out_specs=vmem,
-        out_shape=jax.ShapeDtypeStruct((CHIPS, BLOCK, embed), BF16),
-        compiler_params=PARAMS,
-    )(rows, table)
+    local_rows = table.at[cand_rows].get(mode="promise_in_bounds", unique_indices=True)
+    copies = in_vmem(copies_kernel, local_rows, (CHIPS, BLOCK, embed))
     core = lax.axis_index("c").astype(jnp.int32).reshape(1)
     towers = tower_call(core, states, next_states, next_slate.T, w_hidden, w_embed)
     own = swap(copies, ("x", "l"))
@@ -383,30 +373,26 @@
 
     got = lax.ppermute(send, "c", pair)
     part = (keep + got.astype(F32)).astype(BF16)
-    pieces = in_vmem(cut_kernel, swap(part, ("x", "l")), (DP, PIECE, embed))
-    pieces = in_vmem(piece_kernel, swap(pieces, ("h", "z")), (DP, PIECE, embed))
-    pieces = swap(pieces, ("h", "z"))
+    share = in_vmem(cut_kernel, swap(part, ("x", "l")), (DP[0] * DP[1], PIECE, embed))
+    share = in_vmem(piece_kernel, swap(share, ("h", "z")), (DP[1], PIECE, embed))
+    pieces = swap(share, "z")
     tower = in_vmem(tower_copies_kernel, pieces, (CHIPS * CORES, PACK - BLOCK, embed))
     tower = swap(tower, ITEM)
 
     moment = jax.ShapeDtypeStruct(first_moment.shape, F32)
-    new_first, new_second, direction = pl.pallas_call(
+    new_first, new_second, direction, grad_hidden, grad_embed = pl.pallas_call(
         adam_kernel,
-        in_specs=[vmem] * 4,
-        out_specs=[vmem] * 3,
-        out_shape=[moment, moment, moment],
-        compiler_params=PARAMS,
-    )(rows, pieces, first_moment, second_moment)
-    grad_hidden, grad_embed = pl.pallas_call(
-        unpack_kernel,
-        in_specs=[vmem],
-        out_specs=[vmem] * 2,
+        in_specs=[vmem] * 5,
+        out_specs=[vmem] * 5,
         out_shape=[
+            moment,
+            moment,
+            moment,
             jax.ShapeDtypeStruct(w_hidden.shape, F32),
             jax.ShapeDtypeStruct(w_embed.shape, F32),
         ],
         compiler_params=PARAMS,
-    )(tower)
+    )(rows, pieces, first_moment, second_moment, tower)
     return (new_first, new_second, direction, grad_hidden, grad_embed, delta.reshape(sessions))
 
 

time: 108 us -> 107 us (level)
  blocking collectives: 66.6 us -> 81.7 us
  starting transfers between devices: 16.5 us -> 8.95 us
  waiting for transfers between devices: 9.16 us -> 2.37 us
  Pallas kernels: 12.5 us -> 10.7 us
    all_to_all x4 -> x5, blocking collectives: 66.6 us -> 81.7 us  [swap(): return lax.all_to_all(array, axes, 0, 0, tiled=True)]
    all_to_all x1 -> x0, starting transfers between devices: 7.54 us -> none  [swap(): return lax.all_to_all(array, axes, 0, 0, tiled=True)]
    all_to_all x1 -> x0, waiting for transfers between devices: 6.8 us -> none  [swap(): return lax.all_to_all(array, axes, 0, 0, tiled=True)]
    unnamed x26 -> x24, local copies, waits for them, and re-layouts: 1.8 us -> 0.36 us
    pallas_call x3 -> x1, Pallas kernels: 2.93 us -> 1.9 us  [shards(): pl.pallas_call(adam_kernel, in_specs=[vmem] * 5, out_specs=[vmem] * 5, ou...]
  transfers between devices with their start and end apart: 3 -> 2, of which waited for: 3 -> 2; matrix products, arithmetic and copies ran while one was open for 0% -> 0% of each run, Pallas kernels for 2% -> 1%
where the time goes in v5:
time: 107 us
  blocking collectives  81.7 us (76%)
  Pallas kernels  10.7 us (10%)
  starting transfers between devices  8.95 us (8%)
  waiting for transfers between devices  2.37 us (2%)
  local copies, waits for them, and re-layouts  1.09 us (1%)
    all_to_all x5, blocking collectives, swap(): return lax.all_to_all(array, axes, 0, 0, tiled=True)  81.7 us
    pallas_call x1, Pallas kernels, main_call(): pl.pallas_call(main_kernel, in_specs=[pl.BlockSpec(memory_space=pltpu.SME...  7.7 us
    ppermute x1, starting transfers between devices, shards(): other = lax.ppermute(own, 'c', pair)  6.68 us
    ppermute x1, starting transfers between devices, shards(): got = lax.ppermute(send, 'c', pair)  2.28 us
  transfers between devices with their start and end apart: 2, of which 2 were waited for; matrix products, arithmetic and copies ran while one was open for 0% of the time, Pallas kernels for 1%

profile of v5, /device:TPU:1, one launch (start us, length us, event | category | flops | bytes accessed | tf_op | source)
XLA Modules:
  0.0 106.6 jit_solution(12344990177009784796)
XLA Ops:
  0.6 0.0 copy-start
  0.6 0.7 compare_select_fusion
  1.4 0.3 copy-done
  1.7 0.0 copy-start.1
  1.7 0.0 copy-start.2
  1.7 0.0 copy-start.5
  1.7 0.0 copy-start.6
  1.7 0.0 copy-start.8
  1.7 0.7 gather_fusion
  2.5 0.0 copy-start.7
  2.5 0.0 copy-start.10
  2.5 0.0 copy-start.11
  2.5 13.2 %all_to_all.25.own_ref = bf16[8,256,128]{2,1,0:T(8,128)(2,1)S(1)} all-to-all(bf16[8,256,128]{2,1,0:T(8,128)(2,1)S(1)} %shard_map.164), channel_id=1, replica_groups=mesh['h'=4,'z'=8,'x'=4,'l'=2,'c'=2] {'x','l'}, dimensions={0} | all-to-all | bytes 1048576 | tf_op jit(solution)/shard_map/all_to_all | solution.py:288
  15.7 6.7 %collective-permute-start = (bf16[8,256,128]{2,1,0:T(8,128)(2,1)S(1)}, bf16[8,256,128]{2,1,0:T(8,128)(2,1)S(1)}, u32[]{:S(2)}, u32[]{:S(2)}) collective-permute-start(bf16[8,256,128]{2,1,0:T(8,128)(2,1)S(1)} %all_to_all.25.own_ref), channel_id=1, source_target_pairs={{0,1},{1,0},{2,3},{3,2},{4,5},{5,4},{6,7},{7,6},{8,9},{9,8},{10,11... | collective-permute-start | bytes 1572872 | tf_op jit(solution)/shard_map/ppermute | solution.py:361
  22.4 0.0 copy-done.1
  22.4 0.0 copy-done.2
  22.4 0.0 copy-done.5
  22.4 0.0 copy-done.6
  22.5 0.0 copy-done.8
  22.5 0.9 shard_map.163
  23.4 0.6 collective-permute-done.other_ref
  23.9 0.0 copy-done.7
  23.9 0.0 copy-done.10
  23.9 0.0 copy-done.11
  23.9 7.7 %shard_map.165 = (f32[8,352,128]{2,1,0:T(8,128)S(1)}, bf16[8,352,128]{2,1,0:T(8,128)(2,1)S(1)}, f32[1,512]{1,0:T(1,128)}) custom-call(s32[1]{0:T(128)} %bitcast.1.core_ref, bf16[512,256]{1,0:T(8,128)(2,1)S(1)} %copy-done.1, bf16[512,512]{1,0:T(8,128)(2,1)S(1)} %get-tuple-element.19.hidden_t_ref, bf16[128,512]{1,0:T(8,128)(2,1)S(1)} %get-tuple-element.20.users_t_ref, ...), custom_call_target="tpu_custom_call" | custom-call | tf_op jit(solution)/shard_map/pallas_call | solution.py:315
  31.6 2.3 %collective-permute-start.1 = (bf16[8,352,128]{2,1,0:T(8,128)(2,1)S(1)}, bf16[8,352,128]{2,1,0:T(8,128)(2,1)S(1)}, u32[]{:S(2)}, u32[]{:S(2)}) collective-permute-start(bf16[8,352,128]{2,1,0:T(8,128)(2,1)S(1)} %get-tuple-element.25), channel_id=1, source_target_pairs={{0,1},{1,0},{2,3},{3,2},{4,5},{5,4},{6,7},{7,6},{8,9},{9,8},{10,11... | collective-permute-start | bytes 2162696 | tf_op jit(solution)/shard_map/ppermute | solution.py:374
  33.9 1.8 %collective-permute-done.1 = bf16[8,352,128]{2,1,0:T(8,128)(2,1)S(1)} collective-permute-done((bf16[8,352,128]{2,1,0:T(8,128)(2,1)S(1)}, bf16[8,352,128]{2,1,0:T(8,128)(2,1)S(1)}, u32[]{:S(2)}, u32[]{:S(2)}) %collective-permute-start.1) | collective-permute-done | bytes 720928 | tf_op jit(solution)/shard_map/ppermute | solution.py:374
  35.7 0.2 add_convert_fusion
  35.9 14.0 %all_to_all.26.parts_ref = bf16[8,352,128]{2,1,0:T(8,128)(2,1)S(1)} all-to-all(bf16[8,352,128]{2,1,0:T(8,128)(2,1)S(1)} %add_convert_fusion), channel_id=1, replica_groups=mesh['h'=4,'z'=8,'x'=4,'l'=2,'c'=2] {'x','l'}, dimensions={0} | all-to-all | bytes 1441792 | tf_op jit(solution)/shard_map/all_to_all | solution.py:288
  49.9 0.1 shard_map.166
  50.0 0.0 copy-start.3
  50.0 0.0 copy-start.4
  50.0 0.0 copy-start.9
  50.0 27.0 %all_to_all.27.parts_ref = bf16[32,48,128]{2,1,0:T(8,128)(2,1)S(1)} all-to-all(bf16[32,48,128]{2,1,0:T(8,128)(2,1)S(1)} %shard_map.166), channel_id=1, replica_groups=mesh['h'=4,'z'=8,'x'=4,'l'=2,'c'=2] {'h','z'}, dimensions={0} | all-to-all | bytes 786432 | tf_op jit(solution)/shard_map/all_to_all | solution.py:288
  77.0 0.1 shard_map.167
  77.1 11.0 %all_to_all.28.pieces_ref = bf16[8,48,128]{2,1,0:T(8,128)(2,1)S(1)} all-to-all(bf16[8,48,128]{2,1,0:T(8,128)(2,1)S(1)} %shard_map.167), channel_id=1, replica_groups=mesh['h'=4,'z'=8,'x'=4,'l'=2,'c'=2] {'z'}, dimensions={0} | all-to-all | bytes 196608 | tf_op jit(solution)/shard_map/all_to_all | solution.py:288
  88.1 0.1 shard_map.168
  88.1 16.6 %all_to_all.29.tower_ref = bf16[16,96,128]{2,1,0:T(8,128)(2,1)S(1)} all-to-all(bf16[16,96,128]{2,1,0:T(8,128)(2,1)S(1)} %shard_map.168), channel_id=1, replica_groups=mesh['h'=4,'z'=8,'x'=4,'l'=2,'c'=2] {'x','l','c'}, dimensions={0} | all-to-all | bytes 786432 | tf_op jit(solution)/shard_map/all_to_all | solution.py:288
  104.7 0.0 copy-done.3
  104.7 0.0 copy-done.4
  104.7 0.0 copy-done.9
  104.7 1.9 %shard_map.169 = (f32[1024,128]{1,0:T(8,128)}, f32[1024,128]{1,0:T(8,128)}, f32[1024,128]{1,0:T(8,128)}, f32[256,512]{1,0:T(8,128)}, f32[512,128]{1,0:T(8,128)}) custom-call(s32[1,256]{1,0:T(1,128)S(1)} %bitcast.9, bf16[8,48,128]{2,1,0:T(8,128)(2,1)S(1)} %all_to_all.28.pieces_ref, f32[1024,128]{1,0:T(8,128)S(1)} %copy-done.3, f32[1024,128]{1,0:T(8,128)S(1)} %copy-done.4, ...), custom_call_target="tpu_custom_call" | custom-call | tf_op jit(solution)/shard_map/pallas_call | solution.py:383
  (2 shorter events, 0.0 us)
Async XLA Ops:
  0.6 1.1 copy-start
  1.7 20.7 %copy-start.1 = (bf16[512,256]{1,0:T(8,128)(2,1)S(1)}, bf16[512,256]{1,0:T(8,128)(2,1)}, u32[]{:S(2)}) copy-start(bf16[512,256]{1,0:T(8,128)(2,1)} %states_ref.3) | copy-start | bytes 786436
  1.7 20.7 %copy-start.2 = (bf16[512,128]{1,0:T(8,128)(2,1)S(1)}, bf16[512,128]{1,0:T(8,128)(2,1)}, u32[]{:S(2)}) copy-start(bf16[512,128]{1,0:T(8,128)(2,1)} %w_embed_ref.3) | copy-start | bytes 393220
  1.7 20.7 %copy-start.5 = (bf16[512,256]{1,0:T(8,128)(2,1)S(1)}, bf16[512,256]{1,0:T(8,128)(2,1)}, u32[]{:S(2)}) copy-start(bf16[512,256]{1,0:T(8,128)(2,1)} %next_ref.1) | copy-start | bytes 786436
  1.7 20.7 %copy-start.6 = (bf16[256,512]{1,0:T(8,128)(2,1)S(1)}, bf16[256,512]{1,0:T(8,128)(2,1)}, u32[]{:S(2)}) copy-start(bf16[256,512]{1,0:T(8,128)(2,1)} %w_hidden_ref.1) | copy-start | bytes 786436
  1.7 20.8 %copy-start.8 = (s32[512,10]{0,1:T(8,128)S(1)}, s32[512,10]{0,1:T(8,128)}, u32[]{:S(2)}) copy-start(s32[512,10]{0,1:T(8,128)} %param.17) | copy-start | bytes 61444
  2.5 21.5 %copy-start.7 = (s32[512,10]{0,1:T(8,128)S(1)}, s32[512,10]{0,1:T(8,128)}, u32[]{:S(2)}) copy-start(s32[512,10]{0,1:T(8,128)} %param.15) | copy-start | bytes 61444
  2.5 21.5 %copy-start.10 = (f32[512]{0:T(512)S(1)}, f32[512]{0:T(512)}, u32[]{:S(2)}) copy-start(f32[512]{0:T(512)} %param.14) | copy-start | bytes 6148
  2.5 21.5 %copy-start.11 = (s32[512]{0:T(512)S(1)}, s32[512]{0:T(512)}, u32[]{:S(2)}) copy-start(s32[512]{0:T(512)} %param.16) | copy-start | bytes 6148
  15.7 8.2 %collective-permute-start = (bf16[8,256,128]{2,1,0:T(8,128)(2,1)S(1)}, bf16[8,256,128]{2,1,0:T(8,128)(2,1)S(1)}, u32[]{:S(2)}, u32[]{:S(2)}) collective-permute-start(bf16[8,256,128]{2,1,0:T(8,128)(2,1)S(1)} %all_to_all.25.own_ref), channel_id=1, source_target_pairs={{0,1},{1,0},{2,3},{3,2},{4,5},{5,4},{6,7},{7,6},{8,9},{9,8},{10,11... | collective-permute-start | bytes 1572872 | tf_op jit(solution)/shard_map/ppermute | solution.py:361
  31.6 4.1 %collective-permute-start.1 = (bf16[8,352,128]{2,1,0:T(8,128)(2,1)S(1)}, bf16[8,352,128]{2,1,0:T(8,128)(2,1)S(1)}, u32[]{:S(2)}, u32[]{:S(2)}) collective-permute-start(bf16[8,352,128]{2,1,0:T(8,128)(2,1)S(1)} %get-tuple-element.25), channel_id=1, source_target_pairs={{0,1},{1,0},{2,3},{3,2},{4,5},{5,4},{6,7},{7,6},{8,9},{9,8},{10,11... | collective-permute-start | bytes 2162696 | tf_op jit(solution)/shard_map/ppermute | solution.py:374
  50.0 54.7 %copy-start.3 = (f32[1024,128]{1,0:T(8,128)S(1)}, f32[1024,128]{1,0:T(8,128)}, u32[]{:S(2)}) copy-start(f32[1024,128]{1,0:T(8,128)} %first_ref.1) | copy-start | bytes 1572868
  50.0 54.7 %copy-start.4 = (f32[1024,128]{1,0:T(8,128)S(1)}, f32[1024,128]{1,0:T(8,128)}, u32[]{:S(2)}) copy-start(f32[1024,128]{1,0:T(8,128)} %second_ref.1) | copy-start | bytes 1572868
  50.0 54.7 %copy-start.9 = (s32[256]{0:T(256)S(1)}, s32[256]{0:T(256)}, u32[]{:S(2)}) copy-start(s32[256]{0:T(256)} %param.21) | copy-start | bytes 3076

commit v6 on v5

--- a/solution.py
+++ b/solution.py
@@ -24,11 +24,12 @@
 SHARE = BLOCK // 8
 PIECE = SHARE + 16
 SLATE = 10
+STEPS = 4
 F32 = jnp.float32
 BF16 = jnp.bfloat16
 NT = (((1,), (1,)), ((), ()))
 NN = (((1,), (0,)), ((), ()))
-PARAMS = pltpu.CompilerParams(vmem_limit_bytes=48 * 1024 * 1024)
+PARAMS = pltpu.CompilerParams(vmem_limit_bytes=40 * 1024 * 1024)
 
 
 def dot(left, right, dims=NN):
@@ -46,6 +47,8 @@
     states_ref,
     next_ref,
     upcoming_ref,
+    slate_ref,
+    chosen_ref,
     w_hidden_ref,
     w_embed_ref,
     hidden_t_ref,
@@ -53,6 +56,7 @@
     next_users_ref,
     low_ref,
     high_ref,
+    clicked_ref,
 ):
     sessions = states_ref.shape[0]
     w_hidden = w_hidden_ref[...]
@@ -63,6 +67,11 @@
     next_hidden = jnp.maximum(dot(next_ref[...], w_hidden), 0.0).astype(BF16)
     next_users_ref[...] = dot(next_hidden, w_embed).astype(BF16)
 
+    slate = jnp.bitwise_xor(slate_ref[...], core_ref[0] * BLOCK)
+    place = lax.broadcasted_iota(jnp.int32, slate.shape, 0)
+    clicked_ref[...] = jnp.sum(
+        jnp.where(place == chosen_ref[...], slate, 0), axis=0, keepdims=True
+    )
     upcoming = jnp.bitwise_xor(upcoming_ref[...], core_ref[0] * BLOCK)
     padded = jnp.concatenate(
         [upcoming, jnp.zeros((128 - SLATE, sessions), jnp.int32)], axis=0
@@ -72,6 +81,87 @@
         turned = padded[:, rows].astype(F32).T.astype(jnp.int32)
         low_ref[rows, :] = jnp.bitwise_and(turned, 127)
         high_ref[rows, :] = lax.shift_right_logical(turned, 7)
+
+
+def score_side(
+    side,
+    slab_ref,
+    users_t_ref,
+    next_users_ref,
+    low_ref,
+    high_ref,
+    behind,
+    highest,
+    picked,
+    before_ref,
+    scores_ref,
+    next_scores_ref,
+    next_q_ref,
+):
+    next_users = next_users_ref[...]
+    for chip in range(CHIPS):
+        next_scores = dot(next_users, slab_ref[chip], NT)
+        next_scores_ref[chip * 2] = next_scores[:, :128]
+        next_scores_ref[chip * 2 + 1] = next_scores[:, 128:]
+    groups = next_users.shape[0] // 8 // CHIPS
+    for chip in range(CHIPS):
+        for group in range(chip * groups, (chip + 1) * groups):
+            rows = slice(group * 8, group * 8 + 8)
+            low = low_ref[rows, :]
+            high = high_ref[rows, :]
+            found = jnp.zeros((8, 128), F32) if before_ref is None else before_ref[rows, :]
+            for chunk in range(2 * CHIPS):
+                piece = jnp.take_along_axis(
+                    next_scores_ref[chunk, rows, :], low, axis=1, mode="promise_in_bounds"
+                )
+                number = (chunk // 2 * CORES + side) * 2 + chunk % 2
+                found = jnp.where(high == number, piece, found)
+            next_q_ref[rows, :] = found
+        scores = dot(slab_ref[chip], users_t_ref[...])
+        scores_ref[chip] = scores
+        first = (chip * CORES + side) * BLOCK
+        for step in range(BLOCK // 8):
+            piece = scores[step * 8 : step * 8 + 8]
+            highest = jnp.maximum(highest, piece)
+            picked = jnp.where(behind == first + step * 8, piece, picked)
+    return highest, picked
+
+
+def behind_of(clicked_ref):
+    sessions = clicked_ref.shape[1]
+    sub = lax.broadcasted_iota(jnp.int32, (8, sessions), 0)
+    return jnp.broadcast_to(clicked_ref[...], (8, sessions)) - sub
+
+
+def own_kernel(
+    users_t_ref,
+    next_users_ref,
+    low_ref,
+    high_ref,
+    clicked_ref,
+    own_ref,
+    scores_ref,
+    highest_ref,
+    picked_ref,
+    next_q_ref,
+    next_scores_ref,
+):
+    shape = highest_ref.shape
+    highest_ref[...], picked_ref[...] = score_side(
+        0,
+        own_ref,
+        users_t_ref,
+        next_users_ref,
+        low_ref,
+        high_ref,
+        behind_of(clicked_ref),
+        jnp.full(shape, -jnp.inf, F32),
+        jnp.zeros(shape, F32),
+        None,
+        scores_ref,
+        next_scores_ref,
+        next_q_ref,
+    )
 
 
 def main_kernel(
@@ -82,11 +172,14 @@
     next_users_ref,
     low_ref,
     high_ref,
+    clicked_ref,
     rewards_ref,
-    slate_ref,
-    chosen_ref,
     own_ref,
     other_ref,
+    own_scores_ref,
+    own_highest_ref,
+    own_picked_ref,
+    own_next_q_ref,
     w_embed_ref,
     keep_ref,
     send_ref,
@@ -103,41 +196,23 @@
     slabs = (own_ref, other_ref)
     outs = (keep_ref, send_ref)
     w_embed = w_embed_ref[...]
-
-    slate = jnp.bitwise_xor(slate_ref[...], core * BLOCK)
-    place = lax.broadcasted_iota(jnp.int32, slate.shape, 0)
-    clicked = jnp.sum(jnp.where(place == chosen_ref[...], slate, 0), axis=0, keepdims=True)
-    sub = lax.broadcasted_iota(jnp.int32, (8, sessions), 0)
-    behind = jnp.broadcast_to(clicked, (8, sessions)) - sub
-
     blocks = [(chip, side) for chip in range(CHIPS) for side in range(CORES)]
-    next_users = next_users_ref[...]
-    for block, (chip, side) in enumerate(blocks):
-        next_scores = dot(next_users, slabs[side][chip], NT)
-        next_scores_ref[block * 2] = next_scores[:, :128]
-        next_scores_ref[block * 2 + 1] = next_scores[:, 128:]
-
-    highest = jnp.full((8, sessions), -jnp.inf, F32)
-    picked = jnp.zeros((8, sessions), F32)
-    groups = sessions // 8 // len(blocks)
-    for block, (chip, side) in enumerate(blocks):
-        for group in range(block * groups, (block + 1) * groups):
-            rows = slice(group * 8, group * 8 + 8)
-            low = low_ref[rows, :]
-            high = high_ref[rows, :]
-            found = jnp.zeros((8, 128), F32)
-            for chunk in range(next_scores_ref.shape[0]):
-                piece = jnp.take_along_axis(
-                    next_scores_ref[chunk, rows, :], low, axis=1, mode="promise_in_bounds"
-                )
-                found = jnp.where(high == chunk, piece, found)
-            next_q_ref[rows, :] = found
-        scores = dot(slabs[side][chip], users_t_ref[...])
-        scores_ref[block] = scores
-        for step in range(BLOCK // 8):
-            piece = scores[step * 8 : step * 8 + 8]
-            highest = jnp.maximum(highest, piece)
-            picked = jnp.where(behind == block * BLOCK + step * 8, piece, picked)
+    behind = behind_of(clicked_ref)
+    highest, picked = score_side(
+        1,
+        other_ref,
+        users_t_ref,
+        next_users_ref,
+        low_ref,
+        high_ref,
+        behind,
+        own_highest_ref[...],
+        own_picked_ref[...],
+        own_next_q_ref,
+        scores_ref.at[1],
+        next_scores_ref,
+        next_q_ref,
+    )
     highest = jnp.max(highest, axis=0, keepdims=True)
     picked = jnp.sum(picked, axis=0, keepdims=True)
 
@@ -154,17 +229,18 @@
     delta = picked - (rewards_ref[...] + DISCOUNT * mean)
     delta_ref[...] = delta
 
-    def exponentials(block, total):
-        for step in range(BLOCK // 8):
-            rows = slice(step * 8, step * 8 + 8)
-            piece = jnp.exp(scores_ref[block, rows, :] - highest)
-            scores_ref[block, rows, :] = piece
-            total = total + piece
-        return total
-
-    total = lax.fori_loop(
-        0, CHIPS * CORES, exponentials, jnp.zeros((8, sessions), F32), unroll=8
-    )
+    total = jnp.zeros((8, sessions), F32)
+    for side, from_ref in enumerate((own_scores_ref, scores_ref.at[1])):
+
+        def exponentials(chip, total):
+            for step in range(BLOCK // 8):
+                rows = slice(step * 8, step * 8 + 8)
+                piece = jnp.exp(from_ref[chip, rows, :] - highest)
+                scores_ref[side, chip, rows, :] = piece
+                total = total + piece
+            return total
+
+        total = lax.fori_loop(0, CHIPS, exponentials, total, unroll=4)
     total = jnp.sum(total, axis=0, keepdims=True)
     scale = 1.0 / sessions
     gain = jnp.broadcast_to((PENALTY * scale) / total, (8, sessions))
@@ -176,7 +252,7 @@
             pieces = []
             for inner in range(2):
                 row = step * 16 + inner * 8
-                piece = scores_ref[block, row : row + 8, :] * gain
+                piece = scores_ref[side, chip, row : row + 8, :] * gain
                 pieces.append(
                     piece + jnp.where(behind == block * BLOCK + row, extra, 0.0)
                 )
@@ -248,29 +324,53 @@
     first_ref,
     second_ref,
     tower_ref,
+    new_first_out,
+    new_second_out,
+    direction_out,
+    grad_hidden_out,
+    grad_embed_out,
     new_first_ref,
     new_second_ref,
     direction_ref,
     grad_hidden_ref,
     grad_embed_ref,
+    sems,
 ):
+    copies = []
+
+    def send(source, target):
+        copies.append(pltpu.make_async_copy(source, target, sems.at[len(copies)]))
+        copies[-1].start()
+
     for item in range(CHIPS * CORES):
         for quarter in range(4):
             grad_hidden_ref[item * 16 : item * 16 + 16, quarter * 128 : quarter * 128 + 128] = (
                 tower_ref[item, quarter * 16 : quarter * 16 + 16, :].astype(F32)
             )
         grad_embed_ref[item * 32 : item * 32 + 32, :] = tower_ref[item, 64:, :].astype(F32)
-    shape = (first_ref.shape[0], BLOCK)
-    onehot = lax.broadcasted_iota(jnp.int32, shape, 0) == rows_ref[...]
+    send(grad_hidden_ref, grad_hidden_out)
+    send(grad_embed_ref, grad_embed_out)
     grad = jnp.concatenate([pieces_ref[z, :SHARE, :] for z in range(DP[1])], axis=0)
-    table_grad = dot(onehot.astype(F32).astype(BF16), grad)
-    new_first = BETA_ONE * first_ref[...] + (1.0 - BETA_ONE) * table_grad
-    new_second = BETA_TWO * second_ref[...] + (1.0 - BETA_TWO) * table_grad * table_grad
-    new_first_ref[...] = new_first
-    new_second_ref[...] = new_second
+    length = first_ref.shape[0] // STEPS
     correct_one = 1.0 - BETA_ONE**ADAM_STEP
     correct_two = 1.0 - BETA_TWO**ADAM_STEP
-    direction_ref[...] = new_first / correct_one / (jnp.sqrt(new_second / correct_two) + EPSILON)
+    for step in range(STEPS):
+        rows = pl.ds(step * length, length)
+        place = lax.broadcasted_iota(jnp.int32, (length, BLOCK), 0) + step * length
+        onehot = place == rows_ref[...]
+        table_grad = dot(onehot.astype(F32).astype(BF16), grad)
+        new_first = BETA_ONE * first_ref[rows, :] + (1.0 - BETA_ONE) * table_grad
+        new_second = BETA_TWO * second_ref[rows, :] + (1.0 - BETA_TWO) * table_grad * table_grad
+        new_first_ref[rows, :] = new_first
+        new_second_ref[rows, :] = new_second
+        direction_ref[rows, :] = (
+            new_first / correct_one / (jnp.sqrt(new_second / correct_two) + EPSILON)
+        )
+        send(new_first_ref.at[rows], new_first_out.at[rows])
+        send(new_second_ref.at[rows], new_second_out.at[rows])
+        send(direction_ref.at[rows], direction_out.at[rows])
+    for copy in copies:
+        copy.wait()
 
 
 def in_vmem(kernel, array, shape):
@@ -288,49 +388,70 @@
     return lax.all_to_all(array, axes, 0, 0, tiled=True)
 
 
-def tower_call(core, states, next_states, next_slate_t, w_hidden, w_embed):
+def tower_call(core, states, next_states, next_slate_t, slate_t, chosen, w_hidden, w_embed):
     sessions = states.shape[0]
     hidden, embed = w_embed.shape
     vmem = pl.BlockSpec(memory_space=pltpu.VMEM)
     places = jax.ShapeDtypeStruct((sessions, 128), jnp.int32)
     return pl.pallas_call(
         tower_kernel,
-        in_specs=[pl.BlockSpec(memory_space=pltpu.SMEM)] + [vmem] * 5,
-        out_specs=[vmem] * 5,
+        in_specs=[pl.BlockSpec(memory_space=pltpu.SMEM)] + [vmem] * 7,
+        out_specs=[vmem] * 6,
         out_shape=[
             jax.ShapeDtypeStruct((hidden, sessions), BF16),
             jax.ShapeDtypeStruct((embed, sessions), BF16),
             jax.ShapeDtypeStruct((sessions, embed), BF16),
             places,
             places,
+            jax.ShapeDtypeStruct((1, sessions), jnp.int32),
         ],
         compiler_params=PARAMS,
-    )(core, states, next_states, next_slate_t, w_hidden, w_embed)
-
-
-def main_call(core, states, towers, rewards, slate_t, chosen, own, other, w_embed):
+    )(core, states, next_states, next_slate_t, slate_t, chosen, w_hidden, w_embed)
+
+
+def own_call(towers, own):
+    sessions = towers[1].shape[1]
+    vmem = pl.BlockSpec(memory_space=pltpu.VMEM)
+    line = jax.ShapeDtypeStruct((8, sessions), F32)
+    return pl.pallas_call(
+        own_kernel,
+        in_specs=[vmem] * 6,
+        out_specs=[vmem] * 4,
+        out_shape=[
+            jax.ShapeDtypeStruct((CHIPS, BLOCK, sessions), F32),
+            line,
+            line,
+            jax.ShapeDtypeStruct((sessions, 128), F32),
+        ],
+        scratch_shapes=[pltpu.VMEM((CHIPS * 2, sessions, 128), F32)],
+        compiler_params=PARAMS,
+    )(*towers[1:], own)
+
+
+def main_call(core, states, towers, rewards, own, other, begun, w_embed):
     sessions, features = states.shape
     hidden, embed = w_embed.shape
     vmem = pl.BlockSpec(memory_space=pltpu.VMEM)
+    pack = (CHIPS, PACK, embed)
     return pl.pallas_call(
         main_kernel,
-        in_specs=[pl.BlockSpec(memory_space=pltpu.SMEM)] + [vmem] * 12,
+        in_specs=[pl.BlockSpec(memory_space=pltpu.SMEM)] + [vmem] * 15,
         out_specs=[vmem] * 3,
         out_shape=[
-            jax.ShapeDtypeStruct((CHIPS, PACK, embed), F32),
-            jax.ShapeDtypeStruct((CHIPS, PACK, embed), BF16),
+            jax.ShapeDtypeStruct(pack, F32),
+            jax.ShapeDtypeStruct(pack, BF16),
             jax.ShapeDtypeStruct((1, sessions), F32),
         ],
         scratch_shapes=[
-            pltpu.VMEM((CHIPS * CORES, BLOCK, sessions), F32),
-            pltpu.VMEM((CHIPS * CORES * 2, sessions, 128), F32),
+            pltpu.VMEM((CORES, CHIPS, BLOCK, sessions), F32),
+            pltpu.VMEM((CHIPS * 2, sessions, 128), F32),
             pltpu.VMEM((sessions, 128), F32),
             pltpu.VMEM((CHIPS * CORES, BLOCK, sessions), BF16),
             pltpu.VMEM((features, hidden), F32),
             pltpu.VMEM((hidden, embed), F32),
         ],
         compiler_params=PARAMS,
-    )(core, states, *towers, rewards, slate_t, chosen, own, other, w_embed)
+    )(core, states, *towers, rewards, own, other, *begun, w_embed)
 
 
 def shards(
@@ -356,20 +477,15 @@
     local_rows = table.at[cand_rows].get(mode="promise_in_bounds", unique_indices=True)
     copies = in_vmem(copies_kernel, local_rows, (CHIPS, BLOCK, embed))
     core = lax.axis_index("c").astype(jnp.int32).reshape(1)
-    towers = tower_call(core, states, next_states, next_slate.T, w_hidden, w_embed)
+    chosen = chosen.reshape(1, sessions)
+    towers = tower_call(
+        core, states, next_states, next_slate.T, slate_ids.T, chosen, w_hidden, w_embed
+    )
     own = swap(copies, ("x", "l"))
     other = lax.ppermute(own, "c", pair)
-    keep, send, delta = main_call(
-        core,
-        states,
-        towers,
-        rewards.reshape(1, sessions),
-        slate_ids.T,
-        chosen.reshape(1, sessions),
-        own,
-        other,
-        w_embed,
-    )
+    begun = own_call(towers, own)
+    rewards = rewards.reshape(1, sessions)
+    keep, send, delta = main_call(core, states, towers, rewards, own, other, begun, w_embed)
 
     got = lax.ppermute(send, "c", pair)
     part = (keep + got.astype(F32)).astype(BF16)
@@ -379,18 +495,15 @@
     tower = in_vmem(tower_copies_kernel, pieces, (CHIPS * CORES, PACK - BLOCK, embed))
     tower = swap(tower, ITEM)
 
-    moment = jax.ShapeDtypeStruct(first_moment.shape, F32)
+    last = [jax.ShapeDtypeStruct(first_moment.shape, F32)] * 3
+    last += [jax.ShapeDtypeStruct(array.shape, F32) for array in (w_hidden, w_embed)]
     new_first, new_second, direction, grad_hidden, grad_embed = pl.pallas_call(
         adam_kernel,
         in_specs=[vmem] * 5,
-        out_specs=[vmem] * 5,
-        out_shape=[
-            moment,
-            moment,
-            moment,
-            jax.ShapeDtypeStruct(w_hidden.shape, F32),
-            jax.ShapeDtypeStruct(w_embed.shape, F32),
-        ],
+        out_specs=[pl.BlockSpec(memory_space=pl.ANY)] * 5,
+        out_shape=last,
+        scratch_shapes=[pltpu.VMEM(out.shape, F32) for out in last]
+        + [pltpu.SemaphoreType.DMA((2 + 3 * STEPS,))],
         compiler_params=PARAMS,
     )(rows, pieces, first_moment, second_moment, tower)
     return (new_first, new_second, direction, grad_hidden, grad_embed, delta.reshape(sessions))

time: 107 us -> 107 us (level)
    pallas_call x1 -> x2, Pallas kernels: 1.9 us -> 3.83 us  [the longest x1 1.92 us: shards(): pl.pallas_call(adam_kernel, in_specs=[vmem] * 5, out_specs=[pl.BlockSpec(...]
    pallas_call x1, Pallas kernels: 7.7 us -> 6.2 us  [main_call(): pl.pallas_call(main_kernel, in_specs=[pl.BlockSpec(memory_space=pltpu.SME...]
  transfers between devices with their start and end apart: 2 -> 2, of which waited for: 2 -> 1; matrix products, arithmetic and copies ran while one was open for 0% -> 0% of each run, Pallas kernels for 1% -> 3%
where the time goes in v6:
time: 107 us
  blocking collectives  82 us (77%)
  Pallas kernels  11.2 us (10%)
  starting transfers between devices  8.59 us (8%)
  waiting for transfers between devices  2.16 us (2%)
  local copies, waits for them, and re-layouts  1.09 us (1%)
    all_to_all x5, blocking collectives, swap(): return lax.all_to_all(array, axes, 0, 0, tiled=True)  82 us
    ppermute x1, starting transfers between devices, shards(): other = lax.ppermute(own, 'c', pair)  6.68 us
    pallas_call x1, Pallas kernels, main_call(): pl.pallas_call(main_kernel, in_specs=[pl.BlockSpec(memory_space=pltpu.SME...  6.2 us
    ppermute x1, waiting for transfers between devices, shards(): got = lax.ppermute(send, 'c', pair)  2.16 us
  transfers between devices with their start and end apart: 2, of which 1 were waited for; matrix products, arithmetic and copies ran while one was open for 0% of the time, Pallas kernels for 3%

profile of v6, /device:TPU:1, one launch (start us, length us, event | category | flops | bytes accessed | tf_op | source)
XLA Modules:
  0.0 106.7 jit_solution(14458935550702421343)
XLA Ops:
  0.6 0.0 copy-start
  0.6 0.7 compare_select_fusion
  1.4 0.3 copy-done
  1.7 0.0 copy-start.1
  1.7 0.0 copy-start.2
  1.7 0.0 copy-start.5
  1.7 0.0 copy-start.6
  1.7 0.0 copy-start.7
  1.7 0.0 copy-start.8
  1.7 0.0 copy-start.10
  1.7 0.7 gather_fusion
  2.5 0.0 copy-start.11
  2.5 13.2 %all_to_all.25.own_ref = bf16[8,256,128]{2,1,0:T(8,128)(2,1)S(1)} all-to-all(bf16[8,256,128]{2,1,0:T(8,128)(2,1)S(1)} %shard_map.164), channel_id=1, replica_groups=mesh['h'=4,'z'=8,'x'=4,'l'=2,'c'=2] {'x','l'}, dimensions={0} | all-to-all | bytes 1048576 | tf_op jit(solution)/shard_map/all_to_all | solution.py:388
  15.7 6.7 %collective-permute-start = (bf16[8,256,128]{2,1,0:T(8,128)(2,1)S(1)}, bf16[8,256,128]{2,1,0:T(8,128)(2,1)S(1)}, u32[]{:S(2)}, u32[]{:S(2)}) collective-permute-start(bf16[8,256,128]{2,1,0:T(8,128)(2,1)S(1)} %all_to_all.25.own_ref), channel_id=1, source_target_pairs={{0,1},{1,0},{2,3},{3,2},{4,5},{5,4},{6,7},{7,6},{8,9},{9,8},{10,11... | collective-permute-start | bytes 1572872 | tf_op jit(solution)/shard_map/ppermute | solution.py:485
  22.4 0.0 copy-done.1
  22.4 0.0 copy-done.2
  22.4 0.0 copy-done.5
  22.4 0.0 copy-done.6
  22.5 0.0 copy-done.7
  22.5 0.0 copy-done.8
  22.5 0.0 copy-done.10
  22.5 0.9 shard_map.163
  23.4 1.9 %shard_map.165 = (f32[8,256,512]{2,1,0:T(8,128)S(1)}, f32[8,512]{1,0:T(8,128)S(1)}, f32[8,512]{1,0:T(8,128)S(1)}, f32[512,128]{1,0:T(8,128)S(1)}) custom-call(bf16[128,512]{1,0:T(8,128)(2,1)S(1)} %get-tuple-element.25.users_t_ref, bf16[512,128]{1,0:T(8,128)(2,1)S(1)} %get-tuple-element.26.next_users_ref, s32[512,128]{1,0:T(8,128)S(1)} %get-tuple-element.27.low_ref, ...), custom_call_target="tpu_custom_call" | custom-call | tf_op jit(solution)/shard_map/pallas_call | solution.py:416
  25.3 0.0 collective-permute-done.other_ref
  25.3 0.0 copy-done.11
  25.3 6.2 %shard_map.166 = (f32[8,352,128]{2,1,0:T(8,128)S(1)}, bf16[8,352,128]{2,1,0:T(8,128)(2,1)S(1)}, f32[1,512]{1,0:T(1,128)}) custom-call(s32[1]{0:T(128)} %bitcast.1.core_ref, bf16[512,256]{1,0:T(8,128)(2,1)S(1)} %copy-done.1, bf16[512,512]{1,0:T(8,128)(2,1)S(1)} %get-tuple-element.24.hidden_t_ref, bf16[128,512]{1,0:T(8,128)(2,1)S(1)} %get-tuple-element.25.users_t_ref, ...), custom_call_target="tpu_custom_call" | custom-call | tf_op jit(solution)/shard_map/pallas_call | solution.py:436
  31.5 1.9 %collective-permute-start.1 = (bf16[8,352,128]{2,1,0:T(8,128)(2,1)S(1)}, bf16[8,352,128]{2,1,0:T(8,128)(2,1)S(1)}, u32[]{:S(2)}, u32[]{:S(2)}) collective-permute-start(bf16[8,352,128]{2,1,0:T(8,128)(2,1)S(1)} %get-tuple-element.35), channel_id=1, source_target_pairs={{0,1},{1,0},{2,3},{3,2},{4,5},{5,4},{6,7},{7,6},{8,9},{9,8},{10,11... | collective-permute-start | bytes 2162696 | tf_op jit(solution)/shard_map/ppermute | solution.py:490
  33.4 2.2 %collective-permute-done.1 = bf16[8,352,128]{2,1,0:T(8,128)(2,1)S(1)} collective-permute-done((bf16[8,352,128]{2,1,0:T(8,128)(2,1)S(1)}, bf16[8,352,128]{2,1,0:T(8,128)(2,1)S(1)}, u32[]{:S(2)}, u32[]{:S(2)}) %collective-permute-start.1) | collective-permute-done | bytes 720928 | tf_op jit(solution)/shard_map/ppermute | solution.py:490
  35.6 0.2 add_convert_fusion
  35.8 14.5 %all_to_all.26.parts_ref = bf16[8,352,128]{2,1,0:T(8,128)(2,1)S(1)} all-to-all(bf16[8,352,128]{2,1,0:T(8,128)(2,1)S(1)} %add_convert_fusion), channel_id=1, replica_groups=mesh['h'=4,'z'=8,'x'=4,'l'=2,'c'=2] {'x','l'}, dimensions={0} | all-to-all | bytes 1441792 | tf_op jit(solution)/shard_map/all_to_all | solution.py:388
  50.3 0.1 shard_map.167
  50.4 0.0 copy-start.3
  50.4 0.0 copy-start.4
  50.4 0.0 copy-start.9
  50.4 26.8 %all_to_all.27.parts_ref = bf16[32,48,128]{2,1,0:T(8,128)(2,1)S(1)} all-to-all(bf16[32,48,128]{2,1,0:T(8,128)(2,1)S(1)} %shard_map.167), channel_id=1, replica_groups=mesh['h'=4,'z'=8,'x'=4,'l'=2,'c'=2] {'h','z'}, dimensions={0} | all-to-all | bytes 786432 | tf_op jit(solution)/shard_map/all_to_all | solution.py:388
  77.2 0.1 shard_map.168
  77.3 10.8 %all_to_all.28.pieces_ref = bf16[8,48,128]{2,1,0:T(8,128)(2,1)S(1)} all-to-all(bf16[8,48,128]{2,1,0:T(8,128)(2,1)S(1)} %shard_map.168), channel_id=1, replica_groups=mesh['h'=4,'z'=8,'x'=4,'l'=2,'c'=2] {'z'}, dimensions={0} | all-to-all | bytes 196608 | tf_op jit(solution)/shard_map/all_to_all | solution.py:388
  88.1 0.1 shard_map.169
  88.1 16.7 %all_to_all.29.tower_ref = bf16[16,96,128]{2,1,0:T(8,128)(2,1)S(1)} all-to-all(bf16[16,96,128]{2,1,0:T(8,128)(2,1)S(1)} %shard_map.169), channel_id=1, replica_groups=mesh['h'=4,'z'=8,'x'=4,'l'=2,'c'=2] {'x','l','c'}, dimensions={0} | all-to-all | bytes 786432 | tf_op jit(solution)/shard_map/all_to_all | solution.py:388
  104.8 0.0 copy-done.3
  104.8 0.0 copy-done.4
  104.8 0.0 copy-done.9
  104.8 1.9 %shard_map.170 = (f32[1024,128]{1,0:T(8,128)}, f32[1024,128]{1,0:T(8,128)}, f32[1024,128]{1,0:T(8,128)}, f32[256,512]{1,0:T(8,128)}, f32[512,128]{1,0:T(8,128)}) custom-call(s32[1,256]{1,0:T(1,128)S(1)} %bitcast.9, bf16[8,48,128]{2,1,0:T(8,128)(2,1)S(1)} %all_to_all.28.pieces_ref, f32[1024,128]{1,0:T(8,128)S(1)} %copy-done.3, f32[1024,128]{1,0:T(8,128)S(1)} %copy-done.4, ...), custom_call_target="tpu_custom_call" | custom-call | tf_op jit(solution)/shard_map/pallas_call | solution.py:500
  (2 shorter events, 0.0 us)
Async XLA Ops:
  0.6 1.1 copy-start
  1.7 20.7 %copy-start.1 = (bf16[512,256]{1,0:T(8,128)(2,1)S(1)}, bf16[512,256]{1,0:T(8,128)(2,1)}, u32[]{:S(2)}) copy-start(bf16[512,256]{1,0:T(8,128)(2,1)} %states_ref.3) | copy-start | bytes 786436
  1.7 20.7 %copy-start.2 = (bf16[512,128]{1,0:T(8,128)(2,1)S(1)}, bf16[512,128]{1,0:T(8,128)(2,1)}, u32[]{:S(2)}) copy-start(bf16[512,128]{1,0:T(8,128)(2,1)} %w_embed_ref.3) | copy-start | bytes 393220
  1.7 20.7 %copy-start.5 = (bf16[512,256]{1,0:T(8,128)(2,1)S(1)}, bf16[512,256]{1,0:T(8,128)(2,1)}, u32[]{:S(2)}) copy-start(bf16[512,256]{1,0:T(8,128)(2,1)} %next_ref.1) | copy-start | bytes 786436
  1.7 20.7 %copy-start.6 = (bf16[256,512]{1,0:T(8,128)(2,1)S(1)}, bf16[256,512]{1,0:T(8,128)(2,1)}, u32[]{:S(2)}) copy-start(bf16[256,512]{1,0:T(8,128)(2,1)} %w_hidden_ref.1) | copy-start | bytes 786436
  1.7 20.8 %copy-start.7 = (s32[512,10]{0,1:T(8,128)S(1)}, s32[512,10]{0,1:T(8,128)}, u32[]{:S(2)}) copy-start(s32[512,10]{0,1:T(8,128)} %param.17) | copy-start | bytes 61444
  1.7 20.7 %copy-start.8 = (s32[512,10]{0,1:T(8,128)S(1)}, s32[512,10]{0,1:T(8,128)}, u32[]{:S(2)}) copy-start(s32[512,10]{0,1:T(8,128)} %param.15) | copy-start | bytes 61444
  1.7 20.7 %copy-start.10 = (s32[512]{0:T(512)S(1)}, s32[512]{0:T(512)}, u32[]{:S(2)}) copy-start(s32[512]{0:T(512)} %param.16) | copy-start | bytes 6148
  2.5 22.8 %copy-start.11 = (f32[512]{0:T(512)S(1)}, f32[512]{0:T(512)}, u32[]{:S(2)}) copy-start(f32[512]{0:T(512)} %param.14) | copy-start | bytes 6148
  15.7 9.6 %collective-permute-start = (bf16[8,256,128]{2,1,0:T(8,128)(2,1)S(1)}, bf16[8,256,128]{2,1,0:T(8,128)(2,1)S(1)}, u32[]{:S(2)}, u32[]{:S(2)}) collective-permute-start(bf16[8,256,128]{2,1,0:T(8,128)(2,1)S(1)} %all_to_all.25.own_ref), channel_id=1, source_target_pairs={{0,1},{1,0},{2,3},{3,2},{4,5},{5,4},{6,7},{7,6},{8,9},{9,8},{10,11... | collective-permute-start | bytes 1572872 | tf_op jit(solution)/shard_map/ppermute | solution.py:485
  31.5 4.1 %collective-permute-start.1 = (bf16[8,352,128]{2,1,0:T(8,128)(2,1)S(1)}, bf16[8,352,128]{2,1,0:T(8,128)(2,1)S(1)}, u32[]{:S(2)}, u32[]{:S(2)}) collective-permute-start(bf16[8,352,128]{2,1,0:T(8,128)(2,1)S(1)} %get-tuple-element.35), channel_id=1, source_target_pairs={{0,1},{1,0},{2,3},{3,2},{4,5},{5,4},{6,7},{7,6},{8,9},{9,8},{10,11... | collective-permute-start | bytes 2162696 | tf_op jit(solution)/shard_map/ppermute | solution.py:490
  50.4 54.5 %copy-start.3 = (f32[1024,128]{1,0:T(8,128)S(1)}, f32[1024,128]{1,0:T(8,128)}, u32[]{:S(2)}) copy-start(f32[1024,128]{1,0:T(8,128)} %first_ref.1) | copy-start | bytes 1572868
  50.4 54.5 %copy-start.4 = (f32[1024,128]{1,0:T(8,128)S(1)}, f32[1024,128]{1,0:T(8,128)}, u32[]{:S(2)}) copy-start(f32[1024,128]{1,0:T(8,128)} %second_ref.1) | copy-start | bytes 1572868
  50.4 54.4 %copy-start.9 = (s32[256]{0:T(256)S(1)}, s32[256]{0:T(256)}, u32[]{:S(2)}) copy-start(s32[256]{0:T(256)} %param.21) | copy-start | bytes 3076

commit v7 on v6

--- a/solution.py
+++ b/solution.py
@@ -20,9 +20,9 @@
 CORES = 2
 BLOCK = 256
 PACK = 352
-DP = (4, 8)
-SHARE = BLOCK // 8
-PIECE = SHARE + 16
+DP = 32
+PIECE = 16
+TOWER_PIECES = (PACK - BLOCK) // 8
 SLATE = 10
 STEPS = 4
 F32 = jnp.float32
@@ -284,22 +284,22 @@
 
 
 def cut_kernel(parts_ref, out_ref):
-    def total(first, length):
-        rows = slice(first, first + length)
+    def total(first):
+        rows = slice(first, first + 16)
         return sum(parts_ref[chip, rows, :].astype(F32) for chip in range(parts_ref.shape[0]))
 
-    for z in range(DP[1]):
-        if z < 4:
-            tower = total(BLOCK + z * 16, 16)
-        else:
-            both = total(BLOCK + 64 + (z - 4) // 2 * 16, 16)
-            half = both[(z - 4) % 2 * 8 : (z - 4) % 2 * 8 + 8]
-            tower = jnp.concatenate([half, jnp.zeros_like(half)], axis=0)
-        cands = total(z * SHARE, SHARE).astype(BF16)
-        tower = tower.astype(BF16)
-        for h in range(DP[0]):
-            out_ref[h * DP[1] + z, :SHARE, :] = cands
-            out_ref[h * DP[1] + z, SHARE:, :] = tower
+    towers = []
+    for first in range(BLOCK, PACK, 16):
+        both = total(first)
+        towers += [both[:8], both[8:]]
+    for first in range(0, BLOCK, 16):
+        both = total(first)
+        for inner in range(2):
+            piece = first // 8 + inner
+            tower = towers[piece] if piece < TOWER_PIECES else jnp.zeros_like(both[:8])
+            out_ref[piece] = jnp.concatenate(
+                [both[inner * 8 : inner * 8 + 8], tower], axis=0
+            ).astype(BF16)
 
 
 def piece_kernel(parts_ref, out_ref):
@@ -309,11 +309,9 @@
 
 
 def tower_copies_kernel(pieces_ref, out_ref):
-    parts = [pieces_ref[z, SHARE:, :] for z in range(4)]
-    for z in range(4, 8, 2):
-        halves = [pieces_ref[z + more, SHARE:, :].astype(F32)[:8] for more in range(2)]
-        parts.append(jnp.concatenate(halves, axis=0).astype(BF16))
-    rows = jnp.concatenate(parts, axis=0)
+    rows = jnp.concatenate(
+        [pieces_ref[piece].astype(F32)[8:] for piece in range(TOWER_PIECES)], axis=0
+    ).astype(BF16)
     for copy in range(out_ref.shape[0]):
         out_ref[copy] = rows
 
@@ -342,15 +340,18 @@
         copies.append(pltpu.make_async_copy(source, target, sems.at[len(copies)]))
         copies[-1].start()
 
-    for item in range(CHIPS * CORES):
+    for sender in range(CHIPS * CORES):
+        item = sender // 4 * 4 + sender % 2 * 2 + sender // 2 % 2
         for quarter in range(4):
             grad_hidden_ref[item * 16 : item * 16 + 16, quarter * 128 : quarter * 128 + 128] = (
-                tower_ref[item, quarter * 16 : quarter * 16 + 16, :].astype(F32)
+                tower_ref[sender, quarter * 16 : quarter * 16 + 16, :].astype(F32)
             )
-        grad_embed_ref[item * 32 : item * 32 + 32, :] = tower_ref[item, 64:, :].astype(F32)
+        grad_embed_ref[item * 32 : item * 32 + 32, :] = tower_ref[sender, 64:, :].astype(F32)
     send(grad_hidden_ref, grad_hidden_out)
     send(grad_embed_ref, grad_embed_out)
-    grad = jnp.concatenate([pieces_ref[z, :SHARE, :] for z in range(DP[1])], axis=0)
+    grad = jnp.concatenate(
+        [pieces_ref[piece].astype(F32)[:8] for piece in range(DP)], axis=0
+    ).astype(BF16)
     length = first_ref.shape[0] // STEPS
     correct_one = 1.0 - BETA_ONE**ADAM_STEP
     correct_two = 1.0 - BETA_TWO**ADAM_STEP
@@ -489,11 +490,11 @@
 
     got = lax.ppermute(send, "c", pair)
     part = (keep + got.astype(F32)).astype(BF16)
-    share = in_vmem(cut_kernel, swap(part, ("x", "l")), (DP[0] * DP[1], PIECE, embed))
-    share = in_vmem(piece_kernel, swap(share, ("h", "z")), (DP[1], PIECE, embed))
-    pieces = swap(share, "z")
+    pieces = in_vmem(cut_kernel, swap(part, ("x", "l")), (DP, PIECE, embed))
+    pieces = in_vmem(piece_kernel, swap(pieces, ("z", "h")), (DP, PIECE, embed))
+    pieces = swap(pieces, ("z", "h"))
     tower = in_vmem(tower_copies_kernel, pieces, (CHIPS * CORES, PACK - BLOCK, embed))
-    tower = swap(tower, ITEM)
+    tower = swap(tower, ("x", "c", "l"))
 
     last = [jax.ShapeDtypeStruct(first_moment.shape, F32)] * 3
     last += [jax.ShapeDtypeStruct(array.shape, F32) for array in (w_hidden, w_embed)]

time: 107 us -> 106 us (level)
  no operation moved by 1% of the time
where the time goes in v7:
time: 106 us
  blocking collectives  81.3 us (77%)
  Pallas kernels  11.1 us (10%)
  starting transfers between devices  8.59 us (8%)
  waiting for transfers between devices  2.16 us (2%)
  local copies, waits for them, and re-layouts  1.09 us (1%)
    all_to_all x5, blocking collectives, swap(): return lax.all_to_all(array, axes, 0, 0, tiled=True)  81.3 us
    ppermute x1, starting transfers between devices, shards(): other = lax.ppermute(own, 'c', pair)  6.68 us
    pallas_call x1, Pallas kernels, main_call(): pl.pallas_call(main_kernel, in_specs=[pl.BlockSpec(memory_space=pltpu.SME...  6.2 us
    ppermute x1, waiting for transfers between devices, shards(): got = lax.ppermute(send, 'c', pair)  2.16 us
  transfers between devices with their start and end apart: 2, of which 1 were waited for; matrix products, arithmetic and copies ran while one was open for 0% of the time, Pallas kernels for 3%

profile of v7, /device:TPU:1, one launch (start us, length us, event | category | flops | bytes accessed | tf_op | source)
XLA Modules:
  0.0 106.0 jit_solution(1704755649018331408)
XLA Ops:
  0.6 0.0 copy-start
  0.6 0.7 compare_select_fusion
  1.4 0.3 copy-done
  1.7 0.0 copy-start.1
  1.7 0.0 copy-start.2
  1.7 0.0 copy-start.5
  1.7 0.0 copy-start.6
  1.7 0.0 copy-start.7
  1.7 0.0 copy-start.8
  1.7 0.0 copy-start.10
  1.7 0.7 gather_fusion
  2.5 0.0 copy-start.11
  2.5 13.2 %all_to_all.25.own_ref = bf16[8,256,128]{2,1,0:T(8,128)(2,1)S(1)} all-to-all(bf16[8,256,128]{2,1,0:T(8,128)(2,1)S(1)} %shard_map.164), channel_id=1, replica_groups=mesh['h'=4,'z'=8,'x'=4,'l'=2,'c'=2] {'x','l'}, dimensions={0} | all-to-all | bytes 1048576 | tf_op jit(solution)/shard_map/all_to_all | solution.py:389
  15.7 6.7 %collective-permute-start = (bf16[8,256,128]{2,1,0:T(8,128)(2,1)S(1)}, bf16[8,256,128]{2,1,0:T(8,128)(2,1)S(1)}, u32[]{:S(2)}, u32[]{:S(2)}) collective-permute-start(bf16[8,256,128]{2,1,0:T(8,128)(2,1)S(1)} %all_to_all.25.own_ref), channel_id=1, source_target_pairs={{0,1},{1,0},{2,3},{3,2},{4,5},{5,4},{6,7},{7,6},{8,9},{9,8},{10,11... | collective-permute-start | bytes 1572872 | tf_op jit(solution)/shard_map/ppermute | solution.py:486
  22.4 0.0 copy-done.1
  22.4 0.0 copy-done.2
  22.4 0.0 copy-done.5
  22.4 0.0 copy-done.6
  22.5 0.0 copy-done.7
  22.5 0.0 copy-done.8
  22.5 0.0 copy-done.10
  22.5 0.9 shard_map.163
  23.4 1.9 %shard_map.165 = (f32[8,256,512]{2,1,0:T(8,128)S(1)}, f32[8,512]{1,0:T(8,128)S(1)}, f32[8,512]{1,0:T(8,128)S(1)}, f32[512,128]{1,0:T(8,128)S(1)}) custom-call(bf16[128,512]{1,0:T(8,128)(2,1)S(1)} %get-tuple-element.25.users_t_ref, bf16[512,128]{1,0:T(8,128)(2,1)S(1)} %get-tuple-element.26.next_users_ref, s32[512,128]{1,0:T(8,128)S(1)} %get-tuple-element.27.low_ref, ...), custom_call_target="tpu_custom_call" | custom-call | tf_op jit(solution)/shard_map/pallas_call | solution.py:417
  25.3 0.0 collective-permute-done.other_ref
  25.3 0.0 copy-done.11
  25.3 6.2 %shard_map.166 = (f32[8,352,128]{2,1,0:T(8,128)S(1)}, bf16[8,352,128]{2,1,0:T(8,128)(2,1)S(1)}, f32[1,512]{1,0:T(1,128)}) custom-call(s32[1]{0:T(128)} %bitcast.1.core_ref, bf16[512,256]{1,0:T(8,128)(2,1)S(1)} %copy-done.1, bf16[512,512]{1,0:T(8,128)(2,1)S(1)} %get-tuple-element.24.hidden_t_ref, bf16[128,512]{1,0:T(8,128)(2,1)S(1)} %get-tuple-element.25.users_t_ref, ...), custom_call_target="tpu_custom_call" | custom-call | tf_op jit(solution)/shard_map/pallas_call | solution.py:437
  31.5 1.9 %collective-permute-start.1 = (bf16[8,352,128]{2,1,0:T(8,128)(2,1)S(1)}, bf16[8,352,128]{2,1,0:T(8,128)(2,1)S(1)}, u32[]{:S(2)}, u32[]{:S(2)}) collective-permute-start(bf16[8,352,128]{2,1,0:T(8,128)(2,1)S(1)} %get-tuple-element.35), channel_id=1, source_target_pairs={{0,1},{1,0},{2,3},{3,2},{4,5},{5,4},{6,7},{7,6},{8,9},{9,8},{10,11... | collective-permute-start | bytes 2162696 | tf_op jit(solution)/shard_map/ppermute | solution.py:491
  33.4 2.2 %collective-permute-done.1 = bf16[8,352,128]{2,1,0:T(8,128)(2,1)S(1)} collective-permute-done((bf16[8,352,128]{2,1,0:T(8,128)(2,1)S(1)}, bf16[8,352,128]{2,1,0:T(8,128)(2,1)S(1)}, u32[]{:S(2)}, u32[]{:S(2)}) %collective-permute-start.1) | collective-permute-done | bytes 720928 | tf_op jit(solution)/shard_map/ppermute | solution.py:491
  35.6 0.2 add_convert_fusion
  35.8 14.5 %all_to_all.26.parts_ref = bf16[8,352,128]{2,1,0:T(8,128)(2,1)S(1)} all-to-all(bf16[8,352,128]{2,1,0:T(8,128)(2,1)S(1)} %add_convert_fusion), channel_id=1, replica_groups=mesh['h'=4,'z'=8,'x'=4,'l'=2,'c'=2] {'x','l'}, dimensions={0} | all-to-all | bytes 1441792 | tf_op jit(solution)/shard_map/all_to_all | solution.py:389
  50.3 0.0 copy-start.3
  50.3 0.0 copy-start.4
  50.3 0.0 copy-start.9
  50.3 0.1 shard_map.167
  50.4 24.4 %all_to_all.27.parts_ref = bf16[32,16,128]{2,1,0:T(8,128)(2,1)S(1)} all-to-all(bf16[32,16,128]{2,1,0:T(8,128)(2,1)S(1)} %shard_map.167), channel_id=1, replica_groups=mesh['h'=4,'z'=8,'x'=4,'l'=2,'c'=2] {'z','h'}, dimensions={0} | all-to-all | bytes 262144 | tf_op jit(solution)/shard_map/all_to_all | solution.py:389
  74.8 14.4 %all_to_all.28.pieces_ref = bf16[32,16,128]{2,1,0:T(8,128)(2,1)S(1)} all-to-all(bf16[32,16,128]{2,1,0:T(8,128)(2,1)S(1)} %shard_map.168), channel_id=1, replica_groups=mesh['h'=4,'z'=8,'x'=4,'l'=2,'c'=2] {'z','h'}, dimensions={0} | all-to-all | bytes 262144 | tf_op jit(solution)/shard_map/all_to_all | solution.py:389
  89.2 0.1 shard_map.169
  89.3 14.8 %all_to_all.29.tower_ref = bf16[16,96,128]{2,1,0:T(8,128)(2,1)S(1)} all-to-all(bf16[16,96,128]{2,1,0:T(8,128)(2,1)S(1)} %shard_map.169), channel_id=1, replica_groups=mesh['h'=4,'z'=8,'x'=4,'l'=2,'c'=2] {'x','c','l'}, dimensions={0} | all-to-all | bytes 786432 | tf_op jit(solution)/shard_map/all_to_all | solution.py:389
  104.1 0.0 copy-done.3
  104.1 0.0 copy-done.4
  104.1 0.0 copy-done.9
  104.1 1.9 %shard_map.170 = (f32[1024,128]{1,0:T(8,128)}, f32[1024,128]{1,0:T(8,128)}, f32[1024,128]{1,0:T(8,128)}, f32[256,512]{1,0:T(8,128)}, f32[512,128]{1,0:T(8,128)}) custom-call(s32[1,256]{1,0:T(1,128)S(1)} %bitcast.9, bf16[32,16,128]{2,1,0:T(8,128)(2,1)S(1)} %all_to_all.28.pieces_ref, f32[1024,128]{1,0:T(8,128)S(1)} %copy-done.3, f32[1024,128]{1,0:T(8,128)S(1)} %copy-done.4, ...), custom_call_target="tpu_custom_call" | custom-call | tf_op jit(solution)/shard_map/pallas_call | solution.py:501
  (3 shorter events, 0.1 us)
Async XLA Ops:
  0.6 1.1 %copy-start = (f32[1024,128]{1,0:T(8,128)S(1)}, f32[1024,128]{1,0:T(8,128)}, u32[]{:S(2)}) copy-start(f32[1024,128]{1,0:T(8,128)} %param.18) | copy-start | bytes 1572868
  1.7 20.7 %copy-start.1 = (bf16[512,256]{1,0:T(8,128)(2,1)S(1)}, bf16[512,256]{1,0:T(8,128)(2,1)}, u32[]{:S(2)}) copy-start(bf16[512,256]{1,0:T(8,128)(2,1)} %states_ref.3) | copy-start | bytes 786436
  1.7 20.7 %copy-start.2 = (bf16[512,128]{1,0:T(8,128)(2,1)S(1)}, bf16[512,128]{1,0:T(8,128)(2,1)}, u32[]{:S(2)}) copy-start(bf16[512,128]{1,0:T(8,128)(2,1)} %w_embed_ref.3) | copy-start | bytes 393220
  1.7 20.7 %copy-start.5 = (bf16[512,256]{1,0:T(8,128)(2,1)S(1)}, bf16[512,256]{1,0:T(8,128)(2,1)}, u32[]{:S(2)}) copy-start(bf16[512,256]{1,0:T(8,128)(2,1)} %next_ref.1) | copy-start | bytes 786436
  1.7 20.7 %copy-start.6 = (bf16[256,512]{1,0:T(8,128)(2,1)S(1)}, bf16[256,512]{1,0:T(8,128)(2,1)}, u32[]{:S(2)}) copy-start(bf16[256,512]{1,0:T(8,128)(2,1)} %w_hidden_ref.1) | copy-start | bytes 786436
  1.7 20.8 %copy-start.7 = (s32[512,10]{0,1:T(8,128)S(1)}, s32[512,10]{0,1:T(8,128)}, u32[]{:S(2)}) copy-start(s32[512,10]{0,1:T(8,128)} %param.17) | copy-start | bytes 61444
  1.7 20.7 %copy-start.8 = (s32[512,10]{0,1:T(8,128)S(1)}, s32[512,10]{0,1:T(8,128)}, u32[]{:S(2)}) copy-start(s32[512,10]{0,1:T(8,128)} %param.15) | copy-start | bytes 61444
  1.7 20.7 %copy-start.10 = (s32[512]{0:T(512)S(1)}, s32[512]{0:T(512)}, u32[]{:S(2)}) copy-start(s32[512]{0:T(512)} %param.16) | copy-start | bytes 6148
  2.5 22.8 %copy-start.11 = (f32[512]{0:T(512)S(1)}, f32[512]{0:T(512)}, u32[]{:S(2)}) copy-start(f32[512]{0:T(512)} %param.14) | copy-start | bytes 6148
  15.7 9.6 %collective-permute-start = (bf16[8,256,128]{2,1,0:T(8,128)(2,1)S(1)}, bf16[8,256,128]{2,1,0:T(8,128)(2,1)S(1)}, u32[]{:S(2)}, u32[]{:S(2)}) collective-permute-start(bf16[8,256,128]{2,1,0:T(8,128)(2,1)S(1)} %all_to_all.25.own_ref), channel_id=1, source_target_pairs={{0,1},{1,0},{2,3},{3,2},{4,5},{5,4},{6,7},{7,6},{8,9},{9,8},{10,11... | collective-permute-start | bytes 1572872 | tf_op jit(solution)/shard_map/ppermute | solution.py:486
  31.5 4.1 %collective-permute-start.1 = (bf16[8,352,128]{2,1,0:T(8,128)(2,1)S(1)}, bf16[8,352,128]{2,1,0:T(8,128)(2,1)S(1)}, u32[]{:S(2)}, u32[]{:S(2)}) collective-permute-start(bf16[8,352,128]{2,1,0:T(8,128)(2,1)S(1)} %get-tuple-element.35), channel_id=1, source_target_pairs={{0,1},{1,0},{2,3},{3,2},{4,5},{5,4},{6,7},{7,6},{8,9},{9,8},{10,11... | collective-permute-start | bytes 2162696 | tf_op jit(solution)/shard_map/ppermute | solution.py:491
  50.3 53.8 %copy-start.3 = (f32[1024,128]{1,0:T(8,128)S(1)}, f32[1024,128]{1,0:T(8,128)}, u32[]{:S(2)}) copy-start(f32[1024,128]{1,0:T(8,128)} %first_ref.1) | copy-start | bytes 1572868
  50.3 53.8 %copy-start.4 = (f32[1024,128]{1,0:T(8,128)S(1)}, f32[1024,128]{1,0:T(8,128)}, u32[]{:S(2)}) copy-start(f32[1024,128]{1,0:T(8,128)} %second_ref.1) | copy-start | bytes 1572868
  50.3 53.8 %copy-start.9 = (s32[256]{0:T(256)S(1)}, s32[256]{0:T(256)}, u32[]{:S(2)}) copy-start(s32[256]{0:T(256)} %param.21) | copy-start | bytes 3076

commit v8 on v7

--- a/solution.py
+++ b/solution.py
@@ -181,20 +181,19 @@
     own_picked_ref,
     own_next_q_ref,
     w_embed_ref,
-    keep_ref,
     send_ref,
     delta_ref,
+    own_grad_ref,
+    user_grad_ref,
+    pre_grad_ref,
     scores_ref,
     next_scores_ref,
     next_q_ref,
-    grad_ref,
-    grad_hidden_ref,
-    grad_embed_ref,
-):
-    core = core_ref[0]
+    other_grad_ref,
+):
     sessions = states_ref.shape[0]
     slabs = (own_ref, other_ref)
-    outs = (keep_ref, send_ref)
+    grads = (own_grad_ref, other_grad_ref)
     w_embed = w_embed_ref[...]
     blocks = [(chip, side) for chip in range(CHIPS) for side in range(CORES)]
     behind = behind_of(clicked_ref)
@@ -256,31 +255,44 @@
                 pieces.append(
                     piece + jnp.where(behind == block * BLOCK + row, extra, 0.0)
                 )
-            grad_ref[block, step * 16 : step * 16 + 16, :] = jnp.concatenate(
+            grads[side][chip, step * 16 : step * 16 + 16, :] = jnp.concatenate(
                 pieces, axis=0
             ).astype(BF16)
-        grad = grad_ref[block]
-        slab = slabs[side][chip]
-        user_grad_t = user_grad_t + dot(slab.T, grad)
-        outs[side][chip, :BLOCK, :] = dot(grad, users_t_ref[...], NT).astype(outs[side].dtype)
+        grad = grads[side][chip]
+        user_grad_t = user_grad_t + dot(slabs[side][chip].T, grad)
+        if side == 1:
+            send_ref[chip, :BLOCK, :] = dot(grad, users_t_ref[...], NT).astype(BF16)
     user_grad_t = user_grad_t.astype(BF16)
-
+    user_grad_ref[...] = user_grad_t
     hidden_t = hidden_t_ref[...]
-    grad_embed_ref[...] = dot(hidden_t, user_grad_t, NT)
     back = dot(w_embed, user_grad_t)
     pre_grad_t = jnp.where(hidden_t.astype(F32) > 0, back, 0.0).astype(BF16)
-    grad_hidden_ref[...] = dot(states_ref[...].T, pre_grad_t, NT)
+    pre_grad_ref[...] = pre_grad_t
+    tower_half(1 - core_ref[0], states_ref, hidden_t_ref, user_grad_t, pre_grad_t, send_ref)
+
+
+def tower_half(half, states_ref, hidden_t_ref, user_grad_t, pre_grad_t, out_ref):
+    lanes = pl.ds(pl.multiple_of(half * 128, 128), 128)
+    grad_hidden = dot(states_ref[:, lanes].T, pre_grad_t, NT).astype(out_ref.dtype)
+    rows = pl.ds(pl.multiple_of(half * 256, 256), 256)
+    grad_embed = dot(hidden_t_ref[rows, :], user_grad_t, NT).astype(out_ref.dtype)
     for chip in range(CHIPS):
-        for side in range(CORES):
-            index = chip * CORES + jnp.bitwise_xor(core, side)
-            rows = pl.ds(pl.multiple_of(index * 16, 16), 16)
-            for quarter in range(4):
-                at = BLOCK + quarter * 16
-                outs[side][chip, at : at + 16, :] = grad_hidden_ref[
-                    rows, quarter * 128 : quarter * 128 + 128
-                ].astype(outs[side].dtype)
-            rows = pl.ds(pl.multiple_of(index * 32, 32), 32)
-            outs[side][chip, BLOCK + 64 :, :] = grad_embed_ref[rows, :].astype(outs[side].dtype)
+        for quarter in range(4):
+            at = BLOCK + quarter * 16
+            out_ref[chip, at : at + 16, :] = grad_hidden[
+                chip * 16 : chip * 16 + 16, quarter * 128 : quarter * 128 + 128
+            ]
+        out_ref[chip, BLOCK + 64 :, :] = grad_embed[chip * 32 : chip * 32 + 32]
+
+
+def keep_kernel(
+    core_ref, states_ref, hidden_t_ref, users_t_ref, grad_ref, user_grad_ref, pre_grad_ref, keep_ref
+):
+    for chip in range(CHIPS):
+        keep_ref[chip, :BLOCK, :] = dot(grad_ref[chip], users_t_ref[...], NT)
+    tower_half(
+        core_ref[0], states_ref, hidden_t_ref, user_grad_ref[...], pre_grad_ref[...], keep_ref
+    )
 
 
 def cut_kernel(parts_ref, out_ref):
@@ -341,12 +353,14 @@
         copies[-1].start()
 
     for sender in range(CHIPS * CORES):
-        item = sender // 4 * 4 + sender % 2 * 2 + sender // 2 % 2
+        half, chip = sender // 2 % 2, sender // 4 * 2 + sender % 2
+        row = half * 128 + chip * 16
         for quarter in range(4):
-            grad_hidden_ref[item * 16 : item * 16 + 16, quarter * 128 : quarter * 128 + 128] = (
-                tower_ref[sender, quarter * 16 : quarter * 16 + 16, :].astype(F32)
-            )
-        grad_embed_ref[item * 32 : item * 32 + 32, :] = tower_ref[sender, 64:, :].astype(F32)
+            grad_hidden_ref[row : row + 16, quarter * 128 : quarter * 128 + 128] = tower_ref[
+                sender, quarter * 16 : quarter * 16 + 16, :
+            ].astype(F32)
+        row = half * 256 + chip * 32
+        grad_embed_ref[row : row + 32, :] = tower_ref[sender, 64:, :].astype(F32)
     send(grad_hidden_ref, grad_hidden_out)
     send(grad_embed_ref, grad_embed_out)
     grad = jnp.concatenate(
@@ -430,29 +444,37 @@
 
 
 def main_call(core, states, towers, rewards, own, other, begun, w_embed):
-    sessions, features = states.shape
+    sessions = states.shape[0]
     hidden, embed = w_embed.shape
     vmem = pl.BlockSpec(memory_space=pltpu.VMEM)
-    pack = (CHIPS, PACK, embed)
-    return pl.pallas_call(
+    scalar = pl.BlockSpec(memory_space=pltpu.SMEM)
+    send, delta, *rest = pl.pallas_call(
         main_kernel,
-        in_specs=[pl.BlockSpec(memory_space=pltpu.SMEM)] + [vmem] * 15,
-        out_specs=[vmem] * 3,
+        in_specs=[scalar] + [vmem] * 15,
+        out_specs=[vmem] * 5,
         out_shape=[
-            jax.ShapeDtypeStruct(pack, F32),
-            jax.ShapeDtypeStruct(pack, BF16),
+            jax.ShapeDtypeStruct((CHIPS, PACK, embed), BF16),
             jax.ShapeDtypeStruct((1, sessions), F32),
+            jax.ShapeDtypeStruct((CHIPS, BLOCK, sessions), BF16),
+            jax.ShapeDtypeStruct((embed, sessions), BF16),
+            jax.ShapeDtypeStruct((hidden, sessions), BF16),
         ],
         scratch_shapes=[
             pltpu.VMEM((CORES, CHIPS, BLOCK, sessions), F32),
             pltpu.VMEM((CHIPS * 2, sessions, 128), F32),
             pltpu.VMEM((sessions, 128), F32),
-            pltpu.VMEM((CHIPS * CORES, BLOCK, sessions), BF16),
-            pltpu.VMEM((features, hidden), F32),
-            pltpu.VMEM((hidden, embed), F32),
+            pltpu.VMEM((CHIPS, BLOCK, sessions), BF16),
         ],
         compiler_params=PARAMS,
     )(core, states, *towers, rewards, own, other, *begun, w_embed)
+    keep = pl.pallas_call(
+        keep_kernel,
+        in_specs=[scalar] + [vmem] * 6,
+        out_specs=vmem,
+        out_shape=jax.ShapeDtypeStruct((CHIPS, PACK, embed), F32),
+        compiler_params=PARAMS,
+    )(core, states, *towers[:2], *rest)
+    return keep, send, delta
 
 
 def shards(

time: 106 us -> 106 us (level)
    pallas_call x1 -> x2, Pallas kernels: 6.2 us -> 7.05 us  [the longest x1 6.15 us: main_call(): pl.pallas_call(main_kernel, in_specs=[scalar] + [vmem] * 15, out_specs=[v...]
  transfers between devices with their start and end apart: 2 -> 2, of which waited for: 1 -> 1; matrix products, arithmetic and copies ran while one was open for 0% -> 0% of each run, Pallas kernels for 3% -> 4%
where the time goes in v8:
time: 106 us
  blocking collectives  81.3 us (77%)
  Pallas kernels  12 us (11%)
  starting transfers between devices  8.59 us (8%)
  waiting for transfers between devices  1.26 us (1%)
  local copies, waits for them, and re-layouts  1.09 us (1%)
    all_to_all x5, blocking collectives, swap(): return lax.all_to_all(array, axes, 0, 0, tiled=True)  81.3 us
    ppermute x1, starting transfers between devices, shards(): other = lax.ppermute(own, 'c', pair)  6.68 us
    pallas_call x1, Pallas kernels, main_call(): pl.pallas_call(main_kernel, in_specs=[scalar] + [vmem] * 15, out_specs=[v...  6.15 us
  transfers between devices with their start and end apart: 2, of which 1 were waited for; matrix products, arithmetic and copies ran while one was open for 0% of the time, Pallas kernels for 4%

profile of v8, /device:TPU:1, one launch (start us, length us, event | category | flops | bytes accessed | tf_op | source)
XLA Modules:
  0.0 106.0 jit_solution(4889133463597577830)
XLA Ops:
  0.6 0.0 copy-start
  0.6 0.7 compare_select_fusion
  1.4 0.3 copy-done
  1.7 0.0 copy-start.1
  1.7 0.0 copy-start.2
  1.7 0.0 copy-start.5
  1.7 0.0 copy-start.6
  1.7 0.0 copy-start.7
  1.7 0.0 copy-start.8
  1.7 0.0 copy-start.10
  1.7 0.7 gather_fusion
  2.5 0.0 copy-start.11
  2.5 13.2 %all_to_all.25.own_ref = bf16[8,256,128]{2,1,0:T(8,128)(2,1)S(1)} all-to-all(bf16[8,256,128]{2,1,0:T(8,128)(2,1)S(1)} %shard_map.164), channel_id=1, replica_groups=mesh['h'=4,'z'=8,'x'=4,'l'=2,'c'=2] {'x','l'}, dimensions={0} | all-to-all | bytes 1048576 | tf_op jit(solution)/shard_map/all_to_all | solution.py:403
  15.7 6.7 %collective-permute-start = (bf16[8,256,128]{2,1,0:T(8,128)(2,1)S(1)}, bf16[8,256,128]{2,1,0:T(8,128)(2,1)S(1)}, u32[]{:S(2)}, u32[]{:S(2)}) collective-permute-start(bf16[8,256,128]{2,1,0:T(8,128)(2,1)S(1)} %all_to_all.25.own_ref), channel_id=1, source_target_pairs={{0,1},{1,0},{2,3},{3,2},{4,5},{5,4},{6,7},{7,6},{8,9},{9,8},{10,11... | collective-permute-start | bytes 1572872 | tf_op jit(solution)/shard_map/ppermute | solution.py:508
  22.4 0.0 copy-done.1
  22.4 0.0 copy-done.2
  22.4 0.0 copy-done.5
  22.4 0.0 copy-done.6
  22.5 0.0 copy-done.7
  22.5 0.0 copy-done.8
  22.5 0.0 copy-done.10
  22.5 0.9 shard_map.163
  23.4 2.0 %shard_map.165 = (f32[8,256,512]{2,1,0:T(8,128)S(1)}, f32[8,512]{1,0:T(8,128)S(1)}, f32[8,512]{1,0:T(8,128)S(1)}, f32[512,128]{1,0:T(8,128)S(1)}) custom-call(bf16[128,512]{1,0:T(8,128)(2,1)S(1)} %get-tuple-element.27.users_t_ref, bf16[512,128]{1,0:T(8,128)(2,1)S(1)} %get-tuple-element.28.next_users_ref, s32[512,128]{1,0:T(8,128)S(1)} %get-tuple-element.29.low_ref, ...), custom_call_target="tpu_custom_call" | custom-call | tf_op jit(solution)/shard_map/pallas_call | solution.py:431
  25.3 0.0 collective-permute-done.other_ref
  25.3 0.0 copy-done.11
  25.4 6.2 %shard_map.166 = (bf16[8,352,128]{2,1,0:T(8,128)(2,1)S(1)}, f32[1,512]{1,0:T(1,128)}, bf16[8,256,512]{2,1,0:T(8,128)(2,1)S(1)}, bf16[128,512]{1,0:T(8,128)(2,1)S(1)}, bf16[512,512]{1,0:T(8,128)(2,1)S(1)}) custom-call(s32[1]{0:T(128)} %bitcast.1.core_ref, bf16[512,256]{1,0:T(8,128)(2,1)S(1)} %copy-done.1, ...), custom_call_target="tpu_custom_call" | custom-call | tf_op jit(solution)/shard_map/pallas_call | solution.py:451
  31.5 1.9 %collective-permute-start.1 = (bf16[8,352,128]{2,1,0:T(8,128)(2,1)S(1)}, bf16[8,352,128]{2,1,0:T(8,128)(2,1)S(1)}, u32[]{:S(2)}, u32[]{:S(2)}) collective-permute-start(bf16[8,352,128]{2,1,0:T(8,128)(2,1)S(1)} %get-tuple-element.39), channel_id=1, source_target_pairs={{0,1},{1,0},{2,3},{3,2},{4,5},{5,4},{6,7},{7,6},{8,9},{9,8},{10,11... | collective-permute-start | bytes 2162696 | tf_op jit(solution)/shard_map/ppermute | solution.py:513
  33.4 0.9 shard_map.167
  34.3 1.3 %collective-permute-done.1 = bf16[8,352,128]{2,1,0:T(8,128)(2,1)S(1)} collective-permute-done((bf16[8,352,128]{2,1,0:T(8,128)(2,1)S(1)}, bf16[8,352,128]{2,1,0:T(8,128)(2,1)S(1)}, u32[]{:S(2)}, u32[]{:S(2)}) %collective-permute-start.1) | collective-permute-done | bytes 720928 | tf_op jit(solution)/shard_map/ppermute | solution.py:513
  35.6 0.1 add_convert_fusion
  35.7 14.5 %all_to_all.26.parts_ref = bf16[8,352,128]{2,1,0:T(8,128)(2,1)S(1)} all-to-all(bf16[8,352,128]{2,1,0:T(8,128)(2,1)S(1)} %add_convert_fusion), channel_id=1, replica_groups=mesh['h'=4,'z'=8,'x'=4,'l'=2,'c'=2] {'x','l'}, dimensions={0} | all-to-all | bytes 1441792 | tf_op jit(solution)/shard_map/all_to_all | solution.py:403
  50.2 0.0 copy-start.3
  50.2 0.0 copy-start.4
  50.2 0.0 copy-start.9
  50.2 0.1 shard_map.168
  50.3 24.4 %all_to_all.27.parts_ref = bf16[32,16,128]{2,1,0:T(8,128)(2,1)S(1)} all-to-all(bf16[32,16,128]{2,1,0:T(8,128)(2,1)S(1)} %shard_map.168), channel_id=1, replica_groups=mesh['h'=4,'z'=8,'x'=4,'l'=2,'c'=2] {'z','h'}, dimensions={0} | all-to-all | bytes 262144 | tf_op jit(solution)/shard_map/all_to_all | solution.py:403
  74.8 14.4 %all_to_all.28.pieces_ref = bf16[32,16,128]{2,1,0:T(8,128)(2,1)S(1)} all-to-all(bf16[32,16,128]{2,1,0:T(8,128)(2,1)S(1)} %shard_map.169), channel_id=1, replica_groups=mesh['h'=4,'z'=8,'x'=4,'l'=2,'c'=2] {'z','h'}, dimensions={0} | all-to-all | bytes 262144 | tf_op jit(solution)/shard_map/all_to_all | solution.py:403
  89.2 0.1 shard_map.170
  89.3 14.8 %all_to_all.29.tower_ref = bf16[16,96,128]{2,1,0:T(8,128)(2,1)S(1)} all-to-all(bf16[16,96,128]{2,1,0:T(8,128)(2,1)S(1)} %shard_map.170), channel_id=1, replica_groups=mesh['h'=4,'z'=8,'x'=4,'l'=2,'c'=2] {'x','c','l'}, dimensions={0} | all-to-all | bytes 786432 | tf_op jit(solution)/shard_map/all_to_all | solution.py:403
  104.0 0.0 copy-done.3
  104.0 0.0 copy-done.4
  104.0 0.0 copy-done.9
  104.0 1.9 %shard_map.171 = (f32[1024,128]{1,0:T(8,128)}, f32[1024,128]{1,0:T(8,128)}, f32[1024,128]{1,0:T(8,128)}, f32[256,512]{1,0:T(8,128)}, f32[512,128]{1,0:T(8,128)}) custom-call(s32[1,256]{1,0:T(1,128)S(1)} %bitcast.9, bf16[32,16,128]{2,1,0:T(8,128)(2,1)S(1)} %all_to_all.28.pieces_ref, f32[1024,128]{1,0:T(8,128)S(1)} %copy-done.3, f32[1024,128]{1,0:T(8,128)S(1)} %copy-done.4, ...), custom_call_target="tpu_custom_call" | custom-call | tf_op jit(solution)/shard_map/pallas_call | solution.py:523
  (3 shorter events, 0.1 us)
Async XLA Ops:
  0.6 1.1 %copy-start = (f32[1024,128]{1,0:T(8,128)S(1)}, f32[1024,128]{1,0:T(8,128)}, u32[]{:S(2)}) copy-start(f32[1024,128]{1,0:T(8,128)} %param.18) | copy-start | bytes 1572868
  1.7 20.7 %copy-start.1 = (bf16[512,256]{1,0:T(8,128)(2,1)S(1)}, bf16[512,256]{1,0:T(8,128)(2,1)}, u32[]{:S(2)}) copy-start(bf16[512,256]{1,0:T(8,128)(2,1)} %states_ref.5) | copy-start | bytes 786436
  1.7 20.7 %copy-start.2 = (bf16[512,128]{1,0:T(8,128)(2,1)S(1)}, bf16[512,128]{1,0:T(8,128)(2,1)}, u32[]{:S(2)}) copy-start(bf16[512,128]{1,0:T(8,128)(2,1)} %w_embed_ref.3) | copy-start | bytes 393220
  1.7 20.7 %copy-start.5 = (bf16[512,256]{1,0:T(8,128)(2,1)S(1)}, bf16[512,256]{1,0:T(8,128)(2,1)}, u32[]{:S(2)}) copy-start(bf16[512,256]{1,0:T(8,128)(2,1)} %next_ref.1) | copy-start | bytes 786436
  1.7 20.7 %copy-start.6 = (bf16[256,512]{1,0:T(8,128)(2,1)S(1)}, bf16[256,512]{1,0:T(8,128)(2,1)}, u32[]{:S(2)}) copy-start(bf16[256,512]{1,0:T(8,128)(2,1)} %w_hidden_ref.1) | copy-start | bytes 786436
  1.7 20.7 %copy-start.7 = (s32[512,10]{0,1:T(8,128)S(1)}, s32[512,10]{0,1:T(8,128)}, u32[]{:S(2)}) copy-start(s32[512,10]{0,1:T(8,128)} %param.17) | copy-start | bytes 61444
  1.7 20.7 %copy-start.8 = (s32[512,10]{0,1:T(8,128)S(1)}, s32[512,10]{0,1:T(8,128)}, u32[]{:S(2)}) copy-start(s32[512,10]{0,1:T(8,128)} %param.15) | copy-start | bytes 61444
  1.7 20.7 %copy-start.10 = (s32[512]{0:T(512)S(1)}, s32[512]{0:T(512)}, u32[]{:S(2)}) copy-start(s32[512]{0:T(512)} %param.16) | copy-start | bytes 6148
  2.5 22.8 %copy-start.11 = (f32[512]{0:T(512)S(1)}, f32[512]{0:T(512)}, u32[]{:S(2)}) copy-start(f32[512]{0:T(512)} %param.14) | copy-start | bytes 6148
  15.7 9.6 %collective-permute-start = (bf16[8,256,128]{2,1,0:T(8,128)(2,1)S(1)}, bf16[8,256,128]{2,1,0:T(8,128)(2,1)S(1)}, u32[]{:S(2)}, u32[]{:S(2)}) collective-permute-start(bf16[8,256,128]{2,1,0:T(8,128)(2,1)S(1)} %all_to_all.25.own_ref), channel_id=1, source_target_pairs={{0,1},{1,0},{2,3},{3,2},{4,5},{5,4},{6,7},{7,6},{8,9},{9,8},{10,11... | collective-permute-start | bytes 1572872 | tf_op jit(solution)/shard_map/ppermute | solution.py:508
  31.5 4.1 %collective-permute-start.1 = (bf16[8,352,128]{2,1,0:T(8,128)(2,1)S(1)}, bf16[8,352,128]{2,1,0:T(8,128)(2,1)S(1)}, u32[]{:S(2)}, u32[]{:S(2)}) collective-permute-start(bf16[8,352,128]{2,1,0:T(8,128)(2,1)S(1)} %get-tuple-element.39), channel_id=1, source_target_pairs={{0,1},{1,0},{2,3},{3,2},{4,5},{5,4},{6,7},{7,6},{8,9},{9,8},{10,11... | collective-permute-start | bytes 2162696 | tf_op jit(solution)/shard_map/ppermute | solution.py:513
  50.2 53.8 %copy-start.3 = (f32[1024,128]{1,0:T(8,128)S(1)}, f32[1024,128]{1,0:T(8,128)}, u32[]{:S(2)}) copy-start(f32[1024,128]{1,0:T(8,128)} %first_ref.1) | copy-start | bytes 1572868
  50.2 53.8 %copy-start.4 = (f32[1024,128]{1,0:T(8,128)S(1)}, f32[1024,128]{1,0:T(8,128)}, u32[]{:S(2)}) copy-start(f32[1024,128]{1,0:T(8,128)} %second_ref.1) | copy-start | bytes 1572868
  50.2 53.8 %copy-start.9 = (s32[256]{0:T(256)S(1)}, s32[256]{0:T(256)}, u32[]{:S(2)}) copy-start(s32[256]{0:T(256)} %param.21) | copy-start | bytes 3076

commit v9 on v8

--- a/solution.py
+++ b/solution.py
@@ -497,7 +497,9 @@
     rows = cand_rows.reshape(1, BLOCK)
     pair = [(0, 1), (1, 0)]
 
-    local_rows = table.at[cand_rows].get(mode="promise_in_bounds", unique_indices=True)
+    local_rows = table.at[cand_rows].get(
+        mode="promise_in_bounds", unique_indices=True, wrap_negative_indices=False
+    )
     copies = in_vmem(copies_kernel, local_rows, (CHIPS, BLOCK, embed))
     core = lax.axis_index("c").astype(jnp.int32).reshape(1)
     chosen = chosen.reshape(1, sessions)

time: 106 us -> 106 us (level)
  no operation moved by 1% of the time
where the time goes in v9:
time: 106 us
  blocking collectives  81.3 us (77%)
  Pallas kernels  12 us (11%)
  starting transfers between devices  8.59 us (8%)
  waiting for transfers between devices  1.26 us (1%)
  local copies, waits for them, and re-layouts  1.1 us (1%)
    all_to_all x5, blocking collectives, swap(): return lax.all_to_all(array, axes, 0, 0, tiled=True)  81.3 us
    ppermute x1, starting transfers between devices, shards(): other = lax.ppermute(own, 'c', pair)  6.68 us
    pallas_call x1, Pallas kernels, main_call(): pl.pallas_call(main_kernel, in_specs=[scalar] + [vmem] * 15, out_specs=[v...  6.15 us
  transfers between devices with their start and end apart: 2, of which 1 were waited for; matrix products, arithmetic and copies ran while one was open for 0% of the time, Pallas kernels for 4%

profile of v9, /device:TPU:1, one launch (start us, length us, event | category | flops | bytes accessed | tf_op | source)
XLA Modules:
  0.0 106.0 jit_solution(12156670111829202002)
XLA Ops:
  0.6 0.0 copy-start
  0.6 0.7 pad_clamp_fusion
  1.4 0.3 copy-done
  1.7 0.0 copy-start.1
  1.7 0.0 copy-start.2
  1.7 0.0 copy-start.5
  1.7 0.0 copy-start.6
  1.7 0.0 copy-start.7
  1.7 0.0 copy-start.8
  1.7 0.0 copy-start.10
  1.7 0.7 gather_fusion
  2.5 0.0 copy-start.11
  2.5 13.2 %all_to_all.25.own_ref = bf16[8,256,128]{2,1,0:T(8,128)(2,1)S(1)} all-to-all(bf16[8,256,128]{2,1,0:T(8,128)(2,1)S(1)} %shard_map.164), channel_id=1, replica_groups=mesh['h'=4,'z'=8,'x'=4,'l'=2,'c'=2] {'x','l'}, dimensions={0} | all-to-all | bytes 1048576 | tf_op jit(solution)/shard_map/all_to_all | solution.py:403
  15.7 6.7 %collective-permute-start = (bf16[8,256,128]{2,1,0:T(8,128)(2,1)S(1)}, bf16[8,256,128]{2,1,0:T(8,128)(2,1)S(1)}, u32[]{:S(2)}, u32[]{:S(2)}) collective-permute-start(bf16[8,256,128]{2,1,0:T(8,128)(2,1)S(1)} %all_to_all.25.own_ref), channel_id=1, source_target_pairs={{0,1},{1,0},{2,3},{3,2},{4,5},{5,4},{6,7},{7,6},{8,9},{9,8},{10,11... | collective-permute-start | bytes 1572872 | tf_op jit(solution)/shard_map/ppermute | solution.py:510
  22.4 0.0 copy-done.1
  22.4 0.0 copy-done.2
  22.4 0.0 copy-done.5
  22.4 0.0 copy-done.6
  22.5 0.0 copy-done.7
  22.5 0.0 copy-done.8
  22.5 0.0 copy-done.10
  22.5 0.9 shard_map.163
  23.4 1.9 %shard_map.165 = (f32[8,256,512]{2,1,0:T(8,128)S(1)}, f32[8,512]{1,0:T(8,128)S(1)}, f32[8,512]{1,0:T(8,128)S(1)}, f32[512,128]{1,0:T(8,128)S(1)}) custom-call(bf16[128,512]{1,0:T(8,128)(2,1)S(1)} %get-tuple-element.27.users_t_ref, bf16[512,128]{1,0:T(8,128)(2,1)S(1)} %get-tuple-element.28.next_users_ref, s32[512,128]{1,0:T(8,128)S(1)} %get-tuple-element.29.low_ref, ...), custom_call_target="tpu_custom_call" | custom-call | tf_op jit(solution)/shard_map/pallas_call | solution.py:431
  25.3 0.0 collective-permute-done.other_ref
  25.3 0.0 copy-done.11
  25.4 6.2 %shard_map.166 = (bf16[8,352,128]{2,1,0:T(8,128)(2,1)S(1)}, f32[1,512]{1,0:T(1,128)}, bf16[8,256,512]{2,1,0:T(8,128)(2,1)S(1)}, bf16[128,512]{1,0:T(8,128)(2,1)S(1)}, bf16[512,512]{1,0:T(8,128)(2,1)S(1)}) custom-call(s32[1]{0:T(128)} %bitcast.1.core_ref, bf16[512,256]{1,0:T(8,128)(2,1)S(1)} %copy-done.1, ...), custom_call_target="tpu_custom_call" | custom-call | tf_op jit(solution)/shard_map/pallas_call | solution.py:451
  31.5 1.9 %collective-permute-start.1 = (bf16[8,352,128]{2,1,0:T(8,128)(2,1)S(1)}, bf16[8,352,128]{2,1,0:T(8,128)(2,1)S(1)}, u32[]{:S(2)}, u32[]{:S(2)}) collective-permute-start(bf16[8,352,128]{2,1,0:T(8,128)(2,1)S(1)} %get-tuple-element.39), channel_id=1, source_target_pairs={{0,1},{1,0},{2,3},{3,2},{4,5},{5,4},{6,7},{7,6},{8,9},{9,8},{10,11... | collective-permute-start | bytes 2162696 | tf_op jit(solution)/shard_map/ppermute | solution.py:515
  33.4 0.9 shard_map.167
  34.3 1.3 %collective-permute-done.1 = bf16[8,352,128]{2,1,0:T(8,128)(2,1)S(1)} collective-permute-done((bf16[8,352,128]{2,1,0:T(8,128)(2,1)S(1)}, bf16[8,352,128]{2,1,0:T(8,128)(2,1)S(1)}, u32[]{:S(2)}, u32[]{:S(2)}) %collective-permute-start.1) | collective-permute-done | bytes 720928 | tf_op jit(solution)/shard_map/ppermute | solution.py:515
  35.6 0.1 add_convert_fusion
  35.7 14.5 %all_to_all.26.parts_ref = bf16[8,352,128]{2,1,0:T(8,128)(2,1)S(1)} all-to-all(bf16[8,352,128]{2,1,0:T(8,128)(2,1)S(1)} %add_convert_fusion), channel_id=1, replica_groups=mesh['h'=4,'z'=8,'x'=4,'l'=2,'c'=2] {'x','l'}, dimensions={0} | all-to-all | bytes 1441792 | tf_op jit(solution)/shard_map/all_to_all | solution.py:403
  50.2 0.0 copy-start.3
  50.2 0.0 copy-start.4
  50.2 0.0 copy-start.9
  50.2 0.1 shard_map.168
  50.3 24.4 %all_to_all.27.parts_ref = bf16[32,16,128]{2,1,0:T(8,128)(2,1)S(1)} all-to-all(bf16[32,16,128]{2,1,0:T(8,128)(2,1)S(1)} %shard_map.168), channel_id=1, replica_groups=mesh['h'=4,'z'=8,'x'=4,'l'=2,'c'=2] {'z','h'}, dimensions={0} | all-to-all | bytes 262144 | tf_op jit(solution)/shard_map/all_to_all | solution.py:403
  74.8 14.4 %all_to_all.28.pieces_ref = bf16[32,16,128]{2,1,0:T(8,128)(2,1)S(1)} all-to-all(bf16[32,16,128]{2,1,0:T(8,128)(2,1)S(1)} %shard_map.169), channel_id=1, replica_groups=mesh['h'=4,'z'=8,'x'=4,'l'=2,'c'=2] {'z','h'}, dimensions={0} | all-to-all | bytes 262144 | tf_op jit(solution)/shard_map/all_to_all | solution.py:403
  89.2 0.1 shard_map.170
  89.3 14.8 %all_to_all.29.tower_ref = bf16[16,96,128]{2,1,0:T(8,128)(2,1)S(1)} all-to-all(bf16[16,96,128]{2,1,0:T(8,128)(2,1)S(1)} %shard_map.170), channel_id=1, replica_groups=mesh['h'=4,'z'=8,'x'=4,'l'=2,'c'=2] {'x','c','l'}, dimensions={0} | all-to-all | bytes 786432 | tf_op jit(solution)/shard_map/all_to_all | solution.py:403
  104.0 0.0 copy-done.3
  104.0 0.0 copy-done.4
  104.0 0.0 copy-done.9
  104.0 1.9 %shard_map.171 = (f32[1024,128]{1,0:T(8,128)}, f32[1024,128]{1,0:T(8,128)}, f32[1024,128]{1,0:T(8,128)}, f32[256,512]{1,0:T(8,128)}, f32[512,128]{1,0:T(8,128)}) custom-call(s32[1,256]{1,0:T(1,128)S(1)} %bitcast.9, bf16[32,16,128]{2,1,0:T(8,128)(2,1)S(1)} %all_to_all.28.pieces_ref, f32[1024,128]{1,0:T(8,128)S(1)} %copy-done.3, f32[1024,128]{1,0:T(8,128)S(1)} %copy-done.4, ...), custom_call_target="tpu_custom_call" | custom-call | tf_op jit(solution)/shard_map/pallas_call | solution.py:525
  (2 shorter events, 0.1 us)
Async XLA Ops:
  0.6 1.1 %copy-start = (f32[1024,128]{1,0:T(8,128)S(1)}, f32[1024,128]{1,0:T(8,128)}, u32[]{:S(2)}) copy-start(f32[1024,128]{1,0:T(8,128)} %param.18) | copy-start | bytes 1572868
  1.7 20.7 %copy-start.1 = (bf16[512,256]{1,0:T(8,128)(2,1)S(1)}, bf16[512,256]{1,0:T(8,128)(2,1)}, u32[]{:S(2)}) copy-start(bf16[512,256]{1,0:T(8,128)(2,1)} %states_ref.5) | copy-start | bytes 786436
  1.7 20.7 %copy-start.2 = (bf16[512,128]{1,0:T(8,128)(2,1)S(1)}, bf16[512,128]{1,0:T(8,128)(2,1)}, u32[]{:S(2)}) copy-start(bf16[512,128]{1,0:T(8,128)(2,1)} %w_embed_ref.3) | copy-start | bytes 393220
  1.7 20.7 %copy-start.5 = (bf16[512,256]{1,0:T(8,128)(2,1)S(1)}, bf16[512,256]{1,0:T(8,128)(2,1)}, u32[]{:S(2)}) copy-start(bf16[512,256]{1,0:T(8,128)(2,1)} %next_ref.1) | copy-start | bytes 786436
  1.7 20.7 %copy-start.6 = (bf16[256,512]{1,0:T(8,128)(2,1)S(1)}, bf16[256,512]{1,0:T(8,128)(2,1)}, u32[]{:S(2)}) copy-start(bf16[256,512]{1,0:T(8,128)(2,1)} %w_hidden_ref.1) | copy-start | bytes 786436
  1.7 20.8 %copy-start.7 = (s32[512,10]{0,1:T(8,128)S(1)}, s32[512,10]{0,1:T(8,128)}, u32[]{:S(2)}) copy-start(s32[512,10]{0,1:T(8,128)} %param.17) | copy-start | bytes 61444
  1.7 20.7 %copy-start.8 = (s32[512,10]{0,1:T(8,128)S(1)}, s32[512,10]{0,1:T(8,128)}, u32[]{:S(2)}) copy-start(s32[512,10]{0,1:T(8,128)} %param.15) | copy-start | bytes 61444
  1.7 20.7 %copy-start.10 = (s32[512]{0:T(512)S(1)}, s32[512]{0:T(512)}, u32[]{:S(2)}) copy-start(s32[512]{0:T(512)} %param.16) | copy-start | bytes 6148
  2.5 22.8 %copy-start.11 = (f32[512]{0:T(512)S(1)}, f32[512]{0:T(512)}, u32[]{:S(2)}) copy-start(f32[512]{0:T(512)} %param.14) | copy-start | bytes 6148
  15.7 9.6 %collective-permute-start = (bf16[8,256,128]{2,1,0:T(8,128)(2,1)S(1)}, bf16[8,256,128]{2,1,0:T(8,128)(2,1)S(1)}, u32[]{:S(2)}, u32[]{:S(2)}) collective-permute-start(bf16[8,256,128]{2,1,0:T(8,128)(2,1)S(1)} %all_to_all.25.own_ref), channel_id=1, source_target_pairs={{0,1},{1,0},{2,3},{3,2},{4,5},{5,4},{6,7},{7,6},{8,9},{9,8},{10,11... | collective-permute-start | bytes 1572872 | tf_op jit(solution)/shard_map/ppermute | solution.py:510
  31.5 4.1 %collective-permute-start.1 = (bf16[8,352,128]{2,1,0:T(8,128)(2,1)S(1)}, bf16[8,352,128]{2,1,0:T(8,128)(2,1)S(1)}, u32[]{:S(2)}, u32[]{:S(2)}) collective-permute-start(bf16[8,352,128]{2,1,0:T(8,128)(2,1)S(1)} %get-tuple-element.39), channel_id=1, source_target_pairs={{0,1},{1,0},{2,3},{3,2},{4,5},{5,4},{6,7},{7,6},{8,9},{9,8},{10,11... | collective-permute-start | bytes 2162696 | tf_op jit(solution)/shard_map/ppermute | solution.py:515
  50.2 53.8 %copy-start.3 = (f32[1024,128]{1,0:T(8,128)S(1)}, f32[1024,128]{1,0:T(8,128)}, u32[]{:S(2)}) copy-start(f32[1024,128]{1,0:T(8,128)} %first_ref.1) | copy-start | bytes 1572868
  50.2 53.8 %copy-start.4 = (f32[1024,128]{1,0:T(8,128)S(1)}, f32[1024,128]{1,0:T(8,128)}, u32[]{:S(2)}) copy-start(f32[1024,128]{1,0:T(8,128)} %second_ref.1) | copy-start | bytes 1572868
  50.2 53.8 %copy-start.9 = (s32[256]{0:T(256)S(1)}, s32[256]{0:T(256)}, u32[]{:S(2)}) copy-start(s32[256]{0:T(256)} %param.21) | copy-start | bytes 3076
